TPU v7x, 32 devices: a whole 2x2x4 slice. The times are simulated.
32 devices in a mesh: conf: 2 (over x), virt: 16 (over z, y, core).
Axes of the slice: x: 2, y: 2, z: 4, core: 2. Of those that a mesh axis runs over, the one named last changes fastest.
Arguments:
- i_factors: float32 [32, 1024, 2048], P('conf', 'virt'), parts along dimension 0, may hold values from -0.6 to 0.6
- j_factors: float32 [4, 1024, 2048], P('conf', 'virt'), parts along dimension 0, may hold values from -0.6 to 0.6
- occ_i: float32 [32], P('conf'), parts along dimension 0, may hold values from -2 to -0.3
- occ_j: float32 [4], P('conf'), parts along dimension 0, may hold values from -2 to -0.3
- virt_energy: float32 [2048], P(('conf', 'virt')), parts along dimension 0, may hold values from 0.3 to 3
Outputs:
- density: float32 [32, 1024, 2048], P('conf', 'virt'), parts along dimension 0
There are 2 independent parts, one for each index of `conf`. A program takes and returns all parts, laid end to end along the dimension named above; each array names one. Nothing has to cross between parts.
All inputs are finite; a program needn't handle non-finite values.
Results may differ from a plain program's by a relative error of at most 0.00005.
Values sent between devices are 32-bit elements; how exact they have to be, the bound alone decides.
No kernel may reach another device: no remote copies, remote signals or barrier semaphores. Data moves between devices by JAX's collectives and lax.ppermute only.
A program may use at most 128 MiB of HBM per device.

v0:
```python
import jax
import jax.numpy as jnp
from jax import lax
from jax.sharding import PartitionSpec as P


def transpose_blocks(pair_block, blocks):
    leading = pair_block.shape[:-2]
    height = pair_block.shape[-2]
    width = pair_block.shape[-1]
    split = pair_block.reshape(leading + (height, blocks, height))
    moved = jnp.swapaxes(split, -1, -3)
    return moved.reshape(leading + (height, width))


def body(i_factors, j_factors, occ_i, occ_j, virt_energy):
    blocks = lax.axis_size("virt")
    left_rows = i_factors.reshape(-1, i_factors.shape[2])
    density = jnp.zeros(i_factors.shape, jnp.float32)
    for index in range(j_factors.shape[0]):
        whole_rows, whole_energy = (
            lax.all_gather(j_factors[index], "virt", axis=0, tiled=True),
            lax.all_gather(virt_energy, "virt", axis=0, tiled=True),
        )
        pair_block = jnp.dot(left_rows, whole_rows.T, precision=lax.Precision.HIGHEST)
        pair_block = pair_block.reshape(i_factors.shape[0], i_factors.shape[1], whole_rows.shape[0])
        swapped = lax.all_to_all(
            transpose_blocks(pair_block, blocks), "virt", split_axis=2, concat_axis=2, tiled=True
        )
        denominator = (
            virt_energy[None, :, None]
            + whole_energy[None, None, :]
            - occ_i[:, None, None]
            - occ_j[index]
        )
        amplitude = (swapped - 2.0 * pair_block) / denominator
        density = density + jnp.einsum(
            "iab,bp->iap", amplitude, whole_rows, precision=lax.Precision.HIGHEST
        )
    return density


def solution(mesh):
    placed = (
        P("conf", "virt", None),
        P("conf", "virt", None),
        P("conf"),
        P("conf"),
        P(("conf", "virt")),
    )
    return jax.shard_map(
        body, mesh=mesh, in_specs=placed, out_specs=P("conf", "virt", None), check_vma=False
    )
```

profile of v0, /device:TPU:16, one launch (start us, length us, event | category | flops | bytes accessed | tf_op | source)
XLA Modules:
  0.0 498.3 jit_solution(2721540128642686611)
XLA Ops:
  6.5 0.0 all-gather.7.cloned.1.call-start
  6.5 2.3 fusion.25
  8.8 0.0 all-gather.7.cloned.1.call-update
  8.8 0.0 all-gather.5.cloned.1.call-start
  8.9 0.7 all-gather.5.cloned.1.call-update
  9.6 75.1 %all-gather.7.cloned.1.call-done = f32[1,1024,2048]{2,1,0:T(8,128)} async-done(((f32[1,64,2048]{2,1,0:T(8,128)}), f32[1,1024,2048]{2,1,0:T(8,128)}) %all-gather.7.cloned.1.call-update) | async-done | bytes 8388624 | tf_op jit(solution)/shard_map/all_gather | solution.py:22
  84.7 33.7 %broadcast_multiply_fusion = (f32[1024,1024]{1,0:T(8,128)}, f32[1024,1024]{1,0:T(8,128)}) fusion(f32[1024,2048]{1,0:T(8,128)} %bitcast.40, f32[1,1024,2048]{2,1,0:T(8,128)} %all-gather.7.cloned.1.call-done), kind=kOutput, calls=%fused_computation.21 | convolution fusion | flops 25770852352 | bytes 25165824 | tf_op jit(solution)/shard_map/dot_general | solution.py:25
  118.4 7.3 %reshape_reshape.7 = f32[16,64,16,64]{3,2,1,0:T(8,128)} reshape(f32[1024,1024]{1,0:T(8,128)} %get-tuple-element.10) | data formatting | bytes 8388608 | tf_op jit(solution)/shard_map/reshape;reshape | solution.py:11
  125.7 11.5 %copy.16 = f32[16,64,16,64]{1,0,3,2:T(8,128)} copy(f32[16,64,16,64]{1,2,3,0:T(8,128)} %bitcast.36) | data formatting | bytes 8388608 | tf_op jit(solution)/shard_map/transpose | solution.py:12
  137.2 13.3 %reshape.60 = f32[16,1,65536]{2,1,0:T(1,128)} reshape(f32[1024,16,64]{2,1,0:T(8,128)} %bitcast.37) | data formatting | bytes 8388608
  150.5 6.2 %all-to-all-start.1 = ((f32[16,1,65536]{2,1,0:T(1,128)}), f32[16,1,65536]{2,1,0:T(1,128)}, u32[]{:S(2)}, u32[]{:S(2)}) async-start(f32[16,1,65536]{2,1,0:T(1,128)} %reshape.60), calls=%async_computation.1 | async-start | bytes 8388608 | tf_op jit(solution)/shard_map/all_to_all | solution.py:27
  156.7 3.3 all-gather.5.cloned.1.call-done
  160.0 33.7 %broadcast_multiply_fusion.1 = (f32[1024,1024]{1,0:T(8,128)}, f32[1024,1024]{1,0:T(8,128)}) fusion(f32[1024,2048]{1,0:T(8,128)} %bitcast.41, f32[1,1024,2048]{2,1,0:T(8,128)} %all-gather.5.cloned.1.call-done), kind=kOutput, calls=%fused_computation.22 | convolution fusion | flops 25770852352 | bytes 25165824 | tf_op jit(solution)/shard_map/dot_general | solution.py:25
  193.7 7.2 %reshape_reshape.6 = f32[16,64,16,64]{3,2,1,0:T(8,128)} reshape(f32[1024,1024]{1,0:T(8,128)} %get-tuple-element.12) | data formatting | bytes 8388608 | tf_op jit(solution)/shard_map/reshape;reshape | solution.py:11
  200.9 11.5 %copy.14 = f32[16,64,16,64]{1,0,3,2:T(8,128)} copy(f32[16,64,16,64]{1,2,3,0:T(8,128)} %bitcast.38) | data formatting | bytes 8388608 | tf_op jit(solution)/shard_map/transpose | solution.py:12
  212.4 13.3 %reshape.62 = f32[16,1,65536]{2,1,0:T(1,128)} reshape(f32[1024,16,64]{2,1,0:T(8,128)} %bitcast.39) | data formatting | bytes 8388608
  225.6 0.0 copy-start.5
  225.6 0.0 copy-start.2
  225.6 0.0 copy-start.1
  225.6 23.6 %all-to-all-done.1 = f32[16,1,65536]{2,1,0:T(1,128)} async-done(((f32[16,1,65536]{2,1,0:T(1,128)}), f32[16,1,65536]{2,1,0:T(1,128)}, u32[]{:S(2)}, u32[]{:S(2)}) %all-to-all-start.1) | async-done | bytes 4194336 | tf_op jit(solution)/shard_map/all_to_all | solution.py:27
  249.2 4.7 all-to-all-start
  253.9 0.0 copy-done.5
  253.9 0.6 dynamic-slice
  255.2 0.0 copy-done.2
  255.2 0.2 dynamic-update-slice
  255.4 109.5 %all-reduce = f32[1024]{0:T(1024)S(1)} all-reduce(f32[1024]{0:T(1024)S(1)} %dynamic-update-slice), channel_id=1, replica_groups=mesh['conf'=2,'virt'=16] {'virt'}, use_global_device_ids=true, to_apply=%add | all-reduce | flops 1024 | bytes 8192
  364.9 0.0 copy-done.1
  364.9 0.6 fusion.26
  365.5 0.1 broadcast_add_fusion
  365.6 0.6 broadcast.34
  366.2 13.7 %reduce = f32[16,65536]{1,0:T(8,128)} reduce(f32[16,1,65536]{2,1,0:T(1,128)} %all-to-all-done.1, f32[]{:T(128)} %broadcast.34), dimensions={1}, to_apply=%all_to_all.7.reduce_sub_computation | reduce | bytes 8388612 | tf_op jit(solution)/shard_map/all_to_all | solution.py:27
  379.9 6.9 %reshape.61 = f32[1024,16,64]{2,1,0:T(8,128)} reshape(f32[16,65536]{1,0:T(8,128)} %reduce) | data formatting | bytes 8388608
  386.8 6.8 %copy.17 = f32[16,64,1024]{2,1,0:T(8,128)} copy(f32[16,64,1024]{1,0,2:T(8,128)} %bitcast.34) | data formatting | bytes 8388608 | tf_op jit(solution)/shard_map/all_to_all | solution.py:27
  393.7 0.0 all-to-all-done
  393.7 13.8 %reduce.1 = f32[16,65536]{1,0:T(8,128)} reduce(f32[16,1,65536]{2,1,0:T(1,128)} %all-to-all-done, f32[]{:T(128)} %broadcast.34), dimensions={1}, to_apply=%all_to_all.6.reduce_sub_computation | reduce | bytes 8388612 | tf_op jit(solution)/shard_map/all_to_all | solution.py:27
  407.5 6.9 %reshape.63 = f32[1024,16,64]{2,1,0:T(8,128)} reshape(f32[16,65536]{1,0:T(8,128)} %reduce.1) | data formatting | bytes 8388608
  414.5 0.0 copy-start.3
  414.5 6.9 %copy.15 = f32[16,64,1024]{2,1,0:T(8,128)} copy(f32[16,64,1024]{1,0,2:T(8,128)} %bitcast.35) | data formatting | bytes 8388608 | tf_op jit(solution)/shard_map/all_to_all | solution.py:27
  421.3 0.0 copy-done.3
  421.3 0.0 copy-start
  421.3 0.0 copy-start.4
  421.3 33.6 %fusion = f32[16,64,2048]{2,1,0:T(8,128)S(1)} fusion(f32[1,1024,2048]{2,1,0:T(8,128)} %all-gather.7.cloned.1.call-done, f32[16,64,1024]{2,1,0:T(8,128)} %copy.17, f32[16,64,1024]{2,1,0:T(8,128)} %bitcast.42, f32[]{:T(128)} %bitcast.12, f32[16]{0:T(128)S(1)} %copy-done.3, f32[64,1024]{1,0:T(8,128)S(1)} %broadcast_add_fusion), kind=kOutput, calls=%fused_computation | convolution fusion | flops 25773998080 | bytes 25428036 | tf_op jit(solution)/shard_map/iab,bp->iap/dot_general | solution.py:37
  454.9 0.0 copy-done
  454.9 0.0 copy-done.4
  454.9 36.0 %fusion.14 = f32[16,64,2048]{2,1,0:T(8,128)} fusion(f32[16,64,2048]{2,1,0:T(8,128)S(1)} %fusion, f32[1,1024,2048]{2,1,0:T(8,128)} %all-gather.5.cloned.1.call-done, f32[16,64,1024]{2,1,0:T(8,128)S(1)} %copy-done, f32[16,64,1024]{2,1,0:T(8,128)S(1)} %bitcast.43, f32[]{:T(128)} %bitcast.6, f32[16]{0:T(128)S(1)} %copy-done.3, f32[64,1024]{1,0:T(8,128)S(1)} %broadcast_add_fusion), kind=kOutput, calls=%fused_computation.14 | convolution fusion | flops 25776095232 | bytes 33816644 | tf_op jit(solution)/shard_map/iab,bp->iap/dot_general | solution.py:37
  (1 shorter events, 0.0 us)
Async XLA Ops:
  6.5 78.2 %all-gather.7.cloned.1.call-start = ((), (), s32[]{:S(2)}) async-start(), calls=%async_computation.3 | async-start | bytes 8912896 | tf_op jit(solution)/shard_map/all_gather | solution.py:22
  8.8 151.2 %all-gather.5.cloned.1.call-start = ((), (), s32[]{:S(2)}) async-start(), calls=%async_computation.2 | async-start | bytes 8912896 | tf_op jit(solution)/shard_map/all_gather | solution.py:22
  150.5 98.7 %all-to-all-start.1 = ((f32[16,1,65536]{2,1,0:T(1,128)}), f32[16,1,65536]{2,1,0:T(1,128)}, u32[]{:S(2)}, u32[]{:S(2)}) async-start(f32[16,1,65536]{2,1,0:T(1,128)} %reshape.60), calls=%async_computation.1 | async-start | bytes 8388608 | tf_op jit(solution)/shard_map/all_to_all | solution.py:27
  225.6 28.3 %copy-start.5 = (u32[32]{0:T(128)S(1)}, u32[32]{0:T(128)}, u32[]{:S(2)}) copy-start(u32[32]{0:T(128)} %constant.4) | copy-start | bytes 388
  225.6 29.5 %copy-start.2 = (f32[64]{0:T(128)S(1)}, f32[64]{0:T(128)}, u32[]{:S(2)}) copy-start(f32[64]{0:T(128)} %param.9) | copy-start | bytes 772
  225.6 139.3 %copy-start.1 = (f32[2]{0:T(128)S(1)}, f32[2]{0:T(128)}, u32[]{:S(2)}) copy-start(f32[2]{0:T(128)} %param.8) | copy-start | bytes 28
  249.2 144.4 %all-to-all-start = ((f32[16,1,65536]{2,1,0:T(1,128)}), f32[16,1,65536]{2,1,0:T(1,128)}, u32[]{:S(2)}, u32[]{:S(2)}) async-start(f32[16,1,65536]{2,1,0:T(1,128)} %reshape.62), calls=%async_computation | async-start | bytes 8388608 | tf_op jit(solution)/shard_map/all_to_all | solution.py:27
  414.5 6.9 %copy-start.3 = (f32[16]{0:T(128)S(1)}, f32[16]{0:T(128)}, u32[]{:S(2)}) copy-start(f32[16]{0:T(128)} %param.7) | copy-start | bytes 196
  421.3 33.6 %copy-start = (f32[16,64,1024]{2,1,0:T(8,128)S(1)}, f32[16,64,1024]{2,1,0:T(8,128)}, u32[]{:S(2)}) copy-start(f32[16,64,1024]{2,1,0:T(8,128)} %copy.15) | copy-start | bytes 12582916
  421.3 33.6 %copy-start.4 = (f32[1024,1024]{1,0:T(8,128)S(1)}, f32[1024,1024]{1,0:T(8,128)}, u32[]{:S(2)}) copy-start(f32[1024,1024]{1,0:T(8,128)} %get-tuple-element.11) | copy-start | bytes 12582916
Sparse Core Ops, SparseCore 0:
  9.5 75.1 all-gather.6
  86.8 73.1 all-gather.4
where the time goes:
time: 507 us; the launch traced here: 498 us
  matrix products  137 us (27%)
  blocking collectives  109 us (21%)
  waiting for transfers between devices  103 us (20%)
  local copies, waits for them, and re-layouts  96 us (19%)
  other arithmetic  27.6 us (5%)
  between operations  14.6 us (3%)
  starting transfers between devices  10.9 us (2%)
    unnamed x1, blocking collectives  109 us
    all_gather x2, waiting for transfers between devices, body(): lax.all_gather(j_factors[index], 'virt', axis=0, tiled=True)  78.4 us
    dot_general x2, matrix products, body(): jnp.einsum('iab,bp->iap', amplitude, whole_rows, precision=lax.Precision....  69.6 us
    dot_general x2, matrix products, body(): jnp.dot(left_rows, whole_rows.T, precision=lax.Precision.HIGHEST)  67.4 us
    unnamed x19, local copies, waits for them, and re-layouts  41.3 us
    all_to_all x2, other arithmetic, body(): lax.all_to_all(transpose_blocks(pair_block, blocks), 'virt', split_axis=2...  27.6 us
    all_to_all x2, waiting for transfers between devices, body(): lax.all_to_all(transpose_blocks(pair_block, blocks), 'virt', split_axis=2...  23.6 us
    transpose x2, local copies, waits for them, and re-layouts, transpose_blocks(): moved = jnp.swapaxes(split, -1, -3)  23 us
  transfers between devices with their start and end apart: 4, of which 3 were waited for; matrix products, arithmetic and copies ran while one was open for 32% of the time, Pallas kernels for 0%

commit v1 on v0

v1 whole, which is shorter than its diff:
```python
import functools

import jax
import jax.numpy as jnp
from jax import lax
from jax.experimental import pallas as pl
from jax.experimental.pallas import tpu as pltpu
from jax.sharding import PartitionSpec as P

AXIS = "virt"
F32 = jnp.float32
BF16 = jnp.bfloat16
MIB = 1 << 20


def halves(x):
    high = x.astype(BF16)
    low = (x - high.astype(F32)).astype(BF16)
    return high, low


def product(left, right, dims):
    one = lambda u, v: lax.dot_general(u, v, (dims, ((), ())), preferred_element_type=F32)
    return one(left[0], right[0]) + (one(left[0], right[1]) + one(left[1], right[0]))


def pair_kernel(count, height, orbitals, left_ref, *refs):
    shard_refs = refs[:count]
    direct_refs = refs[count : 2 * count]
    message_refs = refs[2 * count : 3 * count]
    high_ref, low_ref = refs[3 * count :]
    width = orbitals * height

    @pl.when(pl.program_id(0) == 0)
    def _():
        for spot in range(count):
            rows = pl.ds(spot * width, width)
            high_ref[rows, :], low_ref[rows, :] = halves(shard_refs[spot][...])

    block = product(halves(left_ref[...]), (high_ref[...], low_ref[...]), ((1,), (1,)))
    for spot in range(count):
        part = block[:, spot * width : (spot + 1) * width]
        direct_refs[spot][...] = part
        for row in range(0, part.shape[0], height):
            turned = part[row : row + height].T
            message_refs[spot][row : row + height, :] = jnp.concatenate(
                [turned[j * height : (j + 1) * height] for j in range(orbitals)], axis=1
            )


def pair_blocks(left, shards, height, orbitals):
    count = len(shards)
    rows, depth = left.shape
    width = orbitals * height
    if width % 128 or height % 8:
        direct, messages = [], []
        for shard in shards:
            block = jnp.dot(left, shard.T, precision=lax.Precision.HIGHEST)
            turned = block.reshape(rows // height, height, orbitals, height)
            direct.append(block)
            messages.append(turned.transpose(0, 3, 2, 1).reshape(rows, width))
        return direct, messages
    step = height * min(rows // height, max(1, 256 // height))
    while rows % step:
        step -= height
    out = pl.pallas_call(
        functools.partial(pair_kernel, count, height, orbitals),
        grid=(rows // step,),
        in_specs=[pl.BlockSpec((step, depth), lambda s: (s, 0))]
        + [pl.BlockSpec((width, depth), lambda s: (0, 0))] * count,
        out_specs=[pl.BlockSpec((step, width), lambda s: (s, 0))] * (2 * count),
        out_shape=[jax.ShapeDtypeStruct((rows, width), F32)] * (2 * count),
        scratch_shapes=[pltpu.VMEM((count * width, depth), BF16)] * 2,
        compiler_params=pltpu.CompilerParams(vmem_limit_bytes=32 * MIB),
        cost_estimate=pl.CostEstimate(
            flops=6 * rows * depth * count * width,
            bytes_accessed=4 * (rows * depth + count * width * (depth + 2 * rows)),
            transcendentals=0,
        ),
        name="pair_blocks",
    )(left, *shards)
    return out[:count], out[count:]


def density_kernel(count, first, row_ref, column_ref, *refs):
    direct_refs = refs[:count]
    swapped_refs = refs[count : 2 * count]
    shard_refs = refs[2 * count : 3 * count]
    refs = refs[3 * count :]
    if not first:
        before_ref, *refs = refs
    out_ref, high_ref, low_ref, amp_high_ref, amp_low_ref = refs
    width = direct_refs[0].shape[1]

    @pl.when(pl.program_id(0) == 0)
    def _():
        for spot in range(count):
            rows = pl.ds(spot * width, width)
            high_ref[rows, :], low_ref[rows, :] = halves(shard_refs[spot][...])

    for spot in range(count):
        columns = slice(spot * width, (spot + 1) * width)
        denominator = row_ref[...] + column_ref[:, columns]
        amplitude = (swapped_refs[spot][...] - 2.0 * direct_refs[spot][...]) / denominator
        amp_high_ref[:, columns], amp_low_ref[:, columns] = halves(amplitude)
    total = product(
        (amp_high_ref[...], amp_low_ref[...]), (high_ref[...], low_ref[...]), ((1,), (0,))
    )
    out_ref[...] = total if first else before_ref[...] + total


def density_add(before, row_energy, column_energy, direct, swapped, shards):
    count = len(shards)
    width, depth = shards[0].shape
    rows = row_energy.shape[0]
    if width % 128 or rows % 8:
        for spot in range(count):
            denominator = row_energy + column_energy[:, spot * width : (spot + 1) * width]
            amplitude = (swapped[spot] - 2.0 * direct[spot]) / denominator
            term = jnp.dot(amplitude, shards[spot], precision=lax.Precision.HIGHEST)
            before = term if before is None else before + term
        return before
    step = min(rows, 256)
    while rows % step:
        step -= 8
    first = before is None
    by_rows = lambda columns: pl.BlockSpec((step, columns), lambda s: (s, 0))
    whole = lambda height, columns: pl.BlockSpec((height, columns), lambda s: (0, 0))
    return pl.pallas_call(
        functools.partial(density_kernel, count, first),
        grid=(rows // step,),
        in_specs=[by_rows(1), whole(1, count * width)]
        + [by_rows(width)] * (2 * count)
        + [whole(width, depth)] * count
        + ([] if first else [by_rows(depth)]),
        out_specs=by_rows(depth),
        out_shape=jax.ShapeDtypeStruct((rows, depth), F32),
        scratch_shapes=[pltpu.VMEM((count * width, depth), BF16)] * 2
        + [pltpu.VMEM((step, count * width), BF16)] * 2,
        input_output_aliases={} if first else {2 + 3 * count: 0},
        compiler_params=pltpu.CompilerParams(vmem_limit_bytes=40 * MIB),
        cost_estimate=pl.CostEstimate(
            flops=6 * rows * depth * count * width,
            bytes_accessed=4 * (2 * rows * depth + count * width * (depth + 2 * rows)),
            transcendentals=0,
        ),
        name="density_add",
    )(row_energy, column_energy, *direct, *swapped, *shards, *([] if first else [before]))


def across(x, bits):
    size = lax.axis_size(AXIS)
    return lax.ppermute(x, AXIS, [(i, i ^ bits) for i in range(size)])


def body(i_factors, j_factors, occ_i, occ_j, virt_energy):
    size = lax.axis_size(AXIS)
    orbitals, height, depth = j_factors.shape
    width = orbitals * height
    left = i_factors.reshape(-1, depth)
    own = j_factors.reshape(width, depth)

    padded = jnp.zeros((8, 128 * -(-height // 128)), F32).at[0, :height].set(virt_energy)
    energies = lax.all_gather(padded, AXIS, axis=0)[:, 0, :height]
    place = lax.axis_index(AXIS)
    energies = energies[place ^ jnp.arange(size)]
    row_energy = (virt_energy[None, :] - occ_i[:, None]).reshape(-1, 1)
    column_energy = (energies[:, None, :] - occ_j[None, :, None]).reshape(size, width)

    shards = {0: own}
    for k in sorted(range(2, size, 2), key=lambda k: (bin(k).count("1"), -k)):
        low = k & -k
        shards[k] = across(shards[k ^ low], low)
    for k in range(0, size, 2):
        shards[k + 1] = across(shards[k], 1)

    direct, swapped = {}, {}
    order = sorted(range(0, size, 2), key=lambda k: (bin(k).count("1"), -k))
    for k in order:
        group = (k, k + 1)
        ours, messages = pair_blocks(left, [shards[m] for m in group], height, orbitals)
        for m, one, message in zip(group, ours, messages):
            direct[m] = one
            swapped[m] = across(message, m) if m else message

    density = None
    ready = sorted(range(0, size, 2))
    for k in ready:
        group = (k, k + 1)
        density = density_add(
            density,
            row_energy,
            column_energy[k : k + 2].reshape(1, -1),
            [direct[m] for m in group],
            [swapped[m] for m in group],
            [shards[m] for m in group],
        )
    return density.reshape(i_factors.shape)


def solution(mesh):
    placed = (
        P("conf", "virt", None),
        P("conf", "virt", None),
        P("conf"),
        P("conf"),
        P(("conf", "virt")),
    )
    return jax.shard_map(
        body, mesh=mesh, in_specs=placed, out_specs=P("conf", "virt", None), check_vma=False
    )
```

time: 507 us -> 356 us (0.70); the launches traced: 498 us -> 354 us
  matrix products: 137 us -> 0 us
  Pallas kernels: 0 us -> 129 us
  local copies, waits for them, and re-layouts: 96 us -> 18.1 us
  blocking collectives: 109 us -> 34.7 us
  starting transfers between devices: 10.9 us -> 57.5 us
  other arithmetic: 27.6 us -> 0.16 us
  between operations: 14.6 us -> 0.25 us
  waiting for transfers between devices: 103 us -> 114 us
    dot_general x4 -> x0, matrix products: 137 us -> none  [the longest x2 69.6 us: body(): jnp.einsum('iab,bp->iap', amplitude, whole_rows, precision=lax.Precision....]
    pallas_call x0 -> x16, Pallas kernels: none -> 129 us  [the longest x8 76.2 us: density_add(): pl.pallas_call(functools.partial(density_kernel, count, first), grid=(row...]
    ppermute x0 -> x30, waiting for transfers between devices: none -> 114 us  [across(): return lax.ppermute(x, AXIS, [(i, i ^ bits) for i in range(size)])]
    unnamed x1 -> x0, blocking collectives: 109 us -> none
    all_gather x2 -> x0, waiting for transfers between devices: 78.4 us -> none  [body(): lax.all_gather(j_factors[index], 'virt', axis=0, tiled=True)]
    ppermute x0 -> x30, starting transfers between devices: none -> 57.5 us  [across(): return lax.ppermute(x, AXIS, [(i, i ^ bits) for i in range(size)])]
    all_gather x0 -> x1, blocking collectives: none -> 34.7 us  [body(): energies = lax.all_gather(padded, AXIS, axis=0)[:, 0, :height]]
    all_to_all x2 -> x0, other arithmetic: 27.6 us -> none  [body(): lax.all_to_all(transpose_blocks(pair_block, blocks), 'virt', split_axis=2...]
  transfers between devices with their start and end apart: 4 -> 30, of which waited for: 3 -> 13; matrix products, arithmetic and copies ran while one was open for 32% -> 1% of each run, Pallas kernels for 0% -> 34%
where the time goes in v1:
time: 356 us; the launch traced here: 354 us
  Pallas kernels  129 us (36%)
  waiting for transfers between devices  114 us (32%)
  starting transfers between devices  57.5 us (16%)
  blocking collectives  34.7 us (10%)
  local copies, waits for them, and re-layouts  18.1 us (5%)
    ppermute x30, waiting for transfers between devices, across(): return lax.ppermute(x, AXIS, [(i, i ^ bits) for i in range(size)])  114 us
    pallas_call x8, Pallas kernels, density_add(): pl.pallas_call(functools.partial(density_kernel, count, first), grid=(row...  76.2 us
    ppermute x30, starting transfers between devices, across(): return lax.ppermute(x, AXIS, [(i, i ^ bits) for i in range(size)])  57.5 us
    pallas_call x8, Pallas kernels, pair_blocks(): pl.pallas_call(functools.partial(pair_kernel, count, height, orbitals), g...  52.4 us
    all_gather x1, blocking collectives, body(): energies = lax.all_gather(padded, AXIS, axis=0)[:, 0, :height]  34.7 us
    unnamed x30, local copies, waits for them, and re-layouts  16.4 us
  transfers between devices with their start and end apart: 30, of which 13 were waited for; matrix products, arithmetic and copies ran while one was open for 1% of the time, Pallas kernels for 34%

profile of v1, /device:TPU:16, one launch (start us, length us, event | category | flops | bytes accessed | tf_op | source)
XLA Modules:
  0.0 353.5 jit_solution(15087192909922852184)
XLA Ops:
  0.0 1.6 collective-permute-start.24
  1.6 1.6 collective-permute-start.16
  3.5 21.8 %collective-permute-done.24.refs_0_.refs_4_ = f32[128,2048]{1,0:T(8,128)} collective-permute-done((f32[128,2048]{1,0:T(8,128)}, f32[128,2048]{1,0:T(8,128)}, u32[]{:S(2)}, u32[]{:S(2)}) %collective-permute-start.24) | collective-permute-done | bytes 1048608 | tf_op jit(solution)/shard_map/ppermute | solution.py:153
  25.3 1.2 copy-done
  26.5 3.4 copy-done.6
  29.9 6.0 %pair_blocks.15 = (f32[1024,128]{1,0:T(8,128)S(1)}, f32[1024,128]{1,0:T(8,128)S(1)}, f32[1024,128]{1,0:T(8,128)S(1)}, f32[1024,128]{1,0:T(8,128)}) custom-call(f32[1024,2048]{1,0:T(8,128)S(1)} %bitcast.15, f32[128,2048]{1,0:T(8,128)S(1)} %bitcast.13, f32[128,2048]{1,0:T(8,128)S(1)} %collective-permute-done.28.refs_1_.refs_5_), custom_call_target="tpu_custom_call" | custom-call | flops 3221225472 | bytes 12582912 | tf_op jit(solution)/shard_map/pair_blocks/pallas_call | solution.py:66
  38.1 9.8 %collective-permute-done.16.refs_0_.refs_4_ = f32[128,2048]{1,0:T(8,128)} collective-permute-done((f32[128,2048]{1,0:T(8,128)}, f32[128,2048]{1,0:T(8,128)}, u32[]{:S(2)}, u32[]{:S(2)}) %collective-permute-start.16) | collective-permute-done | bytes 1048608 | tf_op jit(solution)/shard_map/ppermute | solution.py:153
  48.9 34.7 %all_gather.7 = f32[16,8,128]{2,1,0:T(8,128)S(1)} all-gather(f32[1,8,128]{2,1,0:T(8,128)S(1)} %scatter.4), channel_id=1, replica_groups=mesh['conf'=2,'virt'=16] {'virt'}, dimensions={0}, use_global_device_ids=true | all-gather | bytes 69632 | tf_op jit(solution)/shard_map/all_gather | solution.py:164
  84.6 1.8 collective-permute-start.9
  86.5 1.5 collective-permute-start.1
  88.6 3.4 copy-done.7
  92.0 6.9 %pair_blocks.14 = (f32[1024,128]{1,0:T(8,128)S(1)}, f32[1024,128]{1,0:T(8,128)S(1)}, f32[1024,128]{1,0:T(8,128)S(1)}, f32[1024,128]{1,0:T(8,128)S(1)}) custom-call(f32[1024,2048]{1,0:T(8,128)S(1)} %bitcast.16, f32[128,2048]{1,0:T(8,128)} %collective-permute-done.24.refs_0_.refs_4_, f32[128,2048]{1,0:T(8,128)} %collective-permute-done.25.refs_1_.refs_5_), custom_call_target="tpu_custom_call" | custom-call | flops 3221225472 | bytes 12582912 | tf_op jit(solution)/shard_map/pair_blocks/pallas_call | solution.py:66
  100.1 7.1 %pair_blocks.13 = (f32[1024,128]{1,0:T(8,128)S(1)}, f32[1024,128]{1,0:T(8,128)S(1)}, f32[1024,128]{1,0:T(8,128)S(1)}, f32[1024,128]{1,0:T(8,128)S(1)}) custom-call(f32[1024,2048]{1,0:T(8,128)S(1)} %bitcast.17, f32[128,2048]{1,0:T(8,128)} %collective-permute-done.16.refs_0_.refs_4_, f32[128,2048]{1,0:T(8,128)} %collective-permute-done.21.refs_1_.refs_5_), custom_call_target="tpu_custom_call" | custom-call | flops 3221225472 | bytes 12582912 | tf_op jit(solution)/shard_map/pair_blocks/pallas_call | solution.py:66
  107.8 2.9 collective-permute-done.9.refs_0_.refs_4_
  110.7 7.2 %density_add.8.refs_6_ = f32[1024,2048]{1,0:T(8,128)} custom-call(f32[1024,1]{1,0:T(8,128)S(1)} %sub.43.row_ref, f32[1,256]{1,0:T(1,128)S(1)} %reshape.133.column_ref, f32[1024,128]{1,0:T(8,128)S(1)} %get-tuple-element.77.refs_0_, f32[1024,128]{1,0:T(8,128)S(1)} %copy-done.3, f32[1024,128]{1,0:T(8,128)S(1)} %copy-done.5, ...), custom_call_target="tpu_custom_call" | custom-call | flops 3221225472 | bytes 20971520 | tf_op jit(solution)/shard_map/density_add/pallas_call | solution.py:129
  117.9 1.9 collective-permute-start.23
  119.8 2.0 collective-permute-done.26.refs_2_
  121.8 9.9 %collective-permute-done.27.refs_3_ = f32[1024,128]{1,0:T(8,128)S(1)} collective-permute-done((f32[1024,128]{1,0:T(8,128)S(1)}, f32[1024,128]{1,0:T(8,128)S(1)}, u32[]{:S(2)}, u32[]{:S(2)}) %collective-permute-start.27) | collective-permute-done | bytes 524320 | tf_op jit(solution)/shard_map/ppermute | solution.py:153
  131.7 1.7 collective-permute-start.2
  133.3 6.7 %pair_blocks.11 = (f32[1024,128]{1,0:T(8,128)S(1)}, f32[1024,128]{1,0:T(8,128)S(1)}, f32[1024,128]{1,0:T(8,128)S(1)}, f32[1024,128]{1,0:T(8,128)S(1)}) custom-call(f32[1024,2048]{1,0:T(8,128)S(1)} %bitcast.20, f32[128,2048]{1,0:T(8,128)S(1)} %collective-permute-done.refs_0_.refs_4_, f32[128,2048]{1,0:T(8,128)} %collective-permute-done.13.refs_1_.refs_5_), custom_call_target="tpu_custom_call" | custom-call | flops 3221225472 | bytes 12582912 | tf_op jit(solution)/shard_map/pair_blocks/pallas_call | solution.py:66
  140.4 10.1 %density_add.9.refs_6_ = f32[1024,2048]{1,0:T(8,128)} custom-call(f32[1024,1]{1,0:T(8,128)S(1)} %sub.43.row_ref, f32[1,256]{1,0:T(1,128)S(1)} %reshape.132.column_ref, f32[1024,128]{1,0:T(8,128)S(1)} %get-tuple-element.73.refs_0_, f32[1024,128]{1,0:T(8,128)S(1)} %get-tuple-element.74.refs_1_, ...), custom_call_target="tpu_custom_call", output_to_operand_aliasing={{}: (8, {})} | custom-call | flops 3221225472 | bytes 20971520 | tf_op jit(solution)/shard_map/density_add/pallas_call | solution.py:129
  150.5 4.1 %collective-permute-start.14 = (f32[1024,128]{1,0:T(8,128)S(1)}, f32[1024,128]{1,0:T(8,128)S(1)}, u32[]{:S(2)}, u32[]{:S(2)}) collective-permute-start(f32[1024,128]{1,0:T(8,128)S(1)} %get-tuple-element.63), channel_id=1, source_target_pairs={{0,8},{1,9},{2,10},{3,11},{4,12},{5,13},{6,14},{7,15},{8,0},{9,1},... | collective-permute-start | bytes 1572872 | tf_op jit(solution)/shard_map/ppermute | solution.py:153
  154.6 10.1 %density_add.10.refs_6_ = f32[1024,2048]{1,0:T(8,128)} custom-call(f32[1024,1]{1,0:T(8,128)S(1)} %sub.43.row_ref, f32[1,256]{1,0:T(1,128)S(1)} %reshape.131.column_ref, f32[1024,128]{1,0:T(8,128)S(1)} %get-tuple-element.69.refs_0_, f32[1024,128]{1,0:T(8,128)S(1)} %get-tuple-element.70.refs_1_, ...), custom_call_target="tpu_custom_call", output_to_operand_aliasing={{}: (8, {})} | custom-call | flops 3221225472 | bytes 20971520 | tf_op jit(solution)/shard_map/density_add/pallas_call | solution.py:129
  164.8 6.7 %pair_blocks.12 = (f32[1024,128]{1,0:T(8,128)S(1)}, f32[1024,128]{1,0:T(8,128)S(1)}, f32[1024,128]{1,0:T(8,128)S(1)}, f32[1024,128]{1,0:T(8,128)S(1)}) custom-call(f32[1024,2048]{1,0:T(8,128)S(1)} %bitcast.21, f32[128,2048]{1,0:T(8,128)} %collective-permute-done.17.refs_0_.refs_4_, f32[128,2048]{1,0:T(8,128)S(1)} %collective-permute-done.18.refs_1_.refs_5_), custom_call_target="tpu_custom_call" | custom-call | flops 3221225472 | bytes 12582912 | tf_op jit(solution)/shard_map/pair_blocks/pallas_call | solution.py:66
  171.6 2.2 collective-permute-start.20
  173.8 0.8 collective-permute-start.3
  174.6 3.4 copy-done.8
  178.0 6.6 %pair_blocks.10 = (f32[1024,128]{1,0:T(8,128)S(1)}, f32[1024,128]{1,0:T(8,128)S(1)}, f32[1024,128]{1,0:T(8,128)S(1)}, f32[1024,128]{1,0:T(8,128)S(1)}) custom-call(f32[1024,2048]{1,0:T(8,128)S(1)} %bitcast.22, f32[128,2048]{1,0:T(8,128)} %collective-permute-done.9.refs_0_.refs_4_, f32[128,2048]{1,0:T(8,128)S(1)} %collective-permute-done.10.refs_1_.refs_5_), custom_call_target="tpu_custom_call" | custom-call | flops 3221225472 | bytes 12582912 | tf_op jit(solution)/shard_map/pair_blocks/pallas_call | solution.py:66
  184.7 6.9 %pair_blocks.9 = (f32[1024,128]{1,0:T(8,128)S(1)}, f32[1024,128]{1,0:T(8,128)S(1)}, f32[1024,128]{1,0:T(8,128)S(1)}, f32[1024,128]{1,0:T(8,128)S(1)}) custom-call(f32[1024,2048]{1,0:T(8,128)S(1)} %bitcast.23, f32[128,2048]{1,0:T(8,128)} %collective-permute-done.1.refs_0_.refs_4_, f32[128,2048]{1,0:T(8,128)S(1)} %collective-permute-done.6.refs_1_.refs_5_), custom_call_target="tpu_custom_call" | custom-call | flops 3221225472 | bytes 12582912 | tf_op jit(solution)/shard_map/pair_blocks/pallas_call | solution.py:66
  191.6 2.8 collective-permute-done.19.refs_2_
  194.4 8.0 %collective-permute-start.11 = (f32[1024,128]{1,0:T(8,128)S(1)}, f32[1024,128]{1,0:T(8,128)S(1)}, u32[]{:S(2)}, u32[]{:S(2)}) collective-permute-start(f32[1024,128]{1,0:T(8,128)S(1)} %get-tuple-element.59), channel_id=1, source_target_pairs={{0,10},{1,11},{2,8},{3,9},{4,14},{5,15},{6,12},{7,13},{8,2},{9,3},... | collective-permute-start | bytes 1572872 | tf_op jit(solution)/shard_map/ppermute | solution.py:153
  202.5 3.7 %collective-permute-done.20.refs_3_ = f32[1024,128]{1,0:T(8,128)S(1)} collective-permute-done((f32[1024,128]{1,0:T(8,128)S(1)}, f32[1024,128]{1,0:T(8,128)S(1)}, u32[]{:S(2)}, u32[]{:S(2)}) %collective-permute-start.20) | collective-permute-done | bytes 524320 | tf_op jit(solution)/shard_map/ppermute | solution.py:153
  206.1 7.2 %collective-permute-start.12 = (f32[1024,128]{1,0:T(8,128)S(1)}, f32[1024,128]{1,0:T(8,128)S(1)}, u32[]{:S(2)}, u32[]{:S(2)}) collective-permute-start(f32[1024,128]{1,0:T(8,128)S(1)} %get-tuple-element.60), channel_id=1, source_target_pairs={{0,11},{1,10},{2,9},{3,8},{4,15},{5,14},{6,13},{7,12},{8,3},{9,2},... | collective-permute-start | bytes 1572872 | tf_op jit(solution)/shard_map/ppermute | solution.py:153
  213.3 9.8 %density_add.11.refs_6_ = f32[1024,2048]{1,0:T(8,128)} custom-call(f32[1024,1]{1,0:T(8,128)S(1)} %sub.43.row_ref, f32[1,256]{1,0:T(1,128)S(1)} %reshape.130.column_ref, f32[1024,128]{1,0:T(8,128)S(1)} %get-tuple-element.65.refs_0_, f32[1024,128]{1,0:T(8,128)S(1)} %get-tuple-element.66.refs_1_, ...), custom_call_target="tpu_custom_call", output_to_operand_aliasing={{}: (8, {})} | custom-call | flops 3221225472 | bytes 20971520 | tf_op jit(solution)/shard_map/density_add/pallas_call | solution.py:129
  223.2 19.1 %collective-permute-start.8 = (f32[1024,128]{1,0:T(8,128)S(1)}, f32[1024,128]{1,0:T(8,128)S(1)}, u32[]{:S(2)}, u32[]{:S(2)}) collective-permute-start(f32[1024,128]{1,0:T(8,128)S(1)} %get-tuple-element.56), channel_id=1, source_target_pairs={{0,13},{1,12},{2,15},{3,14},{4,9},{5,8},{6,11},{7,10},{8,5},{9,4},... | collective-permute-start | bytes 1572872 | tf_op jit(solution)/shard_map/ppermute | solution.py:153
  242.3 9.8 %density_add.12.refs_6_ = f32[1024,2048]{1,0:T(8,128)} custom-call(f32[1024,1]{1,0:T(8,128)S(1)} %sub.43.row_ref, f32[1,256]{1,0:T(1,128)S(1)} %reshape.129.column_ref, f32[1024,128]{1,0:T(8,128)S(1)} %get-tuple-element.61.refs_0_, f32[1024,128]{1,0:T(8,128)S(1)} %get-tuple-element.62.refs_1_, ...), custom_call_target="tpu_custom_call", output_to_operand_aliasing={{}: (8, {})} | custom-call | flops 3221225472 | bytes 20971520 | tf_op jit(solution)/shard_map/density_add/pallas_call | solution.py:129
  252.1 3.4 copy-done.9
  255.5 5.4 %pair_blocks.8 = (f32[1024,128]{1,0:T(8,128)S(1)}, f32[1024,128]{1,0:T(8,128)S(1)}, f32[1024,128]{1,0:T(8,128)S(1)}, f32[1024,128]{1,0:T(8,128)S(1)}) custom-call(f32[1024,2048]{1,0:T(8,128)S(1)} %bitcast.24, f32[128,2048]{1,0:T(8,128)S(1)} %collective-permute-done.2.refs_0_.refs_4_, f32[128,2048]{1,0:T(8,128)S(1)} %collective-permute-done.3.refs_1_.refs_5_), custom_call_target="tpu_custom_call" | custom-call | flops 3221225472 | bytes 12582912 | tf_op jit(solution)/shard_map/pair_blocks/pallas_call | solution.py:66
  260.9 1.3 collective-permute-start.4
  262.2 1.7 collective-permute-done.11.refs_2_
  264.6 33.0 %collective-permute-done.12.refs_3_ = f32[1024,128]{1,0:T(8,128)S(1)} collective-permute-done((f32[1024,128]{1,0:T(8,128)S(1)}, f32[1024,128]{1,0:T(8,128)S(1)}, u32[]{:S(2)}, u32[]{:S(2)}) %collective-permute-start.12) | collective-permute-done | bytes 524320 | tf_op jit(solution)/shard_map/ppermute | solution.py:153
  297.6 9.8 %density_add.13.refs_6_ = f32[1024,2048]{1,0:T(8,128)} custom-call(f32[1024,1]{1,0:T(8,128)S(1)} %sub.43.row_ref, f32[1,256]{1,0:T(1,128)S(1)} %reshape.128.column_ref, f32[1024,128]{1,0:T(8,128)S(1)} %get-tuple-element.57.refs_0_, f32[1024,128]{1,0:T(8,128)S(1)} %get-tuple-element.58.refs_1_, ...), custom_call_target="tpu_custom_call", output_to_operand_aliasing={{}: (8, {})} | custom-call | flops 3221225472 | bytes 20971520 | tf_op jit(solution)/shard_map/density_add/pallas_call | solution.py:129
  307.4 4.0 %collective-permute-done.7.refs_2_ = f32[1024,128]{1,0:T(8,128)S(1)} collective-permute-done((f32[1024,128]{1,0:T(8,128)S(1)}, f32[1024,128]{1,0:T(8,128)S(1)}, u32[]{:S(2)}, u32[]{:S(2)}) %collective-permute-start.7) | collective-permute-done | bytes 524320 | tf_op jit(solution)/shard_map/ppermute | solution.py:153
  311.4 10.3 %collective-permute-done.8.refs_3_ = f32[1024,128]{1,0:T(8,128)S(1)} collective-permute-done((f32[1024,128]{1,0:T(8,128)S(1)}, f32[1024,128]{1,0:T(8,128)S(1)}, u32[]{:S(2)}, u32[]{:S(2)}) %collective-permute-start.8) | collective-permute-done | bytes 524320 | tf_op jit(solution)/shard_map/ppermute | solution.py:153
  321.7 9.8 %density_add.14.refs_6_ = f32[1024,2048]{1,0:T(8,128)} custom-call(f32[1024,1]{1,0:T(8,128)S(1)} %sub.43.row_ref, f32[1,256]{1,0:T(1,128)S(1)} %reshape.127.column_ref, f32[1024,128]{1,0:T(8,128)S(1)} %get-tuple-element.53.refs_0_, f32[1024,128]{1,0:T(8,128)S(1)} %get-tuple-element.54.refs_1_, ...), custom_call_target="tpu_custom_call", output_to_operand_aliasing={{}: (8, {})} | custom-call | flops 3221225472 | bytes 20971520 | tf_op jit(solution)/shard_map/density_add/pallas_call | solution.py:129
  331.5 2.4 collective-permute-done.4.refs_2_
  333.9 10.1 %collective-permute-done.5.refs_3_ = f32[1024,128]{1,0:T(8,128)S(1)} collective-permute-done((f32[1024,128]{1,0:T(8,128)S(1)}, f32[1024,128]{1,0:T(8,128)S(1)}, u32[]{:S(2)}, u32[]{:S(2)}) %collective-permute-start.5) | collective-permute-done | bytes 524320 | tf_op jit(solution)/shard_map/ppermute | solution.py:153
  344.0 9.5 %density_add.15 = f32[1024,2048]{1,0:T(8,128)} custom-call(f32[1024,1]{1,0:T(8,128)S(1)} %sub.43.row_ref, f32[1,256]{1,0:T(1,128)S(1)} %reshape.124.column_ref, f32[1024,128]{1,0:T(8,128)S(1)} %get-tuple-element.49.refs_0_, f32[1024,128]{1,0:T(8,128)S(1)} %get-tuple-element.50.refs_1_, ...), custom_call_target="tpu_custom_call", output_to_operand_aliasing={{}: (8, {})} | custom-call | flops 3221225472 | bytes 20971520 | tf_op jit(solution)/shard_map/density_add/pallas_call | solution.py:129
  (77 shorter events, 8.2 us)
Async XLA Ops:
  0.0 48.3 %copy-start.10 = (f32[64]{0:T(128)S(1)}, f32[64]{0:T(128)}, u32[]{:S(2)}) copy-start(f32[64]{0:T(128)} %param.11) | copy-start | bytes 772
  0.0 48.3 %copy-start.11 = (f32[16]{0:T(128)S(1)}, f32[16]{0:T(128)}, u32[]{:S(2)}) copy-start(f32[16]{0:T(128)} %param.9) | copy-start | bytes 196
  0.0 86.4 %copy-start.12 = (f32[2]{0:T(128)S(1)}, f32[2]{0:T(128)}, u32[]{:S(2)}) copy-start(f32[2]{0:T(128)} %param.10) | copy-start | bytes 28
  0.0 25.3 %collective-permute-start.24 = (f32[128,2048]{1,0:T(8,128)}, f32[128,2048]{1,0:T(8,128)}, u32[]{:S(2)}, u32[]{:S(2)}) collective-permute-start(f32[128,2048]{1,0:T(8,128)} %bitcast.9), channel_id=1, source_target_pairs={{0,2},{1,3},{2,0},{3,1},{4,6},{5,7},{6,4},{7,5},{8,10},{9,11},{10,... | collective-permute-start | bytes 3145736 | tf_op jit(solution)/shard_map/ppermute | solution.py:153
  1.6 23.7 %collective-permute-start.28 = (f32[128,2048]{1,0:T(8,128)}, f32[128,2048]{1,0:T(8,128)S(1)}, u32[]{:S(2)}, u32[]{:S(2)}) collective-permute-start(f32[128,2048]{1,0:T(8,128)} %bitcast.10), channel_id=1, source_target_pairs={{0,1},{1,0},{2,3},{3,2},{4,5},{5,4},{6,7},{7,6},{8,9},{9,8},{10,11... | collective-permute-start | bytes 3145736 | tf_op jit(solution)/shard_map/ppermute | solution.py:153
  1.6 46.2 %collective-permute-start.16 = (f32[128,2048]{1,0:T(8,128)}, f32[128,2048]{1,0:T(8,128)}, u32[]{:S(2)}, u32[]{:S(2)}) collective-permute-start(f32[128,2048]{1,0:T(8,128)} %bitcast.11), channel_id=1, source_target_pairs={{0,4},{1,5},{2,6},{3,7},{4,0},{5,1},{6,2},{7,3},{8,12},{9,13},{10,... | collective-permute-start | bytes 3145736 | tf_op jit(solution)/shard_map/ppermute | solution.py:153
  3.2 81.0 %collective-permute-start = (f32[128,2048]{1,0:T(8,128)}, f32[128,2048]{1,0:T(8,128)S(1)}, u32[]{:S(2)}, u32[]{:S(2)}) collective-permute-start(f32[128,2048]{1,0:T(8,128)} %bitcast.12), channel_id=1, source_target_pairs={{0,8},{1,9},{2,10},{3,11},{4,12},{5,13},{6,14},{7,15},{8,0},{9,1},... | collective-permute-start | bytes 3145736 | tf_op jit(solution)/shard_map/ppermute | solution.py:153
  25.3 61.2 %collective-permute-start.25 = (f32[128,2048]{1,0:T(8,128)}, f32[128,2048]{1,0:T(8,128)}, u32[]{:S(2)}, u32[]{:S(2)}) collective-permute-start(f32[128,2048]{1,0:T(8,128)} %collective-permute-done.24.refs_0_.refs_4_), channel_id=1, source_target_pairs={{0,1},{1,0},{2,3},{3,2},{4,5},{5,4},{6,7},{7,6},{8,9},{9,8},{10,11... | collective-permute-start | bytes 3145736 | tf_op jit(solution)/shard_map/ppermute | solution.py:153
  25.3 1.2 copy-start
  26.5 3.4 copy-start.6
  36.0 0.8 copy-start.2
  36.8 0.8 copy-start.4
  37.6 47.0 %collective-permute-start.29 = (f32[1024,128]{1,0:T(8,128)}, f32[1024,128]{1,0:T(8,128)}, u32[]{:S(2)}, u32[]{:S(2)}) collective-permute-start(f32[1024,128]{1,0:T(8,128)} %get-tuple-element.80), channel_id=1, source_target_pairs={{0,1},{1,0},{2,3},{3,2},{4,5},{5,4},{6,7},{7,6},{8,9},{9,8},{10,11... | collective-permute-start | bytes 1572872 | tf_op jit(solution)/shard_map/ppermute | solution.py:153
  47.8 51.2 %collective-permute-start.21 = (f32[128,2048]{1,0:T(8,128)}, f32[128,2048]{1,0:T(8,128)}, u32[]{:S(2)}, u32[]{:S(2)}) collective-permute-start(f32[128,2048]{1,0:T(8,128)} %collective-permute-done.16.refs_0_.refs_4_), channel_id=1, source_target_pairs={{0,1},{1,0},{2,3},{3,2},{4,5},{5,4},{6,7},{7,6},{8,9},{9,8},{10,11... | collective-permute-start | bytes 3145736 | tf_op jit(solution)/shard_map/ppermute | solution.py:153
  47.8 51.8 %collective-permute-start.17 = (f32[128,2048]{1,0:T(8,128)}, f32[128,2048]{1,0:T(8,128)}, u32[]{:S(2)}, u32[]{:S(2)}) collective-permute-start(f32[128,2048]{1,0:T(8,128)} %collective-permute-done.16.refs_0_.refs_4_), channel_id=1, source_target_pairs={{0,2},{1,3},{2,0},{3,1},{4,6},{5,7},{6,4},{7,5},{8,10},{9,11},{10,... | collective-permute-start | bytes 3145736 | tf_op jit(solution)/shard_map/ppermute | solution.py:153
  84.2 23.0 %collective-permute-start.13 = (f32[128,2048]{1,0:T(8,128)S(1)}, f32[128,2048]{1,0:T(8,128)}, u32[]{:S(2)}, u32[]{:S(2)}) collective-permute-start(f32[128,2048]{1,0:T(8,128)S(1)} %collective-permute-done.refs_0_.refs_4_), channel_id=1, source_target_pairs={{0,1},{1,0},{2,3},{3,2},{4,5},{5,4},{6,7},{7,6},{8,9},{9,8},{10,11... | collective-permute-start | bytes 3145736 | tf_op jit(solution)/shard_map/ppermute | solution.py:153
  84.6 26.1 %collective-permute-start.9 = (f32[128,2048]{1,0:T(8,128)S(1)}, f32[128,2048]{1,0:T(8,128)}, u32[]{:S(2)}, u32[]{:S(2)}) collective-permute-start(f32[128,2048]{1,0:T(8,128)S(1)} %collective-permute-done.refs_0_.refs_4_), channel_id=1, source_target_pairs={{0,2},{1,3},{2,0},{3,1},{4,6},{5,7},{6,4},{7,5},{8,10},{9,11},{10,... | collective-permute-start | bytes 3145736 | tf_op jit(solution)/shard_map/ppermute | solution.py:153
  86.5 31.4 %collective-permute-start.1 = (f32[128,2048]{1,0:T(8,128)S(1)}, f32[128,2048]{1,0:T(8,128)}, u32[]{:S(2)}, u32[]{:S(2)}) collective-permute-start(f32[128,2048]{1,0:T(8,128)S(1)} %collective-permute-done.refs_0_.refs_4_), channel_id=1, source_target_pairs={{0,4},{1,5},{2,6},{3,7},{4,0},{5,1},{6,2},{7,3},{8,12},{9,13},{10,... | collective-permute-start | bytes 3145736 | tf_op jit(solution)/shard_map/ppermute | solution.py:153
  88.6 3.4 copy-start.7
  99.0 11.7 %copy-start.1 = (f32[2,64,2048]{2,1,0:T(8,128)S(1)}, f32[2,64,2048]{2,1,0:T(8,128)}, u32[]{:S(2)}) copy-start(f32[2,64,2048]{2,1,0:T(8,128)} %param.8) | copy-start | bytes 3145732
  99.0 11.7 %copy-start.3 = (f32[1024,128]{1,0:T(8,128)S(1)}, f32[1024,128]{1,0:T(8,128)}, u32[]{:S(2)}) copy-start(f32[1024,128]{1,0:T(8,128)} %copy-done.2) | copy-start | bytes 1572868
  99.0 11.7 %copy-start.5 = (f32[1024,128]{1,0:T(8,128)S(1)}, f32[1024,128]{1,0:T(8,128)}, u32[]{:S(2)}) copy-start(f32[1024,128]{1,0:T(8,128)} %copy-done.4) | copy-start | bytes 1572868
  99.0 22.8 %collective-permute-start.26 = (f32[1024,128]{1,0:T(8,128)S(1)}, f32[1024,128]{1,0:T(8,128)S(1)}, u32[]{:S(2)}, u32[]{:S(2)}) collective-permute-start(f32[1024,128]{1,0:T(8,128)S(1)} %get-tuple-element.75), channel_id=1, source_target_pairs={{0,2},{1,3},{2,0},{3,1},{4,6},{5,7},{6,4},{7,5},{8,10},{9,11},{10,... | collective-permute-start | bytes 1572872 | tf_op jit(solution)/shard_map/ppermute | solution.py:153
  99.6 32.1 %collective-permute-start.27 = (f32[1024,128]{1,0:T(8,128)S(1)}, f32[1024,128]{1,0:T(8,128)S(1)}, u32[]{:S(2)}, u32[]{:S(2)}) collective-permute-start(f32[1024,128]{1,0:T(8,128)S(1)} %get-tuple-element.76), channel_id=1, source_target_pairs={{0,3},{1,2},{2,1},{3,0},{4,7},{5,6},{6,5},{7,4},{8,11},{9,10},{10,... | collective-permute-start | bytes 1572872 | tf_op jit(solution)/shard_map/ppermute | solution.py:153
  100.1 33.3 %slice-start = ((s8[8388608]{0:T(1024)(128)(4,1)}), s8[4194304]{0:T(1024)(128)(4,1)S(1)}, s32[]{:S(2)}) async-start(s8[8388608]{0:T(1024)(128)(4,1)} %bitcast.18), calls=%async_computation | async-start | bytes 8388608
  107.2 32.9 %collective-permute-start.22 = (f32[1024,128]{1,0:T(8,128)S(1)}, f32[1024,128]{1,0:T(8,128)S(1)}, u32[]{:S(2)}, u32[]{:S(2)}) collective-permute-start(f32[1024,128]{1,0:T(8,128)S(1)} %get-tuple-element.71), channel_id=1, source_target_pairs={{0,4},{1,5},{2,6},{3,7},{4,0},{5,1},{6,2},{7,3},{8,12},{9,13},{10,... | collective-permute-start | bytes 1572872 | tf_op jit(solution)/shard_map/ppermute | solution.py:153
  110.7 54.1 %collective-permute-start.18 = (f32[128,2048]{1,0:T(8,128)}, f32[128,2048]{1,0:T(8,128)S(1)}, u32[]{:S(2)}, u32[]{:S(2)}) collective-permute-start(f32[128,2048]{1,0:T(8,128)} %collective-permute-done.17.refs_0_.refs_4_), channel_id=1, source_target_pairs={{0,1},{1,0},{2,3},{3,2},{4,5},{5,4},{6,7},{7,6},{8,9},{9,8},{10,11... | collective-permute-start | bytes 3145736 | tf_op jit(solution)/shard_map/ppermute | solution.py:153
  110.7 22.6 %slice-start.1 = ((s8[8388608]{0:T(1024)(128)(4,1)}), s8[4194304]{0:T(1024)(128)(4,1)S(1)}, s32[]{:S(2)}) async-start(s8[8388608]{0:T(1024)(128)(4,1)} %bitcast.18), calls=%async_computation.1 | async-start | bytes 8388608
  117.9 32.6 %collective-permute-start.23 = (f32[1024,128]{1,0:T(8,128)S(1)}, f32[1024,128]{1,0:T(8,128)S(1)}, u32[]{:S(2)}, u32[]{:S(2)}) collective-permute-start(f32[1024,128]{1,0:T(8,128)S(1)} %get-tuple-element.72), channel_id=1, source_target_pairs={{0,5},{1,4},{2,7},{3,6},{4,1},{5,0},{6,3},{7,2},{8,13},{9,12},{10,... | collective-permute-start | bytes 1572872 | tf_op jit(solution)/shard_map/ppermute | solution.py:153
  121.8 49.8 %collective-permute-start.10 = (f32[128,2048]{1,0:T(8,128)}, f32[128,2048]{1,0:T(8,128)S(1)}, u32[]{:S(2)}, u32[]{:S(2)}) collective-permute-start(f32[128,2048]{1,0:T(8,128)} %collective-permute-done.9.refs_0_.refs_4_), channel_id=1, source_target_pairs={{0,1},{1,0},{2,3},{3,2},{4,5},{5,4},{6,7},{7,6},{8,9},{9,8},{10,11... | collective-permute-start | bytes 3145736 | tf_op jit(solution)/shard_map/ppermute | solution.py:153
  131.7 42.1 %collective-permute-start.2 = (f32[128,2048]{1,0:T(8,128)}, f32[128,2048]{1,0:T(8,128)S(1)}, u32[]{:S(2)}, u32[]{:S(2)}) collective-permute-start(f32[128,2048]{1,0:T(8,128)} %collective-permute-done.1.refs_0_.refs_4_), channel_id=1, source_target_pairs={{0,2},{1,3},{2,0},{3,1},{4,6},{5,7},{6,4},{7,5},{8,10},{9,11},{10,... | collective-permute-start | bytes 3145736 | tf_op jit(solution)/shard_map/ppermute | solution.py:153
  140.0 44.6 %collective-permute-start.6 = (f32[128,2048]{1,0:T(8,128)}, f32[128,2048]{1,0:T(8,128)S(1)}, u32[]{:S(2)}, u32[]{:S(2)}) collective-permute-start(f32[128,2048]{1,0:T(8,128)} %collective-permute-done.1.refs_0_.refs_4_), channel_id=1, source_target_pairs={{0,1},{1,0},{2,3},{3,2},{4,5},{5,4},{6,7},{7,6},{8,9},{9,8},{10,11... | collective-permute-start | bytes 3145736 | tf_op jit(solution)/shard_map/ppermute | solution.py:153
  150.5 72.6 %collective-permute-start.14 = (f32[1024,128]{1,0:T(8,128)S(1)}, f32[1024,128]{1,0:T(8,128)S(1)}, u32[]{:S(2)}, u32[]{:S(2)}) collective-permute-start(f32[1024,128]{1,0:T(8,128)S(1)} %get-tuple-element.63), channel_id=1, source_target_pairs={{0,8},{1,9},{2,10},{3,11},{4,12},{5,13},{6,14},{7,15},{8,0},{9,1},... | collective-permute-start | bytes 1572872 | tf_op jit(solution)/shard_map/ppermute | solution.py:153
  171.5 22.9 %collective-permute-start.19 = (f32[1024,128]{1,0:T(8,128)S(1)}, f32[1024,128]{1,0:T(8,128)S(1)}, u32[]{:S(2)}, u32[]{:S(2)}) collective-permute-start(f32[1024,128]{1,0:T(8,128)S(1)} %get-tuple-element.67), channel_id=1, source_target_pairs={{0,6},{1,7},{2,4},{3,5},{4,2},{5,3},{6,0},{7,1},{8,14},{9,15},{10,... | collective-permute-start | bytes 1572872 | tf_op jit(solution)/shard_map/ppermute | solution.py:153
  171.6 34.6 %collective-permute-start.20 = (f32[1024,128]{1,0:T(8,128)S(1)}, f32[1024,128]{1,0:T(8,128)S(1)}, u32[]{:S(2)}, u32[]{:S(2)}) collective-permute-start(f32[1024,128]{1,0:T(8,128)S(1)} %get-tuple-element.68), channel_id=1, source_target_pairs={{0,7},{1,6},{2,5},{3,4},{4,3},{5,2},{6,1},{7,0},{8,15},{9,14},{10,... | collective-permute-start | bytes 1572872 | tf_op jit(solution)/shard_map/ppermute | solution.py:153
  173.8 78.3 %collective-permute-start.3 = (f32[128,2048]{1,0:T(8,128)S(1)}, f32[128,2048]{1,0:T(8,128)S(1)}, u32[]{:S(2)}, u32[]{:S(2)}) collective-permute-start(f32[128,2048]{1,0:T(8,128)S(1)} %collective-permute-done.2.refs_0_.refs_4_), channel_id=1, source_target_pairs={{0,1},{1,0},{2,3},{3,2},{4,5},{5,4},{6,7},{7,6},{8,9},{9,8},{10,11... | collective-permute-start | bytes 3145736 | tf_op jit(solution)/shard_map/ppermute | solution.py:153
  174.6 3.4 copy-start.8
  184.6 38.5 %collective-permute-start.15 = (f32[1024,128]{1,0:T(8,128)S(1)}, f32[1024,128]{1,0:T(8,128)S(1)}, u32[]{:S(2)}, u32[]{:S(2)}) collective-permute-start(f32[1024,128]{1,0:T(8,128)S(1)} %get-tuple-element.64), channel_id=1, source_target_pairs={{0,9},{1,8},{2,11},{3,10},{4,13},{5,12},{6,15},{7,14},{8,1},{9,0},... | collective-permute-start | bytes 1572872 | tf_op jit(solution)/shard_map/ppermute | solution.py:153
  194.4 69.4 %collective-permute-start.11 = (f32[1024,128]{1,0:T(8,128)S(1)}, f32[1024,128]{1,0:T(8,128)S(1)}, u32[]{:S(2)}, u32[]{:S(2)}) collective-permute-start(f32[1024,128]{1,0:T(8,128)S(1)} %get-tuple-element.59), channel_id=1, source_target_pairs={{0,10},{1,11},{2,8},{3,9},{4,14},{5,15},{6,12},{7,13},{8,2},{9,3},... | collective-permute-start | bytes 1572872 | tf_op jit(solution)/shard_map/ppermute | solution.py:153
  206.1 91.4 %collective-permute-start.12 = (f32[1024,128]{1,0:T(8,128)S(1)}, f32[1024,128]{1,0:T(8,128)S(1)}, u32[]{:S(2)}, u32[]{:S(2)}) collective-permute-start(f32[1024,128]{1,0:T(8,128)S(1)} %get-tuple-element.60), channel_id=1, source_target_pairs={{0,11},{1,10},{2,9},{3,8},{4,15},{5,14},{6,13},{7,12},{8,3},{9,2},... | collective-permute-start | bytes 1572872 | tf_op jit(solution)/shard_map/ppermute | solution.py:153
  223.2 88.2 %collective-permute-start.7 = (f32[1024,128]{1,0:T(8,128)S(1)}, f32[1024,128]{1,0:T(8,128)S(1)}, u32[]{:S(2)}, u32[]{:S(2)}) collective-permute-start(f32[1024,128]{1,0:T(8,128)S(1)} %get-tuple-element.55), channel_id=1, source_target_pairs={{0,12},{1,13},{2,14},{3,15},{4,8},{5,9},{6,10},{7,11},{8,4},{9,5},... | collective-permute-start | bytes 1572872 | tf_op jit(solution)/shard_map/ppermute | solution.py:153
  223.2 98.5 %collective-permute-start.8 = (f32[1024,128]{1,0:T(8,128)S(1)}, f32[1024,128]{1,0:T(8,128)S(1)}, u32[]{:S(2)}, u32[]{:S(2)}) collective-permute-start(f32[1024,128]{1,0:T(8,128)S(1)} %get-tuple-element.56), channel_id=1, source_target_pairs={{0,13},{1,12},{2,15},{3,14},{4,9},{5,8},{6,11},{7,10},{8,5},{9,4},... | collective-permute-start | bytes 1572872 | tf_op jit(solution)/shard_map/ppermute | solution.py:153
  252.1 3.4 copy-start.9
  260.9 73.0 %collective-permute-start.4 = (f32[1024,128]{1,0:T(8,128)S(1)}, f32[1024,128]{1,0:T(8,128)S(1)}, u32[]{:S(2)}, u32[]{:S(2)}) collective-permute-start(f32[1024,128]{1,0:T(8,128)S(1)} %get-tuple-element.51), channel_id=1, source_target_pairs={{0,14},{1,15},{2,12},{3,13},{4,10},{5,11},{6,8},{7,9},{8,6},{9,7},... | collective-permute-start | bytes 1572872 | tf_op jit(solution)/shard_map/ppermute | solution.py:153
  263.9 80.1 %collective-permute-start.5 = (f32[1024,128]{1,0:T(8,128)S(1)}, f32[1024,128]{1,0:T(8,128)S(1)}, u32[]{:S(2)}, u32[]{:S(2)}) collective-permute-start(f32[1024,128]{1,0:T(8,128)S(1)} %get-tuple-element.52), channel_id=1, source_target_pairs={{0,15},{1,14},{2,13},{3,12},{4,11},{5,10},{6,9},{7,8},{8,7},{9,6},... | collective-permute-start | bytes 1572872 | tf_op jit(solution)/shard_map/ppermute | solution.py:153

commit v2 on v1

v2 whole, which is shorter than its diff:
```python
import functools

import jax
import jax.numpy as jnp
from jax import lax
from jax.experimental import pallas as pl
from jax.experimental.pallas import tpu as pltpu
from jax.sharding import PartitionSpec as P

AXIS = "virt"
F32 = jnp.float32
BF16 = jnp.bfloat16
MIB = 1 << 20
CHEAP = pl.CostEstimate(flops=1, bytes_accessed=1, transcendentals=0)


def halves(x):
    high = x.astype(BF16)
    low = (x - high.astype(F32)).astype(BF16)
    return high, low


def product(left, right, dims):
    one = lambda u, v: lax.dot_general(u, v, (dims, ((), ())), preferred_element_type=F32)
    return one(left[0], right[0]) + (one(left[0], right[1]) + one(left[1], right[0]))


def pair_kernel(count, waits, height, orbitals, left_ref, *refs):
    shard_refs = refs[:count]
    refs = refs[:count] + refs[count + waits :]
    direct_refs = refs[count : 2 * count]
    message_refs = refs[2 * count : 3 * count]
    high_ref, low_ref = refs[3 * count :]
    width = orbitals * height

    @pl.when(pl.program_id(0) == 0)
    def _():
        for spot in range(count):
            rows = pl.ds(spot * width, width)
            high_ref[rows, :], low_ref[rows, :] = halves(shard_refs[spot][...])

    block = product(halves(left_ref[...]), (high_ref[...], low_ref[...]), ((1,), (1,)))
    for spot in range(count):
        part = block[:, spot * width : (spot + 1) * width]
        direct_refs[spot][...] = part
        for row in range(0, part.shape[0], height):
            turned = part[row : row + height].T
            message_refs[spot][row : row + height, :] = jnp.concatenate(
                [turned[j * height : (j + 1) * height] for j in range(orbitals)], axis=1
            )


def pair_blocks(left, shards, height, orbitals, after):
    count = len(shards)
    rows, depth = left.shape
    width = orbitals * height
    if width % 128 or height % 8:
        direct, messages = [], []
        for shard in shards:
            block = jnp.dot(left, shard[:width].T, precision=lax.Precision.HIGHEST)
            turned = block.reshape(rows // height, height, orbitals, height)
            direct.append(block)
            messages.append(turned.transpose(0, 3, 2, 1).reshape(rows, width))
        return direct, messages
    step = height * min(rows // height, max(1, 256 // height))
    while rows % step:
        step -= height
    out = pl.pallas_call(
        functools.partial(pair_kernel, count, len(after), height, orbitals),
        grid=(rows // step,),
        in_specs=[pl.BlockSpec((step, depth), lambda s: (s, 0))]
        + [pl.BlockSpec((width, depth), lambda s: (0, 0))] * count
        + [pl.BlockSpec(memory_space=pl.ANY)] * len(after),
        out_specs=[pl.BlockSpec((step, width), lambda s: (s, 0))] * (2 * count),
        out_shape=[jax.ShapeDtypeStruct((rows, width), F32)] * (2 * count),
        scratch_shapes=[pltpu.VMEM((count * width, depth), BF16)] * 2,
        compiler_params=pltpu.CompilerParams(vmem_limit_bytes=60 * MIB),
        cost_estimate=CHEAP,
        name="pair_blocks",
    )(left, *shards, *after)
    return out[:count], out[count:]


def density_kernel(count, waits, first, row_ref, *refs):
    direct_refs = refs[:count]
    swapped_refs = refs[count : 2 * count]
    shard_refs = refs[2 * count : 3 * count]
    energy_refs = refs[3 * count : 4 * count]
    refs = refs[4 * count + waits :]
    if not first:
        before_ref, *refs = refs
    out_ref, high_ref, low_ref, amp_high_ref, amp_low_ref = refs
    width = direct_refs[0].shape[1]

    @pl.when(pl.program_id(0) == 0)
    def _():
        for spot in range(count):
            rows = pl.ds(spot * width, width)
            high_ref[rows, :], low_ref[rows, :] = halves(shard_refs[spot][...])

    for spot in range(count):
        columns = slice(spot * width, (spot + 1) * width)
        denominator = row_ref[...] + energy_refs[spot][0:1, :]
        amplitude = (swapped_refs[spot][...] - 2.0 * direct_refs[spot][...]) / denominator
        amp_high_ref[:, columns], amp_low_ref[:, columns] = halves(amplitude)
    total = product(
        (amp_high_ref[...], amp_low_ref[...]), (high_ref[...], low_ref[...]), ((1,), (0,))
    )
    out_ref[...] = total if first else before_ref[...] + total


def density_add(before, row_energy, direct, swapped, shards, after):
    count = len(shards)
    rows, width = direct[0].shape
    depth = shards[0].shape[1]
    if width % 128 or rows % 8:
        for spot in range(count):
            denominator = row_energy + shards[spot][width : width + 1, :width]
            amplitude = (swapped[spot] - 2.0 * direct[spot]) / denominator
            term = jnp.dot(amplitude, shards[spot][:width], precision=lax.Precision.HIGHEST)
            before = term if before is None else before + term
        return before
    step = min(rows, 256)
    while rows % step:
        step -= 8
    first = before is None
    by_rows = lambda columns: pl.BlockSpec((step, columns), lambda s: (s, 0))
    whole = lambda height, columns: pl.BlockSpec((height, columns), lambda s: (0, 0))
    return pl.pallas_call(
        functools.partial(density_kernel, count, len(after), first),
        grid=(rows // step,),
        in_specs=[by_rows(1)]
        + [by_rows(width)] * (2 * count)
        + [whole(width, depth)] * count
        + [pl.BlockSpec((8, width), lambda s: (width // 8, 0))] * count
        + [pl.BlockSpec(memory_space=pl.ANY)] * len(after)
        + ([] if first else [by_rows(depth)]),
        out_specs=by_rows(depth),
        out_shape=jax.ShapeDtypeStruct((rows, depth), F32),
        scratch_shapes=[pltpu.VMEM((count * width, depth), BF16)] * 2
        + [pltpu.VMEM((step, count * width), BF16)] * 2,
        input_output_aliases={} if first else {1 + 4 * count + len(after): 0},
        compiler_params=pltpu.CompilerParams(vmem_limit_bytes=60 * MIB),
        cost_estimate=CHEAP,
        name="density_add",
    )(row_energy, *direct, *swapped, *shards, *shards, *after, *([] if first else [before]))


def across(x, bits):
    size = lax.axis_size(AXIS)
    return lax.ppermute(x, AXIS, [(i, i ^ bits) for i in range(size)])


def phases(size):
    far, flat = size // 2, 2
    middle = range(4, far, 4)
    chips = {
        "far": [far],
        "middle": list(middle),
        "flat": [flat],
        "far_middle": [far | m for m in middle],
        "far_flat": [far | flat],
        "middle_flat": [m | flat for m in middle],
        "all": [far | m | flat for m in middle],
        "own": [0],
    }
    pick = lambda *names: [k for name in names for k in chips[name]]
    other = lambda *names: [k + 1 for k in pick(*names)]
    low = lambda k: (k & ~3 & ~far) & -(k & ~3 & ~far)
    cut = lambda kind, ks, most: [(kind, ks[n : n + most]) for n in range(0, len(ks), most)]
    shard = lambda ks, bits: [("shard", k, bits(k)) for k in ks]
    twin = lambda *names: [("twin", k) for k in pick(*names)]
    reply = lambda ks: [("reply", k) for k in ks]
    pair = lambda ks: cut("pair", ks, 2)
    density = lambda ks: cut("density", ks, 4)
    return [
        shard(pick("far"), lambda k: far)
        + shard(pick("middle"), low)
        + shard(pick("flat"), lambda k: flat)
        + twin("own"),
        twin("far", "middle", "flat") + pair(pick("far", "middle")),
        reply(pick("far"))
        + shard(pick("far_flat"), lambda k: flat)
        + shard(pick("far_middle"), low)
        + pair(other("far", "middle"))
        + pair(pick("own", "flat")),
        reply(other("far"))
        + shard(pick("all"), low)
        + shard(pick("middle_flat"), lambda k: flat)
        + twin("far_flat", "far_middle")
        + pair(pick("far_flat", "far_middle")),
        reply(pick("far_flat", "far_middle"))
        + twin("all", "middle_flat")
        + reply(pick("middle"))
        + pair(other("far_flat", "far_middle"))
        + pair(other("own", "flat")),
        reply(other("far_flat", "far_middle"))
        + pair(pick("all", "middle_flat"))
        + pair(other("all", "middle_flat"))
        + reply(other("middle") + pick("all", "middle_flat") + other("all", "middle_flat"))
        + reply([1] + pick("flat") + other("flat"))
        + density(pick("far") + other("far") + pick("far_flat", "far_middle"))
        + density(pick("middle") + other("middle", "far_flat", "far_middle"))
        + density([0, 1] + pick("flat", "middle_flat"))
        + density(pick("all") + other("all", "middle_flat", "flat")),
    ]


def exchange(left, own, row_energy, height, orbitals):
    shards, direct, swapped, messages = {0: own}, {}, {}, {}
    density, last = None, []
    before, now = [], []

    def send(x, bits):
        if before:
            x, _ = lax.optimization_barrier((x, before))
        now.append(across(x, bits))
        return now[-1]

    for steps in phases(lax.axis_size(AXIS)):
        for kind, what, *bits in steps:
            if kind == "shard":
                shards[what] = send(shards[what ^ bits[0]], bits[0])
            elif kind == "twin":
                shards[what + 1] = send(shards[what], 1)
            elif kind == "reply":
                swapped[what] = send(messages[what], what)
            elif kind == "pair":
                waits = [x for x in before if all(x is not y for y in last)]
                ours, theirs = pair_blocks(
                    left, [shards[k] for k in what], height, orbitals, last + waits
                )
                last = [ours[0]]
                for k, one, message in zip(what, ours, theirs):
                    direct[k], messages[k] = one, message
                    if k == 0:
                        swapped[0] = message
            else:
                density = density_add(
                    density,
                    row_energy,
                    [direct[k] for k in what],
                    [swapped[k] for k in what],
                    [shards[k] for k in what],
                    [x for x in last if x is not density],
                )
                last = [density]
        before, now = now + last, []
    return density


def gathered(left, j_factors, row_energy, virt_energy, occ_j, height):
    blocks = lax.axis_size(AXIS)
    total = jnp.zeros(left.shape, F32)
    for index in range(j_factors.shape[0]):
        rows = lax.all_gather(j_factors[index], AXIS, axis=0, tiled=True)
        energy = lax.all_gather(virt_energy, AXIS, axis=0, tiled=True) - occ_j[index]
        pair = jnp.dot(left, rows.T, precision=lax.Precision.HIGHEST)
        split = pair.reshape(-1, height, blocks, height).transpose(0, 3, 2, 1)
        turned = lax.all_to_all(
            split.reshape(-1, height, blocks * height), AXIS, split_axis=2, concat_axis=2, tiled=True
        )
        amplitude = (turned.reshape(pair.shape) - 2.0 * pair) / (row_energy + energy[None, :])
        total = total + jnp.dot(amplitude, rows, precision=lax.Precision.HIGHEST)
    return total


def body(i_factors, j_factors, occ_i, occ_j, virt_energy):
    size = lax.axis_size(AXIS)
    orbitals, height, depth = j_factors.shape
    width = orbitals * height
    left = i_factors.reshape(-1, depth)
    row_energy = (virt_energy[None, :] - occ_i[:, None]).reshape(-1, 1)
    if size < 8 or size & (size - 1) or width > depth:
        density = gathered(left, j_factors, row_energy, virt_energy, occ_j, height)
        return density.reshape(i_factors.shape)
    energy = (virt_energy[None, :] - occ_j[:, None]).reshape(1, width)
    energy = jnp.pad(energy, ((0, 7), (0, depth - width)))
    own = jnp.concatenate([j_factors.reshape(width, depth), energy], axis=0)
    return exchange(left, own, row_energy, height, orbitals).reshape(i_factors.shape)


def solution(mesh):
    placed = (
        P("conf", "virt", None),
        P("conf", "virt", None),
        P("conf"),
        P("conf"),
        P(("conf", "virt")),
    )
    return jax.shard_map(
        body, mesh=mesh, in_specs=placed, out_specs=P("conf", "virt", None), check_vma=False
    )
```

time: 356 us -> 319 us (0.90)
  waiting for transfers between devices: 114 us -> 155 us
  blocking collectives: 34.7 us -> 0 us
  starting transfers between devices: 57.5 us -> 27.5 us
  local copies, waits for them, and re-layouts: 18.1 us -> 3.24 us
  Pallas kernels: 129 us -> 125 us
    ppermute x30, waiting for transfers between devices: 114 us -> 155 us  [across(): return lax.ppermute(x, AXIS, [(i, i ^ bits) for i in range(size)])]
    all_gather x1 -> x0, blocking collectives: 34.7 us -> none  [body(): energies = lax.all_gather(padded, AXIS, axis=0)[:, 0, :height]]
    ppermute x30, starting transfers between devices: 57.5 us -> 27.5 us  [across(): return lax.ppermute(x, AXIS, [(i, i ^ bits) for i in range(size)])]
    unnamed x30 -> x40, local copies, waits for them, and re-layouts: 16.4 us -> 1.87 us
    pallas_call x16 -> x12, Pallas kernels: 129 us -> 125 us  [the longest x8 70.6 us: pair_blocks(): pl.pallas_call(functools.partial(pair_kernel, count, len(after), height,...]
  transfers between devices with their start and end apart: 30 -> 30, of which waited for: 13 -> 10; matrix products, arithmetic and copies ran while one was open for 1% -> 0% of each run, Pallas kernels for 34% -> 36%
where the time goes in v2:
time: 319 us; the launch traced here: 313 us
  waiting for transfers between devices  155 us (49%)
  Pallas kernels  125 us (39%)
  starting transfers between devices  27.5 us (9%)
  local copies, waits for them, and re-layouts  3.24 us (1%)
    ppermute x30, waiting for transfers between devices, across(): return lax.ppermute(x, AXIS, [(i, i ^ bits) for i in range(size)])  155 us
    pallas_call x8, Pallas kernels, pair_blocks(): pl.pallas_call(functools.partial(pair_kernel, count, len(after), height,...  70.6 us
    pallas_call x4, Pallas kernels, density_add(): pl.pallas_call(functools.partial(density_kernel, count, len(after), first...  54.8 us
    ppermute x30, starting transfers between devices, across(): return lax.ppermute(x, AXIS, [(i, i ^ bits) for i in range(size)])  27.5 us
  transfers between devices with their start and end apart: 30, of which 10 were waited for; matrix products, arithmetic and copies ran while one was open for 0% of the time, Pallas kernels for 36%

profile of v2, /device:TPU:16, one launch (start us, length us, event | category | flops | bytes accessed | tf_op | source)
XLA Modules:
  0.0 313.3 jit_solution(655364615819165580)
XLA Ops:
  0.0 0.7 broadcast_subtract_fusion.1
  0.8 1.3 select_maximum_fusion.refs_0_.refs_8_.refs_12_
  2.3 1.6 collective-permute-start.2
  3.8 1.6 collective-permute-start.1
  5.4 0.3 collective-permute-start
  5.8 23.6 %collective-permute-done.2.refs_4_.refs_1_.refs_10_.refs_14_ = f32[136,2048]{1,0:T(8,128)} collective-permute-done((f32[136,2048]{1,0:T(8,128)S(1)}, f32[136,2048]{1,0:T(8,128)}, u32[]{:S(2)}, u32[]{:S(2)}) %collective-permute-start.2) | collective-permute-done | bytes 1114144 | tf_op jit(solution)/shard_map/ppermute | solution.py:151
  29.3 22.9 %collective-permute-done.1.refs_1_.refs_3_.refs_8_.refs_12_ = f32[136,2048]{1,0:T(8,128)} collective-permute-done((f32[136,2048]{1,0:T(8,128)S(1)}, f32[136,2048]{1,0:T(8,128)}, u32[]{:S(2)}, u32[]{:S(2)}) %collective-permute-start.1) | collective-permute-done | bytes 1114144 | tf_op jit(solution)/shard_map/ppermute | solution.py:151
  52.2 2.2 collective-permute-done.refs_0_.refs_2_.refs_8_.refs_12_
  54.4 0.5 collective-permute-start.5
  55.0 8.8 %pair_blocks.8 = (f32[1024,128]{1,0:T(8,128)}, f32[1024,128]{1,0:T(8,128)}, f32[1024,128]{1,0:T(8,128)}, f32[1024,128]{1,0:T(8,128)}) custom-call(f32[1024,2048]{1,0:T(8,128)} %bitcast.3, f32[136,2048]{1,0:T(8,128)} %collective-permute-done.refs_0_.refs_2_.refs_8_.refs_12_, f32[136,2048]{1,0:T(8,128)} %collective-permute-done.1.refs_1_.refs_3_.refs_8_.refs_12_, ...), custom_call_target="tpu_custom_call" | custom-call | flops 1 | bytes 1 | tf_op jit(solution)/shard_map/pair_blocks/pallas_call | solution.py:68
  63.8 2.8 collective-permute-start.9
  66.6 0.5 collective-permute-start.7
  67.1 0.3 collective-permute-start.8
  67.5 8.8 %pair_blocks.9 = (f32[1024,128]{1,0:T(8,128)}, f32[1024,128]{1,0:T(8,128)}, f32[1024,128]{1,0:T(8,128)}, f32[1024,128]{1,0:T(8,128)}) custom-call(f32[1024,2048]{1,0:T(8,128)} %bitcast.4, f32[136,2048]{1,0:T(8,128)} %copy-done, f32[136,2048]{1,0:T(8,128)} %copy-done.2, f32[1024,128]{1,0:T(8,128)} %get-tuple-element.64.refs_2_.refs_6_.refs_0_, ...), custom_call_target="tpu_custom_call" | custom-call | flops 1 | bytes 1 | tf_op jit(solution)/shard_map/pair_blocks/pallas_call | solution.py:68
  76.3 8.8 %pair_blocks.10 = (f32[1024,128]{1,0:T(8,128)}, f32[1024,128]{1,0:T(8,128)}, f32[1024,128]{1,0:T(8,128)}, f32[1024,128]{1,0:T(8,128)}) custom-call(f32[1024,2048]{1,0:T(8,128)} %bitcast.5, f32[136,2048]{1,0:T(8,128)} %copy-done.8, f32[136,2048]{1,0:T(8,128)} %collective-permute-done.2.refs_4_.refs_1_.refs_10_.refs_14_, ...), custom_call_target="tpu_custom_call" | custom-call | flops 1 | bytes 1 | tf_op jit(solution)/shard_map/pair_blocks/pallas_call | solution.py:68
  85.1 18.2 %collective-permute-done.8.refs_3_.refs_4_ = f32[1024,128]{1,0:T(8,128)S(1)} collective-permute-done((f32[1024,128]{1,0:T(8,128)}, f32[1024,128]{1,0:T(8,128)S(1)}, u32[]{:S(2)}, u32[]{:S(2)}) %collective-permute-start.8) | collective-permute-done | bytes 524320 | tf_op jit(solution)/shard_map/ppermute | solution.py:151
  103.4 1.7 collective-permute-start.10
  105.1 0.5 collective-permute-start.11
  105.6 1.3 collective-permute-start.14
  106.9 8.8 %pair_blocks.11 = (f32[1024,128]{1,0:T(8,128)}, f32[1024,128]{1,0:T(8,128)}, f32[1024,128]{1,0:T(8,128)}, f32[1024,128]{1,0:T(8,128)}) custom-call(f32[1024,2048]{1,0:T(8,128)} %bitcast.6, f32[136,2048]{1,0:T(8,128)} %collective-permute-done.7.refs_0_.refs_4_.refs_10_.refs_14_, f32[136,2048]{1,0:T(8,128)} %collective-permute-done.9.refs_1_.refs_5_.refs_11_.refs_15_, ...), custom_call_target="tpu_custom_call" | custom-call | flops 1 | bytes 1 | tf_op jit(solution)/shard_map/pair_blocks/pallas_call | solution.py:68
  115.7 26.5 %collective-permute-done.14.refs_3_.refs_5_ = f32[1024,128]{1,0:T(8,128)S(1)} collective-permute-done((f32[1024,128]{1,0:T(8,128)}, f32[1024,128]{1,0:T(8,128)S(1)}, u32[]{:S(2)}, u32[]{:S(2)}) %collective-permute-start.14) | collective-permute-done | bytes 524320 | tf_op jit(solution)/shard_map/ppermute | solution.py:151
  142.2 1.0 copy-done.6
  143.3 0.3 collective-permute-start.17
  143.8 0.3 collective-permute-start.19
  144.1 0.5 collective-permute-start.16
  144.6 3.5 %collective-permute-start.15 = (f32[1024,128]{1,0:T(8,128)}, f32[1024,128]{1,0:T(8,128)}, u32[]{:S(2)}, u32[]{:S(2)}) collective-permute-start(f32[1024,128]{1,0:T(8,128)} %get-tuple-element.79), channel_id=1, source_target_pairs={{0,10},{1,11},{2,8},{3,9},{4,14},{5,15},{6,12},{7,13},{8,2},{9,3},... | collective-permute-start | bytes 1572872 | tf_op jit(solution)/shard_map/ppermute | solution.py:151
  148.1 8.8 %pair_blocks.12 = (f32[1024,128]{1,0:T(8,128)}, f32[1024,128]{1,0:T(8,128)}, f32[1024,128]{1,0:T(8,128)}, f32[1024,128]{1,0:T(8,128)}) custom-call(f32[1024,2048]{1,0:T(8,128)} %bitcast.7, f32[136,2048]{1,0:T(8,128)} %copy-done.6, f32[136,2048]{1,0:T(8,128)} %collective-permute-done.13.refs_1_.refs_7_.refs_11_.refs_15_, ...), custom_call_target="tpu_custom_call" | custom-call | flops 1 | bytes 1 | tf_op jit(solution)/shard_map/pair_blocks/pallas_call | solution.py:68
  156.9 8.8 %pair_blocks.13 = (f32[1024,128]{1,0:T(8,128)}, f32[1024,128]{1,0:T(8,128)}, f32[1024,128]{1,0:T(8,128)}, f32[1024,128]{1,0:T(8,128)}) custom-call(f32[1024,2048]{1,0:T(8,128)} %bitcast.8, f32[136,2048]{1,0:T(8,128)} %copy-done.7, f32[136,2048]{1,0:T(8,128)} %copy-done.1, f32[1024,128]{1,0:T(8,128)} %get-tuple-element.76.refs_2_, f32[1024,128]{1,0:T(8,128)} %copy-done.9, ...), custom_call_target="tpu_custom_call" | custom-call | flops 1 | bytes 1 | tf_op jit(solution)/shard_map/pair_blocks/pallas_call | solution.py:68
  165.7 16.0 %collective-permute-done.16.refs_4_.refs_7_ = f32[1024,128]{1,0:T(8,128)} collective-permute-done((f32[1024,128]{1,0:T(8,128)}, f32[1024,128]{1,0:T(8,128)}, u32[]{:S(2)}, u32[]{:S(2)}) %collective-permute-start.16) | collective-permute-done | bytes 524320 | tf_op jit(solution)/shard_map/ppermute | solution.py:151
  181.7 8.3 %collective-permute-done.15.refs_3_.refs_6_ = f32[1024,128]{1,0:T(8,128)} collective-permute-done((f32[1024,128]{1,0:T(8,128)}, f32[1024,128]{1,0:T(8,128)}, u32[]{:S(2)}, u32[]{:S(2)}) %collective-permute-start.15) | collective-permute-done | bytes 524320 | tf_op jit(solution)/shard_map/ppermute | solution.py:151
  190.0 0.6 collective-permute-start.25
  190.6 2.7 collective-permute-start.27
  193.3 0.9 collective-permute-start.28
  194.2 1.9 collective-permute-start.29
  196.0 8.8 %pair_blocks.14 = (f32[1024,128]{1,0:T(8,128)}, f32[1024,128]{1,0:T(8,128)}, f32[1024,128]{1,0:T(8,128)}, f32[1024,128]{1,0:T(8,128)}) custom-call(f32[1024,2048]{1,0:T(8,128)} %bitcast.9, f32[136,2048]{1,0:T(8,128)} %copy-done.3, f32[136,2048]{1,0:T(8,128)} %copy-done.4, f32[1024,128]{1,0:T(8,128)} %get-tuple-element.77.refs_2_.refs_8_.refs_1_, ...), custom_call_target="tpu_custom_call" | custom-call | flops 1 | bytes 1 | tf_op jit(solution)/shard_map/pair_blocks/pallas_call | solution.py:68
  204.9 9.0 %pair_blocks.15 = (f32[1024,128]{1,0:T(8,128)}, f32[1024,128]{1,0:T(8,128)}, f32[1024,128]{1,0:T(8,128)}, f32[1024,128]{1,0:T(8,128)}) custom-call(f32[1024,2048]{1,0:T(8,128)} %bitcast.10, f32[136,2048]{1,0:T(8,128)} %copy-done.5, f32[136,2048]{1,0:T(8,128)} %collective-permute-done.18.refs_6_.refs_1_.refs_10_.refs_14_, ...), custom_call_target="tpu_custom_call" | custom-call | flops 1 | bytes 1 | tf_op jit(solution)/shard_map/pair_blocks/pallas_call | solution.py:68
  213.9 1.7 collective-permute-start.23
  215.6 2.5 collective-permute-start.26
  218.1 10.2 %collective-permute-done.28.refs_6_ = f32[1024,128]{1,0:T(8,128)} collective-permute-done((f32[1024,128]{1,0:T(8,128)}, f32[1024,128]{1,0:T(8,128)}, u32[]{:S(2)}, u32[]{:S(2)}) %collective-permute-start.28) | collective-permute-done | bytes 524320 | tf_op jit(solution)/shard_map/ppermute | solution.py:151
  228.3 0.9 collective-permute-start.20
  229.1 24.7 %collective-permute-done.29.refs_7_ = f32[1024,128]{1,0:T(8,128)} collective-permute-done((f32[1024,128]{1,0:T(8,128)}, f32[1024,128]{1,0:T(8,128)}, u32[]{:S(2)}, u32[]{:S(2)}) %collective-permute-start.29) | collective-permute-done | bytes 524320 | tf_op jit(solution)/shard_map/ppermute | solution.py:151
  254.2 1.3 sub.54.row_ref
  255.5 12.6 %density_add.4.refs_16_ = f32[1024,2048]{1,0:T(8,128)} custom-call(f32[1024,1]{1,0:T(8,128)} %sub.54.row_ref, f32[1024,128]{1,0:T(8,128)} %get-tuple-element.64.refs_2_.refs_6_.refs_0_, f32[1024,128]{1,0:T(8,128)} %get-tuple-element.68.refs_2_.refs_1_, f32[1024,128]{1,0:T(8,128)} %get-tuple-element.73.refs_2_.refs_8_, ...), custom_call_target="tpu_custom_call" | custom-call | flops 1 | bytes 1 | tf_op jit(solution)/shard_map/density_add/pallas_call | solution.py:129
  268.1 14.1 %density_add.5.refs_16_ = f32[1024,2048]{1,0:T(8,128)} custom-call(f32[1024,1]{1,0:T(8,128)} %sub.54.row_ref, f32[1024,128]{1,0:T(8,128)} %get-tuple-element.107.refs_0_, f32[1024,128]{1,0:T(8,128)} %get-tuple-element.108.refs_1_, f32[1024,128]{1,0:T(8,128)} %get-tuple-element.76.refs_2_, ...), custom_call_target="tpu_custom_call", output_to_operand_aliasing={{}: (17, {})} | custom-call | flops 1 | bytes 1 | tf_op jit(solution)/shard_map/density_add/pallas_call | solution.py:129
  282.2 14.1 %density_add.6.refs_16_ = f32[1024,2048]{1,0:T(8,128)} custom-call(f32[1024,1]{1,0:T(8,128)} %sub.54.row_ref, f32[1024,128]{1,0:T(8,128)} %get-tuple-element.69.refs_2_.refs_0_, f32[1024,128]{1,0:T(8,128)} %get-tuple-element.77.refs_2_.refs_8_.refs_1_, f32[1024,128]{1,0:T(8,128)} %get-tuple-element.98.refs_2_, ...), custom_call_target="tpu_custom_call", output_to_operand_aliasing={{}: (17, {})} | custom-call | flops 1 | bytes 1 | tf_op jit(solution)/shard_map/density_add/pallas_call | solution.py:129
  296.3 2.0 collective-permute-done.21.refs_5_
  298.4 0.8 copy-done.17
  299.1 14.0 %density_add.7 = f32[1024,2048]{1,0:T(8,128)} custom-call(f32[1024,1]{1,0:T(8,128)} %sub.54.row_ref, f32[1024,128]{1,0:T(8,128)} %get-tuple-element.86.refs_2_.refs_0_, f32[1024,128]{1,0:T(8,128)} %get-tuple-element.87.refs_16_.refs_1_, f32[1024,128]{1,0:T(8,128)} %get-tuple-element.88.refs_2_, ...), custom_call_target="tpu_custom_call", output_to_operand_aliasing={{}: (17, {})} | custom-call | flops 1 | bytes 1 | tf_op jit(solution)/shard_map/density_add/pallas_call | solution.py:129
  (69 shorter events, 1.0 us)
Async XLA Ops:
  2.2 52.8 %copy-start.8 = (f32[136,2048]{1,0:T(8,128)}, f32[136,2048]{1,0:T(8,128)S(1)}, u32[]{:S(2)}) copy-start(f32[136,2048]{1,0:T(8,128)S(1)} %select_maximum_fusion.refs_0_.refs_8_.refs_12_) | copy-start | bytes 3342340
  2.2 3.6 %collective-permute-start.3 = (f32[136,2048]{1,0:T(8,128)S(1)}, f32[136,2048]{1,0:T(8,128)S(1)}, u32[]{:S(2)}, u32[]{:S(2)}) collective-permute-start(f32[136,2048]{1,0:T(8,128)S(1)} %select_maximum_fusion.refs_0_.refs_8_.refs_12_), channel_id=1, source_target_pairs={{0,1},{1,0},{2,3},{3,2},{4,5},{5,4},{6,7},{7,6},{8,9},{9,8},{10,11... | collective-permute-start | bytes 3342344 | tf_op jit(solution)/shard_map/ppermute | solution.py:151
  2.3 27.1 %collective-permute-start.2 = (f32[136,2048]{1,0:T(8,128)S(1)}, f32[136,2048]{1,0:T(8,128)}, u32[]{:S(2)}, u32[]{:S(2)}) collective-permute-start(f32[136,2048]{1,0:T(8,128)S(1)} %select_maximum_fusion.refs_0_.refs_8_.refs_12_), channel_id=1, source_target_pairs={{0,2},{1,3},{2,0},{3,1},{4,6},{5,7},{6,4},{7,5},{8,10},{9,11},{10,... | collective-permute-start | bytes 3342344 | tf_op jit(solution)/shard_map/ppermute | solution.py:151
  3.8 48.4 %collective-permute-start.1 = (f32[136,2048]{1,0:T(8,128)S(1)}, f32[136,2048]{1,0:T(8,128)}, u32[]{:S(2)}, u32[]{:S(2)}) collective-permute-start(f32[136,2048]{1,0:T(8,128)S(1)} %select_maximum_fusion.refs_0_.refs_8_.refs_12_), channel_id=1, source_target_pairs={{0,4},{1,5},{2,6},{3,7},{4,0},{5,1},{6,2},{7,3},{8,12},{9,13},{10,... | collective-permute-start | bytes 3342344 | tf_op jit(solution)/shard_map/ppermute | solution.py:151
  5.4 49.0 %collective-permute-start = (f32[136,2048]{1,0:T(8,128)S(1)}, f32[136,2048]{1,0:T(8,128)}, u32[]{:S(2)}, u32[]{:S(2)}) collective-permute-start(f32[136,2048]{1,0:T(8,128)S(1)} %select_maximum_fusion.refs_0_.refs_8_.refs_12_), channel_id=1, source_target_pairs={{0,8},{1,9},{2,10},{3,11},{4,12},{5,13},{6,14},{7,15},{8,0},{9,1},... | collective-permute-start | bytes 3342344 | tf_op jit(solution)/shard_map/ppermute | solution.py:151
  5.8 48.7 %copy-start.7 = (f32[136,2048]{1,0:T(8,128)}, f32[136,2048]{1,0:T(8,128)S(1)}, u32[]{:S(2)}) copy-start(f32[136,2048]{1,0:T(8,128)S(1)} %collective-permute-done.3.refs_5_.refs_0_.refs_9_.refs_13_) | copy-start | bytes 3342340
  54.4 9.4 %collective-permute-start.4 = (f32[136,2048]{1,0:T(8,128)}, f32[136,2048]{1,0:T(8,128)S(1)}, u32[]{:S(2)}, u32[]{:S(2)}) collective-permute-start(f32[136,2048]{1,0:T(8,128)} %collective-permute-done.refs_0_.refs_2_.refs_8_.refs_12_), channel_id=1, source_target_pairs={{0,1},{1,0},{2,3},{3,2},{4,5},{5,4},{6,7},{7,6},{8,9},{9,8},{10,11... | collective-permute-start | bytes 3342344 | tf_op jit(solution)/shard_map/ppermute | solution.py:151
  54.4 9.4 %collective-permute-start.5 = (f32[136,2048]{1,0:T(8,128)}, f32[136,2048]{1,0:T(8,128)S(1)}, u32[]{:S(2)}, u32[]{:S(2)}) collective-permute-start(f32[136,2048]{1,0:T(8,128)} %collective-permute-done.1.refs_1_.refs_3_.refs_8_.refs_12_), channel_id=1, source_target_pairs={{0,1},{1,0},{2,3},{3,2},{4,5},{5,4},{6,7},{7,6},{8,9},{9,8},{10,11... | collective-permute-start | bytes 3342344 | tf_op jit(solution)/shard_map/ppermute | solution.py:151
  55.0 8.9 %collective-permute-start.6 = (f32[136,2048]{1,0:T(8,128)}, f32[136,2048]{1,0:T(8,128)S(1)}, u32[]{:S(2)}, u32[]{:S(2)}) collective-permute-start(f32[136,2048]{1,0:T(8,128)} %collective-permute-done.2.refs_4_.refs_1_.refs_10_.refs_14_), channel_id=1, source_target_pairs={{0,1},{1,0},{2,3},{3,2},{4,5},{5,4},{6,7},{7,6},{8,9},{9,8},{10,11... | collective-permute-start | bytes 3342344 | tf_op jit(solution)/shard_map/ppermute | solution.py:151
  63.8 3.7 %copy-start = (f32[136,2048]{1,0:T(8,128)}, f32[136,2048]{1,0:T(8,128)S(1)}, u32[]{:S(2)}) copy-start(f32[136,2048]{1,0:T(8,128)S(1)} %collective-permute-done.4.refs_0_.refs_3_.refs_9_.refs_13_) | copy-start | bytes 3342340
  63.8 3.7 %copy-start.2 = (f32[136,2048]{1,0:T(8,128)}, f32[136,2048]{1,0:T(8,128)S(1)}, u32[]{:S(2)}) copy-start(f32[136,2048]{1,0:T(8,128)S(1)} %collective-permute-done.5.refs_1_.refs_4_.refs_9_.refs_13_) | copy-start | bytes 3342340
  63.8 3.6 %copy-start.1 = (f32[136,2048]{1,0:T(8,128)}, f32[136,2048]{1,0:T(8,128)S(1)}, u32[]{:S(2)}) copy-start(f32[136,2048]{1,0:T(8,128)S(1)} %collective-permute-done.6.refs_5_.refs_1_.refs_11_.refs_15_) | copy-start | bytes 3342340
  63.8 39.5 %collective-permute-start.9 = (f32[136,2048]{1,0:T(8,128)}, f32[136,2048]{1,0:T(8,128)}, u32[]{:S(2)}, u32[]{:S(2)}) collective-permute-start(f32[136,2048]{1,0:T(8,128)} %collective-permute-done.refs_0_.refs_2_.refs_8_.refs_12_), channel_id=1, source_target_pairs={{0,4},{1,5},{2,6},{3,7},{4,0},{5,1},{6,2},{7,3},{8,12},{9,13},{10,... | collective-permute-start | bytes 3342344 | tf_op jit(solution)/shard_map/ppermute | solution.py:151
  66.6 36.7 %collective-permute-start.7 = (f32[136,2048]{1,0:T(8,128)}, f32[136,2048]{1,0:T(8,128)}, u32[]{:S(2)}, u32[]{:S(2)}) collective-permute-start(f32[136,2048]{1,0:T(8,128)} %collective-permute-done.refs_0_.refs_2_.refs_8_.refs_12_), channel_id=1, source_target_pairs={{0,2},{1,3},{2,0},{3,1},{4,6},{5,7},{6,4},{7,5},{8,10},{9,11},{10,... | collective-permute-start | bytes 3342344 | tf_op jit(solution)/shard_map/ppermute | solution.py:151
  67.1 36.2 %collective-permute-start.8 = (f32[1024,128]{1,0:T(8,128)}, f32[1024,128]{1,0:T(8,128)S(1)}, u32[]{:S(2)}, u32[]{:S(2)}) collective-permute-start(f32[1024,128]{1,0:T(8,128)} %get-tuple-element.67), channel_id=1, source_target_pairs={{0,8},{1,9},{2,10},{3,11},{4,12},{5,13},{6,14},{7,15},{8,0},{9,1},... | collective-permute-start | bytes 1572872 | tf_op jit(solution)/shard_map/ppermute | solution.py:151
  103.3 2.3 copy-start.10
  103.3 38.9 %collective-permute-start.12 = (f32[136,2048]{1,0:T(8,128)}, f32[136,2048]{1,0:T(8,128)S(1)}, u32[]{:S(2)}, u32[]{:S(2)}) collective-permute-start(f32[136,2048]{1,0:T(8,128)} %collective-permute-done.7.refs_0_.refs_4_.refs_10_.refs_14_), channel_id=1, source_target_pairs={{0,1},{1,0},{2,3},{3,2},{4,5},{5,4},{6,7},{7,6},{8,9},{9,8},{10,11... | collective-permute-start | bytes 3342344 | tf_op jit(solution)/shard_map/ppermute | solution.py:151
  103.4 38.8 %collective-permute-start.10 = (f32[136,2048]{1,0:T(8,128)}, f32[136,2048]{1,0:T(8,128)S(1)}, u32[]{:S(2)}, u32[]{:S(2)}) collective-permute-start(f32[136,2048]{1,0:T(8,128)} %collective-permute-done.7.refs_0_.refs_4_.refs_10_.refs_14_), channel_id=1, source_target_pairs={{0,4},{1,5},{2,6},{3,7},{4,0},{5,1},{6,2},{7,3},{8,12},{9,13},{10,... | collective-permute-start | bytes 3342344 | tf_op jit(solution)/shard_map/ppermute | solution.py:151
  105.1 37.1 %collective-permute-start.11 = (f32[136,2048]{1,0:T(8,128)}, f32[136,2048]{1,0:T(8,128)S(1)}, u32[]{:S(2)}, u32[]{:S(2)}) collective-permute-start(f32[136,2048]{1,0:T(8,128)} %collective-permute-done.1.refs_1_.refs_3_.refs_8_.refs_12_), channel_id=1, source_target_pairs={{0,2},{1,3},{2,0},{3,1},{4,6},{5,7},{6,4},{7,5},{8,10},{9,11},{10,... | collective-permute-start | bytes 3342344 | tf_op jit(solution)/shard_map/ppermute | solution.py:151
  105.6 36.6 %collective-permute-start.13 = (f32[136,2048]{1,0:T(8,128)}, f32[136,2048]{1,0:T(8,128)}, u32[]{:S(2)}, u32[]{:S(2)}) collective-permute-start(f32[136,2048]{1,0:T(8,128)} %collective-permute-done.9.refs_1_.refs_5_.refs_11_.refs_15_), channel_id=1, source_target_pairs={{0,1},{1,0},{2,3},{3,2},{4,5},{5,4},{6,7},{7,6},{8,9},{9,8},{10,11... | collective-permute-start | bytes 3342344 | tf_op jit(solution)/shard_map/ppermute | solution.py:151
  105.6 36.6 %collective-permute-start.14 = (f32[1024,128]{1,0:T(8,128)}, f32[1024,128]{1,0:T(8,128)S(1)}, u32[]{:S(2)}, u32[]{:S(2)}) collective-permute-start(f32[1024,128]{1,0:T(8,128)} %get-tuple-element.75), channel_id=1, source_target_pairs={{0,9},{1,8},{2,11},{3,10},{4,13},{5,12},{6,15},{7,14},{8,1},{9,0},... | collective-permute-start | bytes 1572872 | tf_op jit(solution)/shard_map/ppermute | solution.py:151
  142.2 5.9 %copy-start.9 = (f32[1024,128]{1,0:T(8,128)}, f32[1024,128]{1,0:T(8,128)S(1)}, u32[]{:S(2)}) copy-start(f32[1024,128]{1,0:T(8,128)S(1)} %collective-permute-done.14.refs_3_.refs_5_) | copy-start | bytes 1572868
  142.2 5.9 %copy-start.3 = (f32[136,2048]{1,0:T(8,128)}, f32[136,2048]{1,0:T(8,128)S(1)}, u32[]{:S(2)}) copy-start(f32[136,2048]{1,0:T(8,128)S(1)} %collective-permute-done.10.refs_4_.refs_0_.refs_8_.refs_12_) | copy-start | bytes 3342340
  142.2 5.9 %copy-start.4 = (f32[136,2048]{1,0:T(8,128)}, f32[136,2048]{1,0:T(8,128)S(1)}, u32[]{:S(2)}) copy-start(f32[136,2048]{1,0:T(8,128)S(1)} %collective-permute-done.11.refs_5_.refs_1_.refs_11_.refs_15_) | copy-start | bytes 3342340
  143.3 46.8 %collective-permute-start.17 = (f32[136,2048]{1,0:T(8,128)S(1)}, f32[136,2048]{1,0:T(8,128)S(1)}, u32[]{:S(2)}, u32[]{:S(2)}) collective-permute-start(f32[136,2048]{1,0:T(8,128)S(1)} %collective-permute-done.10.refs_4_.refs_0_.refs_8_.refs_12_), channel_id=1, source_target_pairs={{0,1},{1,0},{2,3},{3,2},{4,5},{5,4},{6,7},{7,6},{8,9},{9,8},{10,11... | collective-permute-start | bytes 3342344 | tf_op jit(solution)/shard_map/ppermute | solution.py:151
  143.5 46.5 %collective-permute-start.18 = (f32[136,2048]{1,0:T(8,128)S(1)}, f32[136,2048]{1,0:T(8,128)}, u32[]{:S(2)}, u32[]{:S(2)}) collective-permute-start(f32[136,2048]{1,0:T(8,128)S(1)} %collective-permute-done.11.refs_5_.refs_1_.refs_11_.refs_15_), channel_id=1, source_target_pairs={{0,1},{1,0},{2,3},{3,2},{4,5},{5,4},{6,7},{7,6},{8,9},{9,8},{10,11... | collective-permute-start | bytes 3342344 | tf_op jit(solution)/shard_map/ppermute | solution.py:151
  143.8 22.0 %collective-permute-start.19 = (f32[1024,128]{1,0:T(8,128)}, f32[1024,128]{1,0:T(8,128)}, u32[]{:S(2)}, u32[]{:S(2)}) collective-permute-start(f32[1024,128]{1,0:T(8,128)} %get-tuple-element.85), channel_id=1, source_target_pairs={{0,4},{1,5},{2,6},{3,7},{4,0},{5,1},{6,2},{7,3},{8,12},{9,13},{10,... | collective-permute-start | bytes 1572872 | tf_op jit(solution)/shard_map/ppermute | solution.py:151
  144.1 37.6 %collective-permute-start.16 = (f32[1024,128]{1,0:T(8,128)}, f32[1024,128]{1,0:T(8,128)}, u32[]{:S(2)}, u32[]{:S(2)}) collective-permute-start(f32[1024,128]{1,0:T(8,128)} %get-tuple-element.81), channel_id=1, source_target_pairs={{0,12},{1,13},{2,14},{3,15},{4,8},{5,9},{6,10},{7,11},{8,4},{9,5},... | collective-permute-start | bytes 1572872 | tf_op jit(solution)/shard_map/ppermute | solution.py:151
  144.6 45.5 %collective-permute-start.15 = (f32[1024,128]{1,0:T(8,128)}, f32[1024,128]{1,0:T(8,128)}, u32[]{:S(2)}, u32[]{:S(2)}) collective-permute-start(f32[1024,128]{1,0:T(8,128)} %get-tuple-element.79), channel_id=1, source_target_pairs={{0,10},{1,11},{2,8},{3,9},{4,14},{5,15},{6,12},{7,13},{8,2},{9,3},... | collective-permute-start | bytes 1572872 | tf_op jit(solution)/shard_map/ppermute | solution.py:151
  190.0 6.0 %copy-start.5 = (f32[136,2048]{1,0:T(8,128)}, f32[136,2048]{1,0:T(8,128)S(1)}, u32[]{:S(2)}) copy-start(f32[136,2048]{1,0:T(8,128)S(1)} %collective-permute-done.17.refs_5_.refs_0_.refs_9_.refs_13_) | copy-start | bytes 3342340
  190.0 23.8 %collective-permute-start.25 = (f32[1024,128]{1,0:T(8,128)}, f32[1024,128]{1,0:T(8,128)S(1)}, u32[]{:S(2)}, u32[]{:S(2)}) collective-permute-start(f32[1024,128]{1,0:T(8,128)} %get-tuple-element.104), channel_id=1, source_target_pairs={{0,2},{1,3},{2,0},{3,1},{4,6},{5,7},{6,4},{7,5},{8,10},{9,11},{10,... | collective-permute-start | bytes 1572872 | tf_op jit(solution)/shard_map/ppermute | solution.py:151
  190.6 25.0 %collective-permute-start.27 = (f32[1024,128]{1,0:T(8,128)}, f32[1024,128]{1,0:T(8,128)S(1)}, u32[]{:S(2)}, u32[]{:S(2)}) collective-permute-start(f32[1024,128]{1,0:T(8,128)} %get-tuple-element.111), channel_id=1, source_target_pairs={{0,5},{1,4},{2,7},{3,6},{4,1},{5,0},{6,3},{7,2},{8,13},{9,12},{10,... | collective-permute-start | bytes 1572872 | tf_op jit(solution)/shard_map/ppermute | solution.py:151
  193.3 35.0 %collective-permute-start.28 = (f32[1024,128]{1,0:T(8,128)}, f32[1024,128]{1,0:T(8,128)}, u32[]{:S(2)}, u32[]{:S(2)}) collective-permute-start(f32[1024,128]{1,0:T(8,128)} %get-tuple-element.113), channel_id=1, source_target_pairs={{0,11},{1,10},{2,9},{3,8},{4,15},{5,14},{6,13},{7,12},{8,3},{9,2},... | collective-permute-start | bytes 1572872 | tf_op jit(solution)/shard_map/ppermute | solution.py:151
  194.2 59.7 %collective-permute-start.29 = (f32[1024,128]{1,0:T(8,128)}, f32[1024,128]{1,0:T(8,128)}, u32[]{:S(2)}, u32[]{:S(2)}) collective-permute-start(f32[1024,128]{1,0:T(8,128)} %get-tuple-element.115), channel_id=1, source_target_pairs={{0,13},{1,12},{2,15},{3,14},{4,9},{5,8},{6,11},{7,10},{8,5},{9,4},... | collective-permute-start | bytes 1572872 | tf_op jit(solution)/shard_map/ppermute | solution.py:151
  196.0 57.8 %collective-permute-start.24 = (f32[1024,128]{1,0:T(8,128)}, f32[1024,128]{1,0:T(8,128)S(1)}, u32[]{:S(2)}, u32[]{:S(2)}) collective-permute-start(f32[1024,128]{1,0:T(8,128)} %get-tuple-element.102), channel_id=1, source_target_pairs={{0,1},{1,0},{2,3},{3,2},{4,5},{5,4},{6,7},{7,6},{8,9},{9,8},{10,11... | collective-permute-start | bytes 1572872 | tf_op jit(solution)/shard_map/ppermute | solution.py:151
  204.8 49.3 %copy-start.18 = (f32[64]{0:T(128)S(1)}, f32[64]{0:T(128)}, u32[]{:S(2)}) copy-start(f32[64]{0:T(128)} %param.9) | copy-start | bytes 772
  204.8 49.3 %copy-start.19 = (f32[16]{0:T(128)S(1)}, f32[16]{0:T(128)}, u32[]{:S(2)}) copy-start(f32[16]{0:T(128)} %param.7) | copy-start | bytes 196
  213.9 54.2 %copy-start.11 = (f32[1024,128]{1,0:T(8,128)}, f32[1024,128]{1,0:T(8,128)S(1)}, u32[]{:S(2)}) copy-start(f32[1024,128]{1,0:T(8,128)S(1)} %collective-permute-done.25.refs_6_) | copy-start | bytes 1572868
  213.9 82.4 %collective-permute-start.23 = (f32[1024,128]{1,0:T(8,128)}, f32[1024,128]{1,0:T(8,128)S(1)}, u32[]{:S(2)}, u32[]{:S(2)}) collective-permute-start(f32[1024,128]{1,0:T(8,128)} %get-tuple-element.97), channel_id=1, source_target_pairs={{0,3},{1,2},{2,1},{3,0},{4,7},{5,6},{6,5},{7,4},{8,11},{9,10},{10,... | collective-permute-start | bytes 1572872 | tf_op jit(solution)/shard_map/ppermute | solution.py:151
  215.6 38.3 %copy-start.15 = (f32[1024,128]{1,0:T(8,128)}, f32[1024,128]{1,0:T(8,128)S(1)}, u32[]{:S(2)}) copy-start(f32[1024,128]{1,0:T(8,128)S(1)} %collective-permute-done.27.refs_5_) | copy-start | bytes 1572868
  215.6 66.6 %collective-permute-start.26 = (f32[1024,128]{1,0:T(8,128)}, f32[1024,128]{1,0:T(8,128)}, u32[]{:S(2)}, u32[]{:S(2)}) collective-permute-start(f32[1024,128]{1,0:T(8,128)} %get-tuple-element.106), channel_id=1, source_target_pairs={{0,6},{1,7},{2,4},{3,5},{4,2},{5,3},{6,0},{7,1},{8,14},{9,15},{10,... | collective-permute-start | bytes 1572872 | tf_op jit(solution)/shard_map/ppermute | solution.py:151
  228.3 68.0 %collective-permute-start.20 = (f32[1024,128]{1,0:T(8,128)}, f32[1024,128]{1,0:T(8,128)S(1)}, u32[]{:S(2)}, u32[]{:S(2)}) collective-permute-start(f32[1024,128]{1,0:T(8,128)} %get-tuple-element.91), channel_id=1, source_target_pairs={{0,14},{1,15},{2,12},{3,13},{4,10},{5,11},{6,8},{7,9},{8,6},{9,7},... | collective-permute-start | bytes 1572872 | tf_op jit(solution)/shard_map/ppermute | solution.py:151
  253.8 42.5 %collective-permute-start.22 = (f32[1024,128]{1,0:T(8,128)}, f32[1024,128]{1,0:T(8,128)S(1)}, u32[]{:S(2)}, u32[]{:S(2)}) collective-permute-start(f32[1024,128]{1,0:T(8,128)} %get-tuple-element.95), channel_id=1, source_target_pairs={{0,7},{1,6},{2,5},{3,4},{4,3},{5,2},{6,1},{7,0},{8,15},{9,14},{10,... | collective-permute-start | bytes 1572872 | tf_op jit(solution)/shard_map/ppermute | solution.py:151
  253.9 14.3 %copy-start.13 = (f32[1024,128]{1,0:T(8,128)}, f32[1024,128]{1,0:T(8,128)S(1)}, u32[]{:S(2)}) copy-start(f32[1024,128]{1,0:T(8,128)S(1)} %collective-permute-done.24.refs_5_) | copy-start | bytes 1572868
  253.9 44.5 %collective-permute-start.21 = (f32[1024,128]{1,0:T(8,128)}, f32[1024,128]{1,0:T(8,128)S(1)}, u32[]{:S(2)}, u32[]{:S(2)}) collective-permute-start(f32[1024,128]{1,0:T(8,128)} %get-tuple-element.93), channel_id=1, source_target_pairs={{0,15},{1,14},{2,13},{3,12},{4,11},{5,10},{6,9},{7,8},{8,7},{9,6},... | collective-permute-start | bytes 1572872 | tf_op jit(solution)/shard_map/ppermute | solution.py:151
  296.3 2.1 copy-start.12
  296.3 2.0 copy-start.14
  296.3 2.0 copy-start.16
  (2 other events, 1.9 us)

commit v3 on v2

--- a/solution.py
+++ b/solution.py
@@ -193,16 +193,17 @@
         + twin("all", "middle_flat")
         + reply(pick("middle"))
         + pair(other("far_flat", "far_middle"))
-        + pair(other("own", "flat")),
+        + pair(other("own", "flat"))
+        + density(pick("far") + other("far") + [0]),
         reply(other("far_flat", "far_middle"))
         + pair(pick("all", "middle_flat"))
+        + density(pick("far_flat", "far_middle", "middle"))
         + pair(other("all", "middle_flat"))
         + reply(other("middle") + pick("all", "middle_flat") + other("all", "middle_flat"))
         + reply([1] + pick("flat") + other("flat"))
-        + density(pick("far") + other("far") + pick("far_flat", "far_middle"))
-        + density(pick("middle") + other("middle", "far_flat", "far_middle"))
-        + density([0, 1] + pick("flat", "middle_flat"))
-        + density(pick("all") + other("all", "middle_flat", "flat")),
+        + density(other("far_flat", "far_middle", "middle"))
+        + density(pick("all", "middle_flat", "flat"))
+        + density(other("all", "middle_flat", "own", "flat")),
     ]
 
 

time: 319 us -> 311 us (0.975); the launches traced: 313 us -> 309 us
  waiting for transfers between devices: 155 us -> 133 us
  Pallas kernels: 125 us -> 136 us
  local copies, waits for them, and re-layouts: 3.24 us -> 10.9 us
    ppermute x30, waiting for transfers between devices: 155 us -> 133 us  [across(): return lax.ppermute(x, AXIS, [(i, i ^ bits) for i in range(size)])]
    pallas_call x4 -> x5, Pallas kernels: 54.8 us -> 65.8 us  [density_add(): pl.pallas_call(functools.partial(density_kernel, count, len(after), first...]
    unnamed x40 -> x39, local copies, waits for them, and re-layouts: 1.87 us -> 9.56 us
  transfers between devices with their start and end apart: 30 -> 30, of which waited for: 10 -> 11; matrix products, arithmetic and copies ran while one was open for 0% -> 3% of each run, Pallas kernels for 36% -> 40%
where the time goes in v3:
time: 311 us; the launch traced here: 309 us
  Pallas kernels  136 us (44%)
  waiting for transfers between devices  133 us (43%)
  starting transfers between devices  26.3 us (8%)
  local copies, waits for them, and re-layouts  10.9 us (4%)
    ppermute x30, waiting for transfers between devices, across(): return lax.ppermute(x, AXIS, [(i, i ^ bits) for i in range(size)])  133 us
    pallas_call x8, Pallas kernels, pair_blocks(): pl.pallas_call(functools.partial(pair_kernel, count, len(after), height,...  70.7 us
    pallas_call x5, Pallas kernels, density_add(): pl.pallas_call(functools.partial(density_kernel, count, len(after), first...  65.8 us
    ppermute x30, starting transfers between devices, across(): return lax.ppermute(x, AXIS, [(i, i ^ bits) for i in range(size)])  26.3 us
    unnamed x39, local copies, waits for them, and re-layouts  9.56 us
  transfers between devices with their start and end apart: 30, of which 11 were waited for; matrix products, arithmetic and copies ran while one was open for 3% of the time, Pallas kernels for 40%

profile of v3, /device:TPU:16, one launch (start us, length us, event | category | flops | bytes accessed | tf_op | source)
XLA Modules:
  0.0 309.2 jit_solution(3252463856355027866)
XLA Ops:
  0.0 0.7 broadcast_subtract_fusion.1
  0.8 1.3 select_maximum_fusion.refs_0_.refs_8_.refs_11_
  2.3 1.6 collective-permute-start.2
  3.8 1.6 collective-permute-start.1
  5.8 23.6 %collective-permute-done.2.refs_4_.refs_1_.refs_8_.refs_11_ = f32[136,2048]{1,0:T(8,128)} collective-permute-done((f32[136,2048]{1,0:T(8,128)S(1)}, f32[136,2048]{1,0:T(8,128)}, u32[]{:S(2)}, u32[]{:S(2)}) %collective-permute-start.2) | collective-permute-done | bytes 1114144 | tf_op jit(solution)/shard_map/ppermute | solution.py:151
  29.3 22.9 %collective-permute-done.1.refs_1_.refs_3_.refs_8_.refs_11_ = f32[136,2048]{1,0:T(8,128)} collective-permute-done((f32[136,2048]{1,0:T(8,128)S(1)}, f32[136,2048]{1,0:T(8,128)}, u32[]{:S(2)}, u32[]{:S(2)}) %collective-permute-start.1) | collective-permute-done | bytes 1114144 | tf_op jit(solution)/shard_map/ppermute | solution.py:151
  52.2 2.2 collective-permute-done.refs_0_.refs_2_.refs_6_.refs_9_
  54.4 0.5 collective-permute-start.5
  55.0 8.8 %pair_blocks.8 = (f32[1024,128]{1,0:T(8,128)}, f32[1024,128]{1,0:T(8,128)}, f32[1024,128]{1,0:T(8,128)}, f32[1024,128]{1,0:T(8,128)}) custom-call(f32[1024,2048]{1,0:T(8,128)} %bitcast.3, f32[136,2048]{1,0:T(8,128)} %collective-permute-done.refs_0_.refs_2_.refs_6_.refs_9_, f32[136,2048]{1,0:T(8,128)} %collective-permute-done.1.refs_1_.refs_3_.refs_8_.refs_11_, ...), custom_call_target="tpu_custom_call" | custom-call | flops 1 | bytes 1 | tf_op jit(solution)/shard_map/pair_blocks/pallas_call | solution.py:68
  63.9 2.8 collective-permute-start.9
  66.6 0.5 collective-permute-start.7
  67.5 8.8 %pair_blocks.9 = (f32[1024,128]{1,0:T(8,128)}, f32[1024,128]{1,0:T(8,128)}, f32[1024,128]{1,0:T(8,128)}, f32[1024,128]{1,0:T(8,128)}) custom-call(f32[1024,2048]{1,0:T(8,128)} %bitcast.4, f32[136,2048]{1,0:T(8,128)} %copy-done, f32[136,2048]{1,0:T(8,128)} %copy-done.3, f32[1024,128]{1,0:T(8,128)} %get-tuple-element.64.refs_2_.refs_6_.refs_0_, ...), custom_call_target="tpu_custom_call" | custom-call | flops 1 | bytes 1 | tf_op jit(solution)/shard_map/pair_blocks/pallas_call | solution.py:68
  76.3 8.8 %pair_blocks.10 = (f32[1024,128]{1,0:T(8,128)}, f32[1024,128]{1,0:T(8,128)}, f32[1024,128]{1,0:T(8,128)}, f32[1024,128]{1,0:T(8,128)}) custom-call(f32[1024,2048]{1,0:T(8,128)} %bitcast.5, f32[136,2048]{1,0:T(8,128)} %copy-done.6, f32[136,2048]{1,0:T(8,128)} %collective-permute-done.2.refs_4_.refs_1_.refs_8_.refs_11_, ...), custom_call_target="tpu_custom_call" | custom-call | flops 1 | bytes 1 | tf_op jit(solution)/shard_map/pair_blocks/pallas_call | solution.py:68
  85.1 18.2 %collective-permute-done.8.refs_3_ = f32[1024,128]{1,0:T(8,128)S(1)} collective-permute-done((f32[1024,128]{1,0:T(8,128)}, f32[1024,128]{1,0:T(8,128)S(1)}, u32[]{:S(2)}, u32[]{:S(2)}) %collective-permute-start.8) | collective-permute-done | bytes 524320 | tf_op jit(solution)/shard_map/ppermute | solution.py:151
  103.4 1.7 collective-permute-start.10
  105.1 0.5 collective-permute-start.12
  105.6 1.3 collective-permute-start.11
  107.0 8.8 %pair_blocks.11 = (f32[1024,128]{1,0:T(8,128)}, f32[1024,128]{1,0:T(8,128)}, f32[1024,128]{1,0:T(8,128)}, f32[1024,128]{1,0:T(8,128)}) custom-call(f32[1024,2048]{1,0:T(8,128)} %bitcast.6, f32[136,2048]{1,0:T(8,128)} %collective-permute-done.7.refs_0_.refs_4_.refs_6_.refs_9_, f32[136,2048]{1,0:T(8,128)} %collective-permute-done.9.refs_1_.refs_5_.refs_7_.refs_10_, ...), custom_call_target="tpu_custom_call" | custom-call | flops 1 | bytes 1 | tf_op jit(solution)/shard_map/pair_blocks/pallas_call | solution.py:68
  115.8 26.4 %collective-permute-done.11.refs_3_.refs_4_ = f32[1024,128]{1,0:T(8,128)S(1)} collective-permute-done((f32[1024,128]{1,0:T(8,128)}, f32[1024,128]{1,0:T(8,128)S(1)}, u32[]{:S(2)}, u32[]{:S(2)}) %collective-permute-start.11) | collective-permute-done | bytes 524320 | tf_op jit(solution)/shard_map/ppermute | solution.py:151
  142.3 0.8 copy-done.8
  143.6 0.6 collective-permute-start.19
  144.1 0.5 collective-permute-start.18
  144.6 3.3 %collective-permute-start.17 = (f32[1024,128]{1,0:T(8,128)}, f32[1024,128]{1,0:T(8,128)}, u32[]{:S(2)}, u32[]{:S(2)}) collective-permute-start(f32[1024,128]{1,0:T(8,128)} %get-tuple-element.81), channel_id=1, source_target_pairs={{0,10},{1,11},{2,8},{3,9},{4,14},{5,15},{6,12},{7,13},{8,2},{9,3},... | collective-permute-start | bytes 1572872 | tf_op jit(solution)/shard_map/ppermute | solution.py:151
  148.0 1.3 sub.54.row_ref
  149.3 8.8 %pair_blocks.12 = (f32[1024,128]{1,0:T(8,128)}, f32[1024,128]{1,0:T(8,128)}, f32[1024,128]{1,0:T(8,128)}, f32[1024,128]{1,0:T(8,128)}) custom-call(f32[1024,2048]{1,0:T(8,128)} %bitcast.7, f32[136,2048]{1,0:T(8,128)} %copy-done.5, f32[136,2048]{1,0:T(8,128)} %collective-permute-done.14.refs_1_.refs_7_.refs_10_, ...), custom_call_target="tpu_custom_call" | custom-call | flops 1 | bytes 1 | tf_op jit(solution)/shard_map/pair_blocks/pallas_call | solution.py:68
  158.1 8.8 %pair_blocks.13 = (f32[1024,128]{1,0:T(8,128)}, f32[1024,128]{1,0:T(8,128)}, f32[1024,128]{1,0:T(8,128)}, f32[1024,128]{1,0:T(8,128)}) custom-call(f32[1024,2048]{1,0:T(8,128)} %bitcast.8, f32[136,2048]{1,0:T(8,128)} %copy-done.7, f32[136,2048]{1,0:T(8,128)} %copy-done.4, f32[1024,128]{1,0:T(8,128)} %get-tuple-element.87.refs_2_.refs_0_, ...), custom_call_target="tpu_custom_call" | custom-call | flops 1 | bytes 1 | tf_op jit(solution)/shard_map/pair_blocks/pallas_call | solution.py:68
  166.9 11.9 %density_add.5.refs_2_.refs_8_ = f32[1024,2048]{1,0:T(8,128)} custom-call(f32[1024,1]{1,0:T(8,128)} %sub.54.row_ref, f32[1024,128]{1,0:T(8,128)} %get-tuple-element.64.refs_2_.refs_6_.refs_0_, f32[1024,128]{1,0:T(8,128)} %get-tuple-element.68.refs_2_.refs_1_, f32[1024,128]{1,0:T(8,128)} %get-tuple-element.69.refs_2_, f32[1024,128]{1,0:T(8,128)} %copy-done.9, ...), custom_call_target="tpu_custom_call" | custom-call | flops 1 | bytes 1 | tf_op jit(solution)/shard_map/density_add/pallas_call | solution.py:129
  178.8 3.0 collective-permute-done.18.refs_4_
  181.7 8.1 %collective-permute-done.17.refs_3_ = f32[1024,128]{1,0:T(8,128)} collective-permute-done((f32[1024,128]{1,0:T(8,128)}, f32[1024,128]{1,0:T(8,128)}, u32[]{:S(2)}, u32[]{:S(2)}) %collective-permute-start.17) | collective-permute-done | bytes 524320 | tf_op jit(solution)/shard_map/ppermute | solution.py:151
  189.8 0.5 collective-permute-start.26
  190.3 2.6 collective-permute-start.27
  192.9 2.9 collective-permute-start.28
  195.9 9.0 %pair_blocks.14 = (f32[1024,128]{1,0:T(8,128)}, f32[1024,128]{1,0:T(8,128)}, f32[1024,128]{1,0:T(8,128)}, f32[1024,128]{1,0:T(8,128)}) custom-call(f32[1024,2048]{1,0:T(8,128)} %bitcast.9, f32[136,2048]{1,0:T(8,128)} %copy-done.1, f32[136,2048]{1,0:T(8,128)} %copy-done.2, f32[1024,2048]{1,0:T(8,128)} %density_add.5.refs_2_.refs_8_, ...), custom_call_target="tpu_custom_call" | custom-call | flops 1 | bytes 1 | tf_op jit(solution)/shard_map/pair_blocks/pallas_call | solution.py:68
  204.8 1.3 collective-permute-start.25
  206.1 7.9 %copy.15.refs_13_ = f32[1024,2048]{1,0:T(8,128)} copy(f32[1024,2048]{1,0:T(8,128)} %density_add.5.refs_2_.refs_8_) | data formatting | bytes 16777216
  214.0 13.2 %density_add.6.refs_2_.refs_13_ = f32[1024,2048]{1,0:T(8,128)} custom-call(f32[1024,1]{1,0:T(8,128)} %sub.54.row_ref, f32[1024,128]{1,0:T(8,128)} %get-tuple-element.75.refs_2_.refs_8_.refs_0_, f32[1024,128]{1,0:T(8,128)} %get-tuple-element.78.refs_1_, f32[1024,128]{1,0:T(8,128)} %get-tuple-element.79.refs_2_, ...), custom_call_target="tpu_custom_call", output_to_operand_aliasing={{}: (14, {})} | custom-call | flops 1 | bytes 1 | tf_op jit(solution)/shard_map/density_add/pallas_call | solution.py:129
  227.3 8.8 %pair_blocks.15 = (f32[1024,128]{1,0:T(8,128)}, f32[1024,128]{1,0:T(8,128)}, f32[1024,128]{1,0:T(8,128)}, f32[1024,128]{1,0:T(8,128)}) custom-call(f32[1024,2048]{1,0:T(8,128)} %bitcast.10, f32[136,2048]{1,0:T(8,128)} %collective-permute-done.15.refs_5_.refs_0_.refs_8_.refs_12_, f32[136,2048]{1,0:T(8,128)} %collective-permute-done.16.refs_6_.refs_1_.refs_9_.refs_13_, ...), custom_call_target="tpu_custom_call" | custom-call | flops 1 | bytes 1 | tf_op jit(solution)/shard_map/pair_blocks/pallas_call | solution.py:68
  236.1 1.4 collective-permute-start.22
  237.5 0.5 collective-permute-start.24
  238.0 2.4 collective-permute-done.28.refs_4_
  240.6 0.7 collective-permute-start.21
  241.3 11.3 %collective-permute-done.25.refs_4_ = f32[1024,128]{1,0:T(8,128)S(1)} collective-permute-done((f32[1024,128]{1,0:T(8,128)}, f32[1024,128]{1,0:T(8,128)S(1)}, u32[]{:S(2)}, u32[]{:S(2)}) %collective-permute-start.25) | collective-permute-done | bytes 524320 | tf_op jit(solution)/shard_map/ppermute | solution.py:151
  252.6 13.4 %density_add.7.refs_12_ = f32[1024,2048]{1,0:T(8,128)} custom-call(f32[1024,1]{1,0:T(8,128)} %sub.54.row_ref, f32[1024,128]{1,0:T(8,128)} %get-tuple-element.87.refs_2_.refs_0_, f32[1024,128]{1,0:T(8,128)} %get-tuple-element.109.refs_1_, f32[1024,128]{1,0:T(8,128)} %get-tuple-element.110.refs_2_, ...), custom_call_target="tpu_custom_call", output_to_operand_aliasing={{}: (14, {})} | custom-call | flops 1 | bytes 1 | tf_op jit(solution)/shard_map/density_add/pallas_call | solution.py:129
  266.0 8.9 %collective-permute-done.24.refs_3_ = f32[1024,128]{1,0:T(8,128)S(1)} collective-permute-done((f32[1024,128]{1,0:T(8,128)}, f32[1024,128]{1,0:T(8,128)S(1)}, u32[]{:S(2)}, u32[]{:S(2)}) %collective-permute-start.24) | collective-permute-done | bytes 524320 | tf_op jit(solution)/shard_map/ppermute | solution.py:151
  274.9 0.8 copy-done.12
  275.7 13.2 %density_add.8.refs_16_ = f32[1024,2048]{1,0:T(8,128)} custom-call(f32[1024,1]{1,0:T(8,128)} %sub.54.row_ref, f32[1024,128]{1,0:T(8,128)} %get-tuple-element.89.refs_12_.refs_0_, f32[1024,128]{1,0:T(8,128)} %get-tuple-element.101.refs_1_, f32[1024,128]{1,0:T(8,128)} %get-tuple-element.102.refs_2_, ...), custom_call_target="tpu_custom_call", output_to_operand_aliasing={{}: (13, {})} | custom-call | flops 1 | bytes 1 | tf_op jit(solution)/shard_map/density_add/pallas_call | solution.py:129
  289.0 6.0 %collective-permute-done.20.refs_4_ = f32[1024,128]{1,0:T(8,128)} collective-permute-done((f32[1024,128]{1,0:T(8,128)}, f32[1024,128]{1,0:T(8,128)}, u32[]{:S(2)}, u32[]{:S(2)}) %collective-permute-start.20) | collective-permute-done | bytes 524320 | tf_op jit(solution)/shard_map/ppermute | solution.py:151
  295.0 14.0 %density_add.9 = f32[1024,2048]{1,0:T(8,128)} custom-call(f32[1024,1]{1,0:T(8,128)} %sub.54.row_ref, f32[1024,128]{1,0:T(8,128)} %get-tuple-element.90.refs_12_.refs_0_, f32[1024,128]{1,0:T(8,128)} %get-tuple-element.91.refs_1_, f32[1024,128]{1,0:T(8,128)} %get-tuple-element.88.refs_12_.refs_2_, ...), custom_call_target="tpu_custom_call", output_to_operand_aliasing={{}: (17, {})} | custom-call | flops 1 | bytes 1 | tf_op jit(solution)/shard_map/density_add/pallas_call | solution.py:129
  (69 shorter events, 1.9 us)
Async XLA Ops:
  2.2 52.3 %copy-start.6 = (f32[136,2048]{1,0:T(8,128)}, f32[136,2048]{1,0:T(8,128)S(1)}, u32[]{:S(2)}) copy-start(f32[136,2048]{1,0:T(8,128)S(1)} %select_maximum_fusion.refs_0_.refs_8_.refs_11_) | copy-start | bytes 3342340
  2.2 3.6 %collective-permute-start.3 = (f32[136,2048]{1,0:T(8,128)S(1)}, f32[136,2048]{1,0:T(8,128)S(1)}, u32[]{:S(2)}, u32[]{:S(2)}) collective-permute-start(f32[136,2048]{1,0:T(8,128)S(1)} %select_maximum_fusion.refs_0_.refs_8_.refs_11_), channel_id=1, source_target_pairs={{0,1},{1,0},{2,3},{3,2},{4,5},{5,4},{6,7},{7,6},{8,9},{9,8},{10,11... | collective-permute-start | bytes 3342344 | tf_op jit(solution)/shard_map/ppermute | solution.py:151
  2.3 27.1 %collective-permute-start.2 = (f32[136,2048]{1,0:T(8,128)S(1)}, f32[136,2048]{1,0:T(8,128)}, u32[]{:S(2)}, u32[]{:S(2)}) collective-permute-start(f32[136,2048]{1,0:T(8,128)S(1)} %select_maximum_fusion.refs_0_.refs_8_.refs_11_), channel_id=1, source_target_pairs={{0,2},{1,3},{2,0},{3,1},{4,6},{5,7},{6,4},{7,5},{8,10},{9,11},{10,... | collective-permute-start | bytes 3342344 | tf_op jit(solution)/shard_map/ppermute | solution.py:151
  3.8 48.4 %collective-permute-start.1 = (f32[136,2048]{1,0:T(8,128)S(1)}, f32[136,2048]{1,0:T(8,128)}, u32[]{:S(2)}, u32[]{:S(2)}) collective-permute-start(f32[136,2048]{1,0:T(8,128)S(1)} %select_maximum_fusion.refs_0_.refs_8_.refs_11_), channel_id=1, source_target_pairs={{0,4},{1,5},{2,6},{3,7},{4,0},{5,1},{6,2},{7,3},{8,12},{9,13},{10,... | collective-permute-start | bytes 3342344 | tf_op jit(solution)/shard_map/ppermute | solution.py:151
  5.4 49.0 %collective-permute-start = (f32[136,2048]{1,0:T(8,128)S(1)}, f32[136,2048]{1,0:T(8,128)}, u32[]{:S(2)}, u32[]{:S(2)}) collective-permute-start(f32[136,2048]{1,0:T(8,128)S(1)} %select_maximum_fusion.refs_0_.refs_8_.refs_11_), channel_id=1, source_target_pairs={{0,8},{1,9},{2,10},{3,11},{4,12},{5,13},{6,14},{7,15},{8,0},{9,1},... | collective-permute-start | bytes 3342344 | tf_op jit(solution)/shard_map/ppermute | solution.py:151
  5.8 49.2 %copy-start.7 = (f32[136,2048]{1,0:T(8,128)}, f32[136,2048]{1,0:T(8,128)S(1)}, u32[]{:S(2)}) copy-start(f32[136,2048]{1,0:T(8,128)S(1)} %collective-permute-done.3.refs_5_.refs_0_.refs_10_.refs_14_) | copy-start | bytes 3342340
  54.4 9.4 %collective-permute-start.4 = (f32[136,2048]{1,0:T(8,128)}, f32[136,2048]{1,0:T(8,128)S(1)}, u32[]{:S(2)}, u32[]{:S(2)}) collective-permute-start(f32[136,2048]{1,0:T(8,128)} %collective-permute-done.refs_0_.refs_2_.refs_6_.refs_9_), channel_id=1, source_target_pairs={{0,1},{1,0},{2,3},{3,2},{4,5},{5,4},{6,7},{7,6},{8,9},{9,8},{10,11... | collective-permute-start | bytes 3342344 | tf_op jit(solution)/shard_map/ppermute | solution.py:151
  54.4 9.4 %collective-permute-start.5 = (f32[136,2048]{1,0:T(8,128)}, f32[136,2048]{1,0:T(8,128)S(1)}, u32[]{:S(2)}, u32[]{:S(2)}) collective-permute-start(f32[136,2048]{1,0:T(8,128)} %collective-permute-done.1.refs_1_.refs_3_.refs_8_.refs_11_), channel_id=1, source_target_pairs={{0,1},{1,0},{2,3},{3,2},{4,5},{5,4},{6,7},{7,6},{8,9},{9,8},{10,11... | collective-permute-start | bytes 3342344 | tf_op jit(solution)/shard_map/ppermute | solution.py:151
  55.0 8.9 %collective-permute-start.6 = (f32[136,2048]{1,0:T(8,128)}, f32[136,2048]{1,0:T(8,128)S(1)}, u32[]{:S(2)}, u32[]{:S(2)}) collective-permute-start(f32[136,2048]{1,0:T(8,128)} %collective-permute-done.2.refs_4_.refs_1_.refs_8_.refs_11_), channel_id=1, source_target_pairs={{0,1},{1,0},{2,3},{3,2},{4,5},{5,4},{6,7},{7,6},{8,9},{9,8},{10,11... | collective-permute-start | bytes 3342344 | tf_op jit(solution)/shard_map/ppermute | solution.py:151
  63.8 3.7 %copy-start = (f32[136,2048]{1,0:T(8,128)}, f32[136,2048]{1,0:T(8,128)S(1)}, u32[]{:S(2)}) copy-start(f32[136,2048]{1,0:T(8,128)S(1)} %collective-permute-done.4.refs_0_.refs_3_.refs_7_.refs_10_) | copy-start | bytes 3342340
  63.8 3.6 %copy-start.3 = (f32[136,2048]{1,0:T(8,128)}, f32[136,2048]{1,0:T(8,128)S(1)}, u32[]{:S(2)}) copy-start(f32[136,2048]{1,0:T(8,128)S(1)} %collective-permute-done.5.refs_1_.refs_4_.refs_8_.refs_11_) | copy-start | bytes 3342340
  63.9 3.6 %copy-start.4 = (f32[136,2048]{1,0:T(8,128)}, f32[136,2048]{1,0:T(8,128)S(1)}, u32[]{:S(2)}) copy-start(f32[136,2048]{1,0:T(8,128)S(1)} %collective-permute-done.6.refs_5_.refs_1_.refs_11_.refs_15_) | copy-start | bytes 3342340
  63.9 39.4 %collective-permute-start.9 = (f32[136,2048]{1,0:T(8,128)}, f32[136,2048]{1,0:T(8,128)}, u32[]{:S(2)}, u32[]{:S(2)}) collective-permute-start(f32[136,2048]{1,0:T(8,128)} %collective-permute-done.refs_0_.refs_2_.refs_6_.refs_9_), channel_id=1, source_target_pairs={{0,4},{1,5},{2,6},{3,7},{4,0},{5,1},{6,2},{7,3},{8,12},{9,13},{10,... | collective-permute-start | bytes 3342344 | tf_op jit(solution)/shard_map/ppermute | solution.py:151
  66.6 36.7 %collective-permute-start.7 = (f32[136,2048]{1,0:T(8,128)}, f32[136,2048]{1,0:T(8,128)}, u32[]{:S(2)}, u32[]{:S(2)}) collective-permute-start(f32[136,2048]{1,0:T(8,128)} %collective-permute-done.refs_0_.refs_2_.refs_6_.refs_9_), channel_id=1, source_target_pairs={{0,2},{1,3},{2,0},{3,1},{4,6},{5,7},{6,4},{7,5},{8,10},{9,11},{10,... | collective-permute-start | bytes 3342344 | tf_op jit(solution)/shard_map/ppermute | solution.py:151
  67.1 36.2 %collective-permute-start.8 = (f32[1024,128]{1,0:T(8,128)}, f32[1024,128]{1,0:T(8,128)S(1)}, u32[]{:S(2)}, u32[]{:S(2)}) collective-permute-start(f32[1024,128]{1,0:T(8,128)} %get-tuple-element.67), channel_id=1, source_target_pairs={{0,8},{1,9},{2,10},{3,11},{4,12},{5,13},{6,14},{7,15},{8,0},{9,1},... | collective-permute-start | bytes 1572872 | tf_op jit(solution)/shard_map/ppermute | solution.py:151
  103.3 2.3 copy-start.9
  103.3 38.9 %collective-permute-start.13 = (f32[136,2048]{1,0:T(8,128)}, f32[136,2048]{1,0:T(8,128)S(1)}, u32[]{:S(2)}, u32[]{:S(2)}) collective-permute-start(f32[136,2048]{1,0:T(8,128)} %collective-permute-done.7.refs_0_.refs_4_.refs_6_.refs_9_), channel_id=1, source_target_pairs={{0,1},{1,0},{2,3},{3,2},{4,5},{5,4},{6,7},{7,6},{8,9},{9,8},{10,11... | collective-permute-start | bytes 3342344 | tf_op jit(solution)/shard_map/ppermute | solution.py:151
  103.4 38.8 %collective-permute-start.10 = (f32[136,2048]{1,0:T(8,128)}, f32[136,2048]{1,0:T(8,128)S(1)}, u32[]{:S(2)}, u32[]{:S(2)}) collective-permute-start(f32[136,2048]{1,0:T(8,128)} %collective-permute-done.7.refs_0_.refs_4_.refs_6_.refs_9_), channel_id=1, source_target_pairs={{0,4},{1,5},{2,6},{3,7},{4,0},{5,1},{6,2},{7,3},{8,12},{9,13},{10,... | collective-permute-start | bytes 3342344 | tf_op jit(solution)/shard_map/ppermute | solution.py:151
  105.1 37.1 %collective-permute-start.12 = (f32[136,2048]{1,0:T(8,128)}, f32[136,2048]{1,0:T(8,128)S(1)}, u32[]{:S(2)}, u32[]{:S(2)}) collective-permute-start(f32[136,2048]{1,0:T(8,128)} %collective-permute-done.1.refs_1_.refs_3_.refs_8_.refs_11_), channel_id=1, source_target_pairs={{0,2},{1,3},{2,0},{3,1},{4,6},{5,7},{6,4},{7,5},{8,10},{9,11},{10,... | collective-permute-start | bytes 3342344 | tf_op jit(solution)/shard_map/ppermute | solution.py:151
  105.6 36.6 %collective-permute-start.14 = (f32[136,2048]{1,0:T(8,128)}, f32[136,2048]{1,0:T(8,128)}, u32[]{:S(2)}, u32[]{:S(2)}) collective-permute-start(f32[136,2048]{1,0:T(8,128)} %collective-permute-done.9.refs_1_.refs_5_.refs_7_.refs_10_), channel_id=1, source_target_pairs={{0,1},{1,0},{2,3},{3,2},{4,5},{5,4},{6,7},{7,6},{8,9},{9,8},{10,11... | collective-permute-start | bytes 3342344 | tf_op jit(solution)/shard_map/ppermute | solution.py:151
  105.6 42.3 %copy-start.17 = (f32[64]{0:T(128)S(1)}, f32[64]{0:T(128)}, u32[]{:S(2)}) copy-start(f32[64]{0:T(128)} %param.9) | copy-start | bytes 772
  105.6 42.3 %copy-start.18 = (f32[16]{0:T(128)S(1)}, f32[16]{0:T(128)}, u32[]{:S(2)}) copy-start(f32[16]{0:T(128)} %param.7) | copy-start | bytes 196
  105.6 36.6 %collective-permute-start.11 = (f32[1024,128]{1,0:T(8,128)}, f32[1024,128]{1,0:T(8,128)S(1)}, u32[]{:S(2)}, u32[]{:S(2)}) collective-permute-start(f32[1024,128]{1,0:T(8,128)} %get-tuple-element.72), channel_id=1, source_target_pairs={{0,9},{1,8},{2,11},{3,10},{4,13},{5,12},{6,15},{7,14},{8,1},{9,0},... | collective-permute-start | bytes 1572872 | tf_op jit(solution)/shard_map/ppermute | solution.py:151
  142.2 0.8 copy-start.8
  142.2 7.0 %copy-start.5 = (f32[136,2048]{1,0:T(8,128)}, f32[136,2048]{1,0:T(8,128)S(1)}, u32[]{:S(2)}) copy-start(f32[136,2048]{1,0:T(8,128)S(1)} %collective-permute-done.13.refs_0_.refs_6_.refs_9_) | copy-start | bytes 3342340
  142.2 7.0 %copy-start.1 = (f32[136,2048]{1,0:T(8,128)}, f32[136,2048]{1,0:T(8,128)S(1)}, u32[]{:S(2)}) copy-start(f32[136,2048]{1,0:T(8,128)S(1)} %collective-permute-done.10.refs_4_.refs_0_.refs_6_.refs_9_) | copy-start | bytes 3342340
  142.2 7.0 %copy-start.2 = (f32[136,2048]{1,0:T(8,128)}, f32[136,2048]{1,0:T(8,128)S(1)}, u32[]{:S(2)}) copy-start(f32[136,2048]{1,0:T(8,128)S(1)} %collective-permute-done.12.refs_5_.refs_1_.refs_7_.refs_10_) | copy-start | bytes 3342340
  143.1 46.8 %collective-permute-start.15 = (f32[136,2048]{1,0:T(8,128)S(1)}, f32[136,2048]{1,0:T(8,128)}, u32[]{:S(2)}, u32[]{:S(2)}) collective-permute-start(f32[136,2048]{1,0:T(8,128)S(1)} %collective-permute-done.10.refs_4_.refs_0_.refs_6_.refs_9_), channel_id=1, source_target_pairs={{0,1},{1,0},{2,3},{3,2},{4,5},{5,4},{6,7},{7,6},{8,9},{9,8},{10,11... | collective-permute-start | bytes 3342344 | tf_op jit(solution)/shard_map/ppermute | solution.py:151
  143.3 46.5 %collective-permute-start.16 = (f32[136,2048]{1,0:T(8,128)S(1)}, f32[136,2048]{1,0:T(8,128)}, u32[]{:S(2)}, u32[]{:S(2)}) collective-permute-start(f32[136,2048]{1,0:T(8,128)S(1)} %collective-permute-done.12.refs_5_.refs_1_.refs_7_.refs_10_), channel_id=1, source_target_pairs={{0,1},{1,0},{2,3},{3,2},{4,5},{5,4},{6,7},{7,6},{8,9},{9,8},{10,11... | collective-permute-start | bytes 3342344 | tf_op jit(solution)/shard_map/ppermute | solution.py:151
  143.6 35.2 %collective-permute-start.19 = (f32[1024,128]{1,0:T(8,128)}, f32[1024,128]{1,0:T(8,128)}, u32[]{:S(2)}, u32[]{:S(2)}) collective-permute-start(f32[1024,128]{1,0:T(8,128)} %get-tuple-element.85), channel_id=1, source_target_pairs={{0,4},{1,5},{2,6},{3,7},{4,0},{5,1},{6,2},{7,3},{8,12},{9,13},{10,... | collective-permute-start | bytes 1572872 | tf_op jit(solution)/shard_map/ppermute | solution.py:151
  144.1 37.6 %collective-permute-start.18 = (f32[1024,128]{1,0:T(8,128)}, f32[1024,128]{1,0:T(8,128)}, u32[]{:S(2)}, u32[]{:S(2)}) collective-permute-start(f32[1024,128]{1,0:T(8,128)} %get-tuple-element.83), channel_id=1, source_target_pairs={{0,12},{1,13},{2,14},{3,15},{4,8},{5,9},{6,10},{7,11},{8,4},{9,5},... | collective-permute-start | bytes 1572872 | tf_op jit(solution)/shard_map/ppermute | solution.py:151
  144.6 45.2 %collective-permute-start.17 = (f32[1024,128]{1,0:T(8,128)}, f32[1024,128]{1,0:T(8,128)}, u32[]{:S(2)}, u32[]{:S(2)}) collective-permute-start(f32[1024,128]{1,0:T(8,128)} %get-tuple-element.81), channel_id=1, source_target_pairs={{0,10},{1,11},{2,8},{3,9},{4,14},{5,15},{6,12},{7,13},{8,2},{9,3},... | collective-permute-start | bytes 1572872 | tf_op jit(solution)/shard_map/ppermute | solution.py:151
  189.8 46.3 %collective-permute-start.26 = (f32[1024,128]{1,0:T(8,128)}, f32[1024,128]{1,0:T(8,128)S(1)}, u32[]{:S(2)}, u32[]{:S(2)}) collective-permute-start(f32[1024,128]{1,0:T(8,128)} %get-tuple-element.108), channel_id=1, source_target_pairs={{0,2},{1,3},{2,0},{3,1},{4,6},{5,7},{6,4},{7,5},{8,10},{9,11},{10,... | collective-permute-start | bytes 1572872 | tf_op jit(solution)/shard_map/ppermute | solution.py:151
  190.3 47.1 %collective-permute-start.27 = (f32[1024,128]{1,0:T(8,128)}, f32[1024,128]{1,0:T(8,128)S(1)}, u32[]{:S(2)}, u32[]{:S(2)}) collective-permute-start(f32[1024,128]{1,0:T(8,128)} %get-tuple-element.112), channel_id=1, source_target_pairs={{0,11},{1,10},{2,9},{3,8},{4,15},{5,14},{6,13},{7,12},{8,3},{9,2},... | collective-permute-start | bytes 1572872 | tf_op jit(solution)/shard_map/ppermute | solution.py:151
  192.9 47.4 %collective-permute-start.28 = (f32[1024,128]{1,0:T(8,128)}, f32[1024,128]{1,0:T(8,128)S(1)}, u32[]{:S(2)}, u32[]{:S(2)}) collective-permute-start(f32[1024,128]{1,0:T(8,128)} %get-tuple-element.114), channel_id=1, source_target_pairs={{0,13},{1,12},{2,15},{3,14},{4,9},{5,8},{6,11},{7,10},{8,5},{9,4},... | collective-permute-start | bytes 1572872 | tf_op jit(solution)/shard_map/ppermute | solution.py:151
  195.8 44.7 %collective-permute-start.29 = (f32[1024,128]{1,0:T(8,128)}, f32[1024,128]{1,0:T(8,128)S(1)}, u32[]{:S(2)}, u32[]{:S(2)}) collective-permute-start(f32[1024,128]{1,0:T(8,128)} %get-tuple-element.116), channel_id=1, source_target_pairs={{0,5},{1,4},{2,7},{3,6},{4,1},{5,0},{6,3},{7,2},{8,13},{9,12},{10,... | collective-permute-start | bytes 1572872 | tf_op jit(solution)/shard_map/ppermute | solution.py:151
  204.8 47.7 %collective-permute-start.25 = (f32[1024,128]{1,0:T(8,128)}, f32[1024,128]{1,0:T(8,128)S(1)}, u32[]{:S(2)}, u32[]{:S(2)}) collective-permute-start(f32[1024,128]{1,0:T(8,128)} %get-tuple-element.106), channel_id=1, source_target_pairs={{0,6},{1,7},{2,4},{3,5},{4,2},{5,3},{6,0},{7,1},{8,14},{9,15},{10,... | collective-permute-start | bytes 1572872 | tf_op jit(solution)/shard_map/ppermute | solution.py:151
  236.1 29.9 %copy-start.10 = (f32[1024,128]{1,0:T(8,128)}, f32[1024,128]{1,0:T(8,128)S(1)}, u32[]{:S(2)}) copy-start(f32[1024,128]{1,0:T(8,128)S(1)} %collective-permute-done.26.refs_5_) | copy-start | bytes 1572868
  236.1 52.9 %collective-permute-start.22 = (f32[1024,128]{1,0:T(8,128)}, f32[1024,128]{1,0:T(8,128)S(1)}, u32[]{:S(2)}, u32[]{:S(2)}) collective-permute-start(f32[1024,128]{1,0:T(8,128)} %get-tuple-element.98), channel_id=1, source_target_pairs={{0,1},{1,0},{2,3},{3,2},{4,5},{5,4},{6,7},{7,6},{8,9},{9,8},{10,11... | collective-permute-start | bytes 1572872 | tf_op jit(solution)/shard_map/ppermute | solution.py:151
  237.5 15.1 %copy-start.14 = (f32[1024,128]{1,0:T(8,128)}, f32[1024,128]{1,0:T(8,128)S(1)}, u32[]{:S(2)}) copy-start(f32[1024,128]{1,0:T(8,128)S(1)} %collective-permute-done.27.refs_3_) | copy-start | bytes 1572868
  237.5 37.4 %collective-permute-start.24 = (f32[1024,128]{1,0:T(8,128)}, f32[1024,128]{1,0:T(8,128)S(1)}, u32[]{:S(2)}, u32[]{:S(2)}) collective-permute-start(f32[1024,128]{1,0:T(8,128)} %get-tuple-element.104), channel_id=1, source_target_pairs={{0,14},{1,15},{2,12},{3,13},{4,10},{5,11},{6,8},{7,9},{8,6},{9,7},... | collective-permute-start | bytes 1572872 | tf_op jit(solution)/shard_map/ppermute | solution.py:151
  240.4 12.2 %copy-start.15 = (f32[1024,128]{1,0:T(8,128)}, f32[1024,128]{1,0:T(8,128)S(1)}, u32[]{:S(2)}) copy-start(f32[1024,128]{1,0:T(8,128)S(1)} %collective-permute-done.28.refs_4_) | copy-start | bytes 1572868
  240.4 48.6 %collective-permute-start.23 = (f32[1024,128]{1,0:T(8,128)}, f32[1024,128]{1,0:T(8,128)}, u32[]{:S(2)}, u32[]{:S(2)}) collective-permute-start(f32[1024,128]{1,0:T(8,128)} %get-tuple-element.100), channel_id=1, source_target_pairs={{0,3},{1,2},{2,1},{3,0},{4,7},{5,6},{6,5},{7,4},{8,11},{9,10},{10,... | collective-permute-start | bytes 1572872 | tf_op jit(solution)/shard_map/ppermute | solution.py:151
  240.6 12.0 %copy-start.16 = (f32[1024,128]{1,0:T(8,128)}, f32[1024,128]{1,0:T(8,128)S(1)}, u32[]{:S(2)}) copy-start(f32[1024,128]{1,0:T(8,128)S(1)} %collective-permute-done.29.refs_5_) | copy-start | bytes 1572868
  240.6 48.4 %collective-permute-start.21 = (f32[1024,128]{1,0:T(8,128)}, f32[1024,128]{1,0:T(8,128)}, u32[]{:S(2)}, u32[]{:S(2)}) collective-permute-start(f32[1024,128]{1,0:T(8,128)} %get-tuple-element.96), channel_id=1, source_target_pairs={{0,7},{1,6},{2,5},{3,4},{4,3},{5,2},{6,1},{7,0},{8,15},{9,14},{10,... | collective-permute-start | bytes 1572872 | tf_op jit(solution)/shard_map/ppermute | solution.py:151
  252.6 13.4 %copy-start.11 = (f32[1024,128]{1,0:T(8,128)}, f32[1024,128]{1,0:T(8,128)S(1)}, u32[]{:S(2)}) copy-start(f32[1024,128]{1,0:T(8,128)S(1)} %collective-permute-done.25.refs_4_) | copy-start | bytes 1572868
  252.6 42.5 %collective-permute-start.20 = (f32[1024,128]{1,0:T(8,128)}, f32[1024,128]{1,0:T(8,128)}, u32[]{:S(2)}, u32[]{:S(2)}) collective-permute-start(f32[1024,128]{1,0:T(8,128)} %get-tuple-element.94), channel_id=1, source_target_pairs={{0,15},{1,14},{2,13},{3,12},{4,11},{5,10},{6,9},{7,8},{8,7},{9,6},... | collective-permute-start | bytes 1572872 | tf_op jit(solution)/shard_map/ppermute | solution.py:151
  289.0 6.1 %copy-start.13 = (f32[1024,128]{1,0:T(8,128)}, f32[1024,128]{1,0:T(8,128)S(1)}, u32[]{:S(2)}) copy-start(f32[1024,128]{1,0:T(8,128)S(1)} %collective-permute-done.22.refs_6_) | copy-start | bytes 1572868
  (1 other events, 0.8 us)

commit v4 on v3

--- a/solution.py
+++ b/solution.py
@@ -178,12 +178,13 @@
         + shard(pick("middle"), low)
         + shard(pick("flat"), lambda k: flat)
         + twin("own"),
-        twin("far", "middle", "flat") + pair(pick("far", "middle")),
+        twin("far", "middle", "flat") + pair(pick("far")),
         reply(pick("far"))
         + shard(pick("far_flat"), lambda k: flat)
         + shard(pick("far_middle"), low)
         + pair(other("far", "middle"))
-        + pair(pick("own", "flat")),
+        + pair(pick("own", "flat"))
+        + pair(pick("middle")),
         reply(other("far"))
         + shard(pick("all"), low)
         + shard(pick("middle_flat"), lambda k: flat)

time: 311 us -> 314 us (level); the launches traced: 309 us -> 308 us
  waiting for transfers between devices: 133 us -> 125 us
  Pallas kernels: 136 us -> 143 us
    ppermute x30, waiting for transfers between devices: 133 us -> 125 us  [across(): return lax.ppermute(x, AXIS, [(i, i ^ bits) for i in range(size)])]
    pallas_call x8 -> x9, Pallas kernels: 70.7 us -> 77.5 us  [pair_blocks(): pl.pallas_call(functools.partial(pair_kernel, count, len(after), height,...]
    unnamed x39 -> x43, local copies, waits for them, and re-layouts: 9.56 us -> 9.54 us
  transfers between devices with their start and end apart: 30 -> 30, of which waited for: 11 -> 11; matrix products, arithmetic and copies ran while one was open for 3% -> 3% of each run, Pallas kernels for 40% -> 42%
where the time goes in v4:
time: 314 us; the launch traced here: 308 us
  Pallas kernels  143 us (46%)
  waiting for transfers between devices  125 us (40%)
  starting transfers between devices  26.8 us (9%)
  local copies, waits for them, and re-layouts  10.9 us (3%)
    ppermute x30, waiting for transfers between devices, across(): return lax.ppermute(x, AXIS, [(i, i ^ bits) for i in range(size)])  125 us
    pallas_call x9, Pallas kernels, pair_blocks(): pl.pallas_call(functools.partial(pair_kernel, count, len(after), height,...  77.5 us
    pallas_call x5, Pallas kernels, density_add(): pl.pallas_call(functools.partial(density_kernel, count, len(after), first...  66 us
    ppermute x30, starting transfers between devices, across(): return lax.ppermute(x, AXIS, [(i, i ^ bits) for i in range(size)])  26.8 us
    unnamed x43, local copies, waits for them, and re-layouts  9.54 us
  transfers between devices with their start and end apart: 30, of which 11 were waited for; matrix products, arithmetic and copies ran while one was open for 3% of the time, Pallas kernels for 42%

profile of v4, /device:TPU:16, one launch (start us, length us, event | category | flops | bytes accessed | tf_op | source)
XLA Modules:
  0.0 308.4 jit_solution(11220418899763991069)
XLA Ops:
  0.0 0.7 broadcast_subtract_fusion.1
  0.8 1.3 select_maximum_fusion.refs_0_.refs_8_.refs_11_
  2.3 1.6 collective-permute-start.2
  3.8 1.6 collective-permute-start.1
  5.8 23.6 %collective-permute-done.2.refs_3_.refs_1_.refs_8_.refs_11_ = f32[136,2048]{1,0:T(8,128)} collective-permute-done((f32[136,2048]{1,0:T(8,128)S(1)}, f32[136,2048]{1,0:T(8,128)}, u32[]{:S(2)}, u32[]{:S(2)}) %collective-permute-start.2) | collective-permute-done | bytes 1114144 | tf_op jit(solution)/shard_map/ppermute | solution.py:151
  29.3 22.9 %collective-permute-done.1.refs_2_.refs_0_.refs_8_.refs_11_ = f32[136,2048]{1,0:T(8,128)} collective-permute-done((f32[136,2048]{1,0:T(8,128)S(1)}, f32[136,2048]{1,0:T(8,128)}, u32[]{:S(2)}, u32[]{:S(2)}) %collective-permute-start.1) | collective-permute-done | bytes 1114144 | tf_op jit(solution)/shard_map/ppermute | solution.py:151
  52.2 2.2 collective-permute-done.refs_0_.refs_1_.refs_6_.refs_9_
  54.4 0.5 collective-permute-start.5
  55.0 7.9 %pair_blocks.9 = (f32[1024,128]{1,0:T(8,128)}, f32[1024,128]{1,0:T(8,128)}) custom-call(f32[1024,2048]{1,0:T(8,128)} %bitcast.3, f32[136,2048]{1,0:T(8,128)} %collective-permute-done.refs_0_.refs_1_.refs_6_.refs_9_, f32[136,2048]{1,0:T(8,128)} %collective-permute-done.refs_0_.refs_1_.refs_6_.refs_9_, ...), custom_call_target="tpu_custom_call" | custom-call | flops 1 | bytes 1 | tf_op jit(solution)/shard_map/pair_blocks/pallas_call | solution.py:68
  63.0 2.8 collective-permute-start.9
  65.7 0.5 collective-permute-start.7
  66.6 8.8 %pair_blocks.10 = (f32[1024,128]{1,0:T(8,128)}, f32[1024,128]{1,0:T(8,128)}, f32[1024,128]{1,0:T(8,128)}, f32[1024,128]{1,0:T(8,128)}) custom-call(f32[1024,2048]{1,0:T(8,128)} %bitcast.4, f32[136,2048]{1,0:T(8,128)} %copy-done, f32[136,2048]{1,0:T(8,128)} %copy-done.1, f32[1024,128]{1,0:T(8,128)} %get-tuple-element.64.refs_2_.refs_6_.refs_5_.refs_0_, ...), custom_call_target="tpu_custom_call" | custom-call | flops 1 | bytes 1 | tf_op jit(solution)/shard_map/pair_blocks/pallas_call | solution.py:68
  75.4 8.8 %pair_blocks.11 = (f32[1024,128]{1,0:T(8,128)}, f32[1024,128]{1,0:T(8,128)}, f32[1024,128]{1,0:T(8,128)}, f32[1024,128]{1,0:T(8,128)}) custom-call(f32[1024,2048]{1,0:T(8,128)} %bitcast.5, f32[136,2048]{1,0:T(8,128)} %copy-done.6, f32[136,2048]{1,0:T(8,128)} %collective-permute-done.2.refs_3_.refs_1_.refs_8_.refs_11_, ...), custom_call_target="tpu_custom_call" | custom-call | flops 1 | bytes 1 | tf_op jit(solution)/shard_map/pair_blocks/pallas_call | solution.py:68
  84.2 7.9 %pair_blocks.12 = (f32[1024,128]{1,0:T(8,128)}, f32[1024,128]{1,0:T(8,128)}) custom-call(f32[1024,2048]{1,0:T(8,128)} %bitcast.6, f32[136,2048]{1,0:T(8,128)} %collective-permute-done.1.refs_2_.refs_0_.refs_8_.refs_11_, f32[1024,128]{1,0:T(8,128)} %get-tuple-element.69.refs_1_.refs_2_, f32[136,2048]{1,0:T(8,128)} %copy-done, f32[136,2048]{1,0:T(8,128)} %copy-done.1, ...), custom_call_target="tpu_custom_call" | custom-call | flops 1 | bytes 1 | tf_op jit(solution)/shard_map/pair_blocks/pallas_call | solution.py:68
  92.1 10.3 %collective-permute-done.8.refs_3_ = f32[1024,128]{1,0:T(8,128)S(1)} collective-permute-done((f32[1024,128]{1,0:T(8,128)}, f32[1024,128]{1,0:T(8,128)S(1)}, u32[]{:S(2)}, u32[]{:S(2)}) %collective-permute-start.8) | collective-permute-done | bytes 524320 | tf_op jit(solution)/shard_map/ppermute | solution.py:151
  102.5 1.7 collective-permute-start.10
  104.2 0.5 collective-permute-start.12
  104.7 1.3 collective-permute-start.11
  106.1 8.8 %pair_blocks.13 = (f32[1024,128]{1,0:T(8,128)}, f32[1024,128]{1,0:T(8,128)}, f32[1024,128]{1,0:T(8,128)}, f32[1024,128]{1,0:T(8,128)}) custom-call(f32[1024,2048]{1,0:T(8,128)} %bitcast.7, f32[136,2048]{1,0:T(8,128)} %collective-permute-done.7.refs_0_.refs_4_.refs_6_.refs_9_, f32[136,2048]{1,0:T(8,128)} %collective-permute-done.9.refs_1_.refs_5_.refs_7_.refs_10_, ...), custom_call_target="tpu_custom_call" | custom-call | flops 1 | bytes 1 | tf_op jit(solution)/shard_map/pair_blocks/pallas_call | solution.py:68
  114.9 26.5 %collective-permute-done.11.refs_3_.refs_4_ = f32[1024,128]{1,0:T(8,128)S(1)} collective-permute-done((f32[1024,128]{1,0:T(8,128)}, f32[1024,128]{1,0:T(8,128)S(1)}, u32[]{:S(2)}, u32[]{:S(2)}) %collective-permute-start.11) | collective-permute-done | bytes 524320 | tf_op jit(solution)/shard_map/ppermute | solution.py:151
  141.4 0.8 copy-done.8
  142.6 0.6 collective-permute-start.19
  143.2 0.5 collective-permute-start.18
  143.7 3.3 %collective-permute-start.17 = (f32[1024,128]{1,0:T(8,128)}, f32[1024,128]{1,0:T(8,128)}, u32[]{:S(2)}, u32[]{:S(2)}) collective-permute-start(f32[1024,128]{1,0:T(8,128)} %get-tuple-element.81), channel_id=1, source_target_pairs={{0,10},{1,11},{2,8},{3,9},{4,14},{5,15},{6,12},{7,13},{8,2},{9,3},... | collective-permute-start | bytes 1572872 | tf_op jit(solution)/shard_map/ppermute | solution.py:151
  147.1 1.3 sub.54.row_ref
  148.3 8.8 %pair_blocks.14 = (f32[1024,128]{1,0:T(8,128)}, f32[1024,128]{1,0:T(8,128)}, f32[1024,128]{1,0:T(8,128)}, f32[1024,128]{1,0:T(8,128)}) custom-call(f32[1024,2048]{1,0:T(8,128)} %bitcast.8, f32[136,2048]{1,0:T(8,128)} %copy-done.5, f32[136,2048]{1,0:T(8,128)} %collective-permute-done.14.refs_1_.refs_7_.refs_10_, ...), custom_call_target="tpu_custom_call" | custom-call | flops 1 | bytes 1 | tf_op jit(solution)/shard_map/pair_blocks/pallas_call | solution.py:68
  157.1 8.8 %pair_blocks.15 = (f32[1024,128]{1,0:T(8,128)}, f32[1024,128]{1,0:T(8,128)}, f32[1024,128]{1,0:T(8,128)}, f32[1024,128]{1,0:T(8,128)}) custom-call(f32[1024,2048]{1,0:T(8,128)} %bitcast.9, f32[136,2048]{1,0:T(8,128)} %copy-done.7, f32[136,2048]{1,0:T(8,128)} %copy-done.2, f32[1024,128]{1,0:T(8,128)} %get-tuple-element.87.refs_2_.refs_0_, ...), custom_call_target="tpu_custom_call" | custom-call | flops 1 | bytes 1 | tf_op jit(solution)/shard_map/pair_blocks/pallas_call | solution.py:68
  166.0 12.1 %density_add.5.refs_2_.refs_8_ = f32[1024,2048]{1,0:T(8,128)} custom-call(f32[1024,1]{1,0:T(8,128)} %sub.54.row_ref, f32[1024,128]{1,0:T(8,128)} %get-tuple-element.64.refs_2_.refs_6_.refs_5_.refs_0_, f32[1024,128]{1,0:T(8,128)} %get-tuple-element.68.refs_2_.refs_1_, f32[1024,128]{1,0:T(8,128)} %get-tuple-element.69.refs_1_.refs_2_, f32[1024,128]{1,0:T(8,128)} %copy-done.9, ...), custom_call_target="tpu_custom_call" | custom-call | flops 1 | bytes 1 | tf_op jit(solution)/shard_map/density_add/pallas_call | solution.py:129
  178.1 2.8 collective-permute-done.18.refs_4_
  180.8 8.1 %collective-permute-done.17.refs_3_ = f32[1024,128]{1,0:T(8,128)} collective-permute-done((f32[1024,128]{1,0:T(8,128)}, f32[1024,128]{1,0:T(8,128)}, u32[]{:S(2)}, u32[]{:S(2)}) %collective-permute-start.17) | collective-permute-done | bytes 524320 | tf_op jit(solution)/shard_map/ppermute | solution.py:151
  188.9 0.6 collective-permute-start.26
  189.5 2.6 collective-permute-start.27
  192.1 3.0 collective-permute-start.28
  195.0 8.8 %pair_blocks.16 = (f32[1024,128]{1,0:T(8,128)}, f32[1024,128]{1,0:T(8,128)}, f32[1024,128]{1,0:T(8,128)}, f32[1024,128]{1,0:T(8,128)}) custom-call(f32[1024,2048]{1,0:T(8,128)} %bitcast.10, f32[136,2048]{1,0:T(8,128)} %copy-done.3, f32[136,2048]{1,0:T(8,128)} %copy-done.4, f32[1024,2048]{1,0:T(8,128)} %density_add.5.refs_2_.refs_8_, ...), custom_call_target="tpu_custom_call" | custom-call | flops 1 | bytes 1 | tf_op jit(solution)/shard_map/pair_blocks/pallas_call | solution.py:68
  203.8 1.4 collective-permute-start.25
  205.3 7.9 %copy.15.refs_13_ = f32[1024,2048]{1,0:T(8,128)} copy(f32[1024,2048]{1,0:T(8,128)} %density_add.5.refs_2_.refs_8_) | data formatting | bytes 16777216
  213.2 13.2 %density_add.6.refs_2_.refs_13_ = f32[1024,2048]{1,0:T(8,128)} custom-call(f32[1024,1]{1,0:T(8,128)} %sub.54.row_ref, f32[1024,128]{1,0:T(8,128)} %get-tuple-element.76.refs_2_.refs_8_.refs_0_, f32[1024,128]{1,0:T(8,128)} %get-tuple-element.79.refs_1_, f32[1024,128]{1,0:T(8,128)} %get-tuple-element.70.refs_2_, ...), custom_call_target="tpu_custom_call", output_to_operand_aliasing={{}: (14, {})} | custom-call | flops 1 | bytes 1 | tf_op jit(solution)/shard_map/density_add/pallas_call | solution.py:129
  226.4 8.8 %pair_blocks.17 = (f32[1024,128]{1,0:T(8,128)}, f32[1024,128]{1,0:T(8,128)}, f32[1024,128]{1,0:T(8,128)}, f32[1024,128]{1,0:T(8,128)}) custom-call(f32[1024,2048]{1,0:T(8,128)} %bitcast.11, f32[136,2048]{1,0:T(8,128)} %collective-permute-done.15.refs_5_.refs_0_.refs_8_.refs_12_, f32[136,2048]{1,0:T(8,128)} %collective-permute-done.16.refs_6_.refs_1_.refs_9_.refs_13_, ...), custom_call_target="tpu_custom_call" | custom-call | flops 1 | bytes 1 | tf_op jit(solution)/shard_map/pair_blocks/pallas_call | solution.py:68
  235.2 1.4 collective-permute-start.22
  237.1 2.2 collective-permute-done.28.refs_4_
  239.5 1.0 collective-permute-start.21
  240.5 11.4 %collective-permute-done.25.refs_4_ = f32[1024,128]{1,0:T(8,128)S(1)} collective-permute-done((f32[1024,128]{1,0:T(8,128)}, f32[1024,128]{1,0:T(8,128)S(1)}, u32[]{:S(2)}, u32[]{:S(2)}) %collective-permute-start.25) | collective-permute-done | bytes 524320 | tf_op jit(solution)/shard_map/ppermute | solution.py:151
  251.9 13.4 %density_add.7.refs_12_ = f32[1024,2048]{1,0:T(8,128)} custom-call(f32[1024,1]{1,0:T(8,128)} %sub.54.row_ref, f32[1024,128]{1,0:T(8,128)} %get-tuple-element.87.refs_2_.refs_0_, f32[1024,128]{1,0:T(8,128)} %get-tuple-element.109.refs_1_, f32[1024,128]{1,0:T(8,128)} %get-tuple-element.110.refs_2_, ...), custom_call_target="tpu_custom_call", output_to_operand_aliasing={{}: (14, {})} | custom-call | flops 1 | bytes 1 | tf_op jit(solution)/shard_map/density_add/pallas_call | solution.py:129
  265.3 8.8 %collective-permute-done.24.refs_3_ = f32[1024,128]{1,0:T(8,128)S(1)} collective-permute-done((f32[1024,128]{1,0:T(8,128)}, f32[1024,128]{1,0:T(8,128)S(1)}, u32[]{:S(2)}, u32[]{:S(2)}) %collective-permute-start.24) | collective-permute-done | bytes 524320 | tf_op jit(solution)/shard_map/ppermute | solution.py:151
  274.1 0.8 copy-done.12
  274.9 13.2 %density_add.8.refs_16_ = f32[1024,2048]{1,0:T(8,128)} custom-call(f32[1024,1]{1,0:T(8,128)} %sub.54.row_ref, f32[1024,128]{1,0:T(8,128)} %get-tuple-element.89.refs_12_.refs_0_, f32[1024,128]{1,0:T(8,128)} %get-tuple-element.101.refs_1_, f32[1024,128]{1,0:T(8,128)} %get-tuple-element.102.refs_2_, ...), custom_call_target="tpu_custom_call", output_to_operand_aliasing={{}: (13, {})} | custom-call | flops 1 | bytes 1 | tf_op jit(solution)/shard_map/density_add/pallas_call | solution.py:129
  288.2 6.0 %collective-permute-done.20.refs_4_ = f32[1024,128]{1,0:T(8,128)} collective-permute-done((f32[1024,128]{1,0:T(8,128)}, f32[1024,128]{1,0:T(8,128)}, u32[]{:S(2)}, u32[]{:S(2)}) %collective-permute-start.20) | collective-permute-done | bytes 524320 | tf_op jit(solution)/shard_map/ppermute | solution.py:151
  294.2 14.0 %density_add.9 = f32[1024,2048]{1,0:T(8,128)} custom-call(f32[1024,1]{1,0:T(8,128)} %sub.54.row_ref, f32[1024,128]{1,0:T(8,128)} %get-tuple-element.90.refs_12_.refs_0_, f32[1024,128]{1,0:T(8,128)} %get-tuple-element.91.refs_1_, f32[1024,128]{1,0:T(8,128)} %get-tuple-element.88.refs_12_.refs_2_, ...), custom_call_target="tpu_custom_call", output_to_operand_aliasing={{}: (17, {})} | custom-call | flops 1 | bytes 1 | tf_op jit(solution)/shard_map/density_add/pallas_call | solution.py:129
  (74 shorter events, 2.3 us)
Async XLA Ops:
  2.2 52.3 %copy-start.6 = (f32[136,2048]{1,0:T(8,128)}, f32[136,2048]{1,0:T(8,128)S(1)}, u32[]{:S(2)}) copy-start(f32[136,2048]{1,0:T(8,128)S(1)} %select_maximum_fusion.refs_0_.refs_8_.refs_11_) | copy-start | bytes 3342340
  2.2 3.6 %collective-permute-start.3 = (f32[136,2048]{1,0:T(8,128)S(1)}, f32[136,2048]{1,0:T(8,128)S(1)}, u32[]{:S(2)}, u32[]{:S(2)}) collective-permute-start(f32[136,2048]{1,0:T(8,128)S(1)} %select_maximum_fusion.refs_0_.refs_8_.refs_11_), channel_id=1, source_target_pairs={{0,1},{1,0},{2,3},{3,2},{4,5},{5,4},{6,7},{7,6},{8,9},{9,8},{10,11... | collective-permute-start | bytes 3342344 | tf_op jit(solution)/shard_map/ppermute | solution.py:151
  2.3 27.1 %collective-permute-start.2 = (f32[136,2048]{1,0:T(8,128)S(1)}, f32[136,2048]{1,0:T(8,128)}, u32[]{:S(2)}, u32[]{:S(2)}) collective-permute-start(f32[136,2048]{1,0:T(8,128)S(1)} %select_maximum_fusion.refs_0_.refs_8_.refs_11_), channel_id=1, source_target_pairs={{0,2},{1,3},{2,0},{3,1},{4,6},{5,7},{6,4},{7,5},{8,10},{9,11},{10,... | collective-permute-start | bytes 3342344 | tf_op jit(solution)/shard_map/ppermute | solution.py:151
  3.8 48.4 %collective-permute-start.1 = (f32[136,2048]{1,0:T(8,128)S(1)}, f32[136,2048]{1,0:T(8,128)}, u32[]{:S(2)}, u32[]{:S(2)}) collective-permute-start(f32[136,2048]{1,0:T(8,128)S(1)} %select_maximum_fusion.refs_0_.refs_8_.refs_11_), channel_id=1, source_target_pairs={{0,4},{1,5},{2,6},{3,7},{4,0},{5,1},{6,2},{7,3},{8,12},{9,13},{10,... | collective-permute-start | bytes 3342344 | tf_op jit(solution)/shard_map/ppermute | solution.py:151
  5.4 49.0 %collective-permute-start = (f32[136,2048]{1,0:T(8,128)S(1)}, f32[136,2048]{1,0:T(8,128)}, u32[]{:S(2)}, u32[]{:S(2)}) collective-permute-start(f32[136,2048]{1,0:T(8,128)S(1)} %select_maximum_fusion.refs_0_.refs_8_.refs_11_), channel_id=1, source_target_pairs={{0,8},{1,9},{2,10},{3,11},{4,12},{5,13},{6,14},{7,15},{8,0},{9,1},... | collective-permute-start | bytes 3342344 | tf_op jit(solution)/shard_map/ppermute | solution.py:151
  5.8 49.2 %copy-start.7 = (f32[136,2048]{1,0:T(8,128)}, f32[136,2048]{1,0:T(8,128)S(1)}, u32[]{:S(2)}) copy-start(f32[136,2048]{1,0:T(8,128)S(1)} %collective-permute-done.3.refs_4_.refs_0_.refs_10_.refs_14_) | copy-start | bytes 3342340
  54.4 8.5 %collective-permute-start.4 = (f32[136,2048]{1,0:T(8,128)}, f32[136,2048]{1,0:T(8,128)S(1)}, u32[]{:S(2)}, u32[]{:S(2)}) collective-permute-start(f32[136,2048]{1,0:T(8,128)} %collective-permute-done.refs_0_.refs_1_.refs_6_.refs_9_), channel_id=1, source_target_pairs={{0,1},{1,0},{2,3},{3,2},{4,5},{5,4},{6,7},{7,6},{8,9},{9,8},{10,11... | collective-permute-start | bytes 3342344 | tf_op jit(solution)/shard_map/ppermute | solution.py:151
  54.4 8.5 %collective-permute-start.5 = (f32[136,2048]{1,0:T(8,128)}, f32[136,2048]{1,0:T(8,128)S(1)}, u32[]{:S(2)}, u32[]{:S(2)}) collective-permute-start(f32[136,2048]{1,0:T(8,128)} %collective-permute-done.1.refs_2_.refs_0_.refs_8_.refs_11_), channel_id=1, source_target_pairs={{0,1},{1,0},{2,3},{3,2},{4,5},{5,4},{6,7},{7,6},{8,9},{9,8},{10,11... | collective-permute-start | bytes 3342344 | tf_op jit(solution)/shard_map/ppermute | solution.py:151
  55.0 8.0 %collective-permute-start.6 = (f32[136,2048]{1,0:T(8,128)}, f32[136,2048]{1,0:T(8,128)S(1)}, u32[]{:S(2)}, u32[]{:S(2)}) collective-permute-start(f32[136,2048]{1,0:T(8,128)} %collective-permute-done.2.refs_3_.refs_1_.refs_8_.refs_11_), channel_id=1, source_target_pairs={{0,1},{1,0},{2,3},{3,2},{4,5},{5,4},{6,7},{7,6},{8,9},{9,8},{10,11... | collective-permute-start | bytes 3342344 | tf_op jit(solution)/shard_map/ppermute | solution.py:151
  62.9 3.7 %copy-start = (f32[136,2048]{1,0:T(8,128)}, f32[136,2048]{1,0:T(8,128)S(1)}, u32[]{:S(2)}) copy-start(f32[136,2048]{1,0:T(8,128)S(1)} %collective-permute-done.4.refs_0_.refs_3_.refs_2_.refs_7_.refs_10_) | copy-start | bytes 3342340
  63.0 3.6 %copy-start.1 = (f32[136,2048]{1,0:T(8,128)}, f32[136,2048]{1,0:T(8,128)S(1)}, u32[]{:S(2)}) copy-start(f32[136,2048]{1,0:T(8,128)S(1)} %collective-permute-done.5.refs_1_.refs_4_.refs_3_.refs_8_.refs_11_) | copy-start | bytes 3342340
  63.0 3.6 %copy-start.2 = (f32[136,2048]{1,0:T(8,128)}, f32[136,2048]{1,0:T(8,128)S(1)}, u32[]{:S(2)}) copy-start(f32[136,2048]{1,0:T(8,128)S(1)} %collective-permute-done.6.refs_5_.refs_4_.refs_1_.refs_11_.refs_15_) | copy-start | bytes 3342340
  63.0 39.4 %collective-permute-start.9 = (f32[136,2048]{1,0:T(8,128)}, f32[136,2048]{1,0:T(8,128)}, u32[]{:S(2)}, u32[]{:S(2)}) collective-permute-start(f32[136,2048]{1,0:T(8,128)} %collective-permute-done.refs_0_.refs_1_.refs_6_.refs_9_), channel_id=1, source_target_pairs={{0,4},{1,5},{2,6},{3,7},{4,0},{5,1},{6,2},{7,3},{8,12},{9,13},{10,... | collective-permute-start | bytes 3342344 | tf_op jit(solution)/shard_map/ppermute | solution.py:151
  65.7 36.7 %collective-permute-start.7 = (f32[136,2048]{1,0:T(8,128)}, f32[136,2048]{1,0:T(8,128)}, u32[]{:S(2)}, u32[]{:S(2)}) collective-permute-start(f32[136,2048]{1,0:T(8,128)} %collective-permute-done.refs_0_.refs_1_.refs_6_.refs_9_), channel_id=1, source_target_pairs={{0,2},{1,3},{2,0},{3,1},{4,6},{5,7},{6,4},{7,5},{8,10},{9,11},{10,... | collective-permute-start | bytes 3342344 | tf_op jit(solution)/shard_map/ppermute | solution.py:151
  66.2 36.2 %collective-permute-start.8 = (f32[1024,128]{1,0:T(8,128)}, f32[1024,128]{1,0:T(8,128)S(1)}, u32[]{:S(2)}, u32[]{:S(2)}) collective-permute-start(f32[1024,128]{1,0:T(8,128)} %get-tuple-element.67), channel_id=1, source_target_pairs={{0,8},{1,9},{2,10},{3,11},{4,12},{5,13},{6,14},{7,15},{8,0},{9,1},... | collective-permute-start | bytes 1572872 | tf_op jit(solution)/shard_map/ppermute | solution.py:151
  102.4 38.9 %collective-permute-start.13 = (f32[136,2048]{1,0:T(8,128)}, f32[136,2048]{1,0:T(8,128)S(1)}, u32[]{:S(2)}, u32[]{:S(2)}) collective-permute-start(f32[136,2048]{1,0:T(8,128)} %collective-permute-done.7.refs_0_.refs_4_.refs_6_.refs_9_), channel_id=1, source_target_pairs={{0,1},{1,0},{2,3},{3,2},{4,5},{5,4},{6,7},{7,6},{8,9},{9,8},{10,11... | collective-permute-start | bytes 3342344 | tf_op jit(solution)/shard_map/ppermute | solution.py:151
  102.5 38.8 %collective-permute-start.10 = (f32[136,2048]{1,0:T(8,128)}, f32[136,2048]{1,0:T(8,128)S(1)}, u32[]{:S(2)}, u32[]{:S(2)}) collective-permute-start(f32[136,2048]{1,0:T(8,128)} %collective-permute-done.7.refs_0_.refs_4_.refs_6_.refs_9_), channel_id=1, source_target_pairs={{0,4},{1,5},{2,6},{3,7},{4,0},{5,1},{6,2},{7,3},{8,12},{9,13},{10,... | collective-permute-start | bytes 3342344 | tf_op jit(solution)/shard_map/ppermute | solution.py:151
  104.2 37.1 %collective-permute-start.12 = (f32[136,2048]{1,0:T(8,128)}, f32[136,2048]{1,0:T(8,128)S(1)}, u32[]{:S(2)}, u32[]{:S(2)}) collective-permute-start(f32[136,2048]{1,0:T(8,128)} %collective-permute-done.1.refs_2_.refs_0_.refs_8_.refs_11_), channel_id=1, source_target_pairs={{0,2},{1,3},{2,0},{3,1},{4,6},{5,7},{6,4},{7,5},{8,10},{9,11},{10,... | collective-permute-start | bytes 3342344 | tf_op jit(solution)/shard_map/ppermute | solution.py:151
  104.7 36.6 %collective-permute-start.14 = (f32[136,2048]{1,0:T(8,128)}, f32[136,2048]{1,0:T(8,128)}, u32[]{:S(2)}, u32[]{:S(2)}) collective-permute-start(f32[136,2048]{1,0:T(8,128)} %collective-permute-done.9.refs_1_.refs_5_.refs_7_.refs_10_), channel_id=1, source_target_pairs={{0,1},{1,0},{2,3},{3,2},{4,5},{5,4},{6,7},{7,6},{8,9},{9,8},{10,11... | collective-permute-start | bytes 3342344 | tf_op jit(solution)/shard_map/ppermute | solution.py:151
  104.7 42.2 %copy-start.17 = (f32[64]{0:T(128)S(1)}, f32[64]{0:T(128)}, u32[]{:S(2)}) copy-start(f32[64]{0:T(128)} %param.9) | copy-start | bytes 772
  104.7 42.2 %copy-start.18 = (f32[16]{0:T(128)S(1)}, f32[16]{0:T(128)}, u32[]{:S(2)}) copy-start(f32[16]{0:T(128)} %param.7) | copy-start | bytes 196
  104.7 36.6 %collective-permute-start.11 = (f32[1024,128]{1,0:T(8,128)}, f32[1024,128]{1,0:T(8,128)S(1)}, u32[]{:S(2)}, u32[]{:S(2)}) collective-permute-start(f32[1024,128]{1,0:T(8,128)} %get-tuple-element.73), channel_id=1, source_target_pairs={{0,9},{1,8},{2,11},{3,10},{4,13},{5,12},{6,15},{7,14},{8,1},{9,0},... | collective-permute-start | bytes 1572872 | tf_op jit(solution)/shard_map/ppermute | solution.py:151
  141.3 7.0 %copy-start.5 = (f32[136,2048]{1,0:T(8,128)}, f32[136,2048]{1,0:T(8,128)S(1)}, u32[]{:S(2)}) copy-start(f32[136,2048]{1,0:T(8,128)S(1)} %collective-permute-done.13.refs_0_.refs_6_.refs_9_) | copy-start | bytes 3342340
  141.3 7.0 %copy-start.3 = (f32[136,2048]{1,0:T(8,128)}, f32[136,2048]{1,0:T(8,128)S(1)}, u32[]{:S(2)}) copy-start(f32[136,2048]{1,0:T(8,128)S(1)} %collective-permute-done.10.refs_4_.refs_0_.refs_6_.refs_9_) | copy-start | bytes 3342340
  141.4 7.0 %copy-start.4 = (f32[136,2048]{1,0:T(8,128)}, f32[136,2048]{1,0:T(8,128)S(1)}, u32[]{:S(2)}) copy-start(f32[136,2048]{1,0:T(8,128)S(1)} %collective-permute-done.12.refs_5_.refs_1_.refs_7_.refs_10_) | copy-start | bytes 3342340
  142.1 46.8 %collective-permute-start.15 = (f32[136,2048]{1,0:T(8,128)S(1)}, f32[136,2048]{1,0:T(8,128)}, u32[]{:S(2)}, u32[]{:S(2)}) collective-permute-start(f32[136,2048]{1,0:T(8,128)S(1)} %collective-permute-done.10.refs_4_.refs_0_.refs_6_.refs_9_), channel_id=1, source_target_pairs={{0,1},{1,0},{2,3},{3,2},{4,5},{5,4},{6,7},{7,6},{8,9},{9,8},{10,11... | collective-permute-start | bytes 3342344 | tf_op jit(solution)/shard_map/ppermute | solution.py:151
  142.4 46.5 %collective-permute-start.16 = (f32[136,2048]{1,0:T(8,128)S(1)}, f32[136,2048]{1,0:T(8,128)}, u32[]{:S(2)}, u32[]{:S(2)}) collective-permute-start(f32[136,2048]{1,0:T(8,128)S(1)} %collective-permute-done.12.refs_5_.refs_1_.refs_7_.refs_10_), channel_id=1, source_target_pairs={{0,1},{1,0},{2,3},{3,2},{4,5},{5,4},{6,7},{7,6},{8,9},{9,8},{10,11... | collective-permute-start | bytes 3342344 | tf_op jit(solution)/shard_map/ppermute | solution.py:151
  142.6 35.4 %collective-permute-start.19 = (f32[1024,128]{1,0:T(8,128)}, f32[1024,128]{1,0:T(8,128)}, u32[]{:S(2)}, u32[]{:S(2)}) collective-permute-start(f32[1024,128]{1,0:T(8,128)} %get-tuple-element.85), channel_id=1, source_target_pairs={{0,4},{1,5},{2,6},{3,7},{4,0},{5,1},{6,2},{7,3},{8,12},{9,13},{10,... | collective-permute-start | bytes 1572872 | tf_op jit(solution)/shard_map/ppermute | solution.py:151
  143.2 37.6 %collective-permute-start.18 = (f32[1024,128]{1,0:T(8,128)}, f32[1024,128]{1,0:T(8,128)}, u32[]{:S(2)}, u32[]{:S(2)}) collective-permute-start(f32[1024,128]{1,0:T(8,128)} %get-tuple-element.83), channel_id=1, source_target_pairs={{0,12},{1,13},{2,14},{3,15},{4,8},{5,9},{6,10},{7,11},{8,4},{9,5},... | collective-permute-start | bytes 1572872 | tf_op jit(solution)/shard_map/ppermute | solution.py:151
  143.7 45.2 %collective-permute-start.17 = (f32[1024,128]{1,0:T(8,128)}, f32[1024,128]{1,0:T(8,128)}, u32[]{:S(2)}, u32[]{:S(2)}) collective-permute-start(f32[1024,128]{1,0:T(8,128)} %get-tuple-element.81), channel_id=1, source_target_pairs={{0,10},{1,11},{2,8},{3,9},{4,14},{5,15},{6,12},{7,13},{8,2},{9,3},... | collective-permute-start | bytes 1572872 | tf_op jit(solution)/shard_map/ppermute | solution.py:151
  166.0 23.0 %copy-start.19 = (f32[1024,128]{1,0:T(8,128)S(1)}, f32[1024,128]{1,0:T(8,128)}, u32[]{:S(2)}) copy-start(f32[1024,128]{1,0:T(8,128)} %get-tuple-element.108) | copy-start | bytes 1572868
  166.0 23.5 %copy-start.20 = (f32[1024,128]{1,0:T(8,128)S(1)}, f32[1024,128]{1,0:T(8,128)}, u32[]{:S(2)}) copy-start(f32[1024,128]{1,0:T(8,128)} %get-tuple-element.112) | copy-start | bytes 1572868
  188.9 46.3 %collective-permute-start.26 = (f32[1024,128]{1,0:T(8,128)S(1)}, f32[1024,128]{1,0:T(8,128)S(1)}, u32[]{:S(2)}, u32[]{:S(2)}) collective-permute-start(f32[1024,128]{1,0:T(8,128)S(1)} %copy-done.19), channel_id=1, source_target_pairs={{0,2},{1,3},{2,0},{3,1},{4,6},{5,7},{6,4},{7,5},{8,10},{9,11},{10,... | collective-permute-start | bytes 1572872 | tf_op jit(solution)/shard_map/ppermute | solution.py:151
  189.5 47.2 %collective-permute-start.27 = (f32[1024,128]{1,0:T(8,128)S(1)}, f32[1024,128]{1,0:T(8,128)S(1)}, u32[]{:S(2)}, u32[]{:S(2)}) collective-permute-start(f32[1024,128]{1,0:T(8,128)S(1)} %copy-done.20), channel_id=1, source_target_pairs={{0,11},{1,10},{2,9},{3,8},{4,15},{5,14},{6,13},{7,12},{8,3},{9,2},... | collective-permute-start | bytes 1572872 | tf_op jit(solution)/shard_map/ppermute | solution.py:151
  192.1 47.3 %collective-permute-start.28 = (f32[1024,128]{1,0:T(8,128)}, f32[1024,128]{1,0:T(8,128)S(1)}, u32[]{:S(2)}, u32[]{:S(2)}) collective-permute-start(f32[1024,128]{1,0:T(8,128)} %get-tuple-element.114), channel_id=1, source_target_pairs={{0,13},{1,12},{2,15},{3,14},{4,9},{5,8},{6,11},{7,10},{8,5},{9,4},... | collective-permute-start | bytes 1572872 | tf_op jit(solution)/shard_map/ppermute | solution.py:151
  195.0 44.5 %collective-permute-start.29 = (f32[1024,128]{1,0:T(8,128)}, f32[1024,128]{1,0:T(8,128)S(1)}, u32[]{:S(2)}, u32[]{:S(2)}) collective-permute-start(f32[1024,128]{1,0:T(8,128)} %get-tuple-element.116), channel_id=1, source_target_pairs={{0,5},{1,4},{2,7},{3,6},{4,1},{5,0},{6,3},{7,2},{8,13},{9,12},{10,... | collective-permute-start | bytes 1572872 | tf_op jit(solution)/shard_map/ppermute | solution.py:151
  203.8 48.0 %collective-permute-start.25 = (f32[1024,128]{1,0:T(8,128)}, f32[1024,128]{1,0:T(8,128)S(1)}, u32[]{:S(2)}, u32[]{:S(2)}) collective-permute-start(f32[1024,128]{1,0:T(8,128)} %get-tuple-element.106), channel_id=1, source_target_pairs={{0,6},{1,7},{2,4},{3,5},{4,2},{5,3},{6,0},{7,1},{8,14},{9,15},{10,... | collective-permute-start | bytes 1572872 | tf_op jit(solution)/shard_map/ppermute | solution.py:151
  235.2 30.0 %copy-start.10 = (f32[1024,128]{1,0:T(8,128)}, f32[1024,128]{1,0:T(8,128)S(1)}, u32[]{:S(2)}) copy-start(f32[1024,128]{1,0:T(8,128)S(1)} %collective-permute-done.26.refs_5_) | copy-start | bytes 1572868
  235.2 52.9 %collective-permute-start.22 = (f32[1024,128]{1,0:T(8,128)}, f32[1024,128]{1,0:T(8,128)S(1)}, u32[]{:S(2)}, u32[]{:S(2)}) collective-permute-start(f32[1024,128]{1,0:T(8,128)} %get-tuple-element.98), channel_id=1, source_target_pairs={{0,1},{1,0},{2,3},{3,2},{4,5},{5,4},{6,7},{7,6},{8,9},{9,8},{10,11... | collective-permute-start | bytes 1572872 | tf_op jit(solution)/shard_map/ppermute | solution.py:151
  236.7 15.2 %copy-start.14 = (f32[1024,128]{1,0:T(8,128)}, f32[1024,128]{1,0:T(8,128)S(1)}, u32[]{:S(2)}) copy-start(f32[1024,128]{1,0:T(8,128)S(1)} %collective-permute-done.27.refs_3_) | copy-start | bytes 1572868
  236.7 37.4 %collective-permute-start.24 = (f32[1024,128]{1,0:T(8,128)}, f32[1024,128]{1,0:T(8,128)S(1)}, u32[]{:S(2)}, u32[]{:S(2)}) collective-permute-start(f32[1024,128]{1,0:T(8,128)} %get-tuple-element.104), channel_id=1, source_target_pairs={{0,14},{1,15},{2,12},{3,13},{4,10},{5,11},{6,8},{7,9},{8,6},{9,7},... | collective-permute-start | bytes 1572872 | tf_op jit(solution)/shard_map/ppermute | solution.py:151
  239.3 12.6 %copy-start.15 = (f32[1024,128]{1,0:T(8,128)}, f32[1024,128]{1,0:T(8,128)S(1)}, u32[]{:S(2)}) copy-start(f32[1024,128]{1,0:T(8,128)S(1)} %collective-permute-done.28.refs_4_) | copy-start | bytes 1572868
  239.3 48.8 %collective-permute-start.23 = (f32[1024,128]{1,0:T(8,128)}, f32[1024,128]{1,0:T(8,128)}, u32[]{:S(2)}, u32[]{:S(2)}) collective-permute-start(f32[1024,128]{1,0:T(8,128)} %get-tuple-element.100), channel_id=1, source_target_pairs={{0,3},{1,2},{2,1},{3,0},{4,7},{5,6},{6,5},{7,4},{8,11},{9,10},{10,... | collective-permute-start | bytes 1572872 | tf_op jit(solution)/shard_map/ppermute | solution.py:151
  239.5 12.4 %copy-start.16 = (f32[1024,128]{1,0:T(8,128)}, f32[1024,128]{1,0:T(8,128)S(1)}, u32[]{:S(2)}) copy-start(f32[1024,128]{1,0:T(8,128)S(1)} %collective-permute-done.29.refs_5_) | copy-start | bytes 1572868
  239.5 48.7 %collective-permute-start.21 = (f32[1024,128]{1,0:T(8,128)}, f32[1024,128]{1,0:T(8,128)}, u32[]{:S(2)}, u32[]{:S(2)}) collective-permute-start(f32[1024,128]{1,0:T(8,128)} %get-tuple-element.96), channel_id=1, source_target_pairs={{0,7},{1,6},{2,5},{3,4},{4,3},{5,2},{6,1},{7,0},{8,15},{9,14},{10,... | collective-permute-start | bytes 1572872 | tf_op jit(solution)/shard_map/ppermute | solution.py:151
  251.9 13.4 %copy-start.11 = (f32[1024,128]{1,0:T(8,128)}, f32[1024,128]{1,0:T(8,128)S(1)}, u32[]{:S(2)}) copy-start(f32[1024,128]{1,0:T(8,128)S(1)} %collective-permute-done.25.refs_4_) | copy-start | bytes 1572868
  251.9 42.4 %collective-permute-start.20 = (f32[1024,128]{1,0:T(8,128)}, f32[1024,128]{1,0:T(8,128)}, u32[]{:S(2)}, u32[]{:S(2)}) collective-permute-start(f32[1024,128]{1,0:T(8,128)} %get-tuple-element.94), channel_id=1, source_target_pairs={{0,15},{1,14},{2,13},{3,12},{4,11},{5,10},{6,9},{7,8},{8,7},{9,6},... | collective-permute-start | bytes 1572872 | tf_op jit(solution)/shard_map/ppermute | solution.py:151
  288.2 6.1 %copy-start.13 = (f32[1024,128]{1,0:T(8,128)}, f32[1024,128]{1,0:T(8,128)S(1)}, u32[]{:S(2)}) copy-start(f32[1024,128]{1,0:T(8,128)S(1)} %collective-permute-done.22.refs_6_) | copy-start | bytes 1572868
  (3 other events, 3.9 us)
